TPU v7x, 128 devices: a whole 4x4x4 slice. The times are simulated.
128 devices in a mesh: seq: 8 (over y, x_lo), fsdp: 16 (over z, x_hi, core).
Axes of the slice: x: 4 (x_hi: 2, x_lo: 2; x = x_hi * 2 + x_lo), y: 4, z: 4, core: 2. Of those that a mesh axis runs over, the one named last changes fastest.
Arguments:
- tokens: bfloat16 [16, 1024, 1536], P('fsdp', 'seq'), may hold values from -6 to 6
- segments: int32 [16, 1024], P('fsdp', 'seq'), may hold values from 0 to 2, as said below
- out_grad: bfloat16 [16, 1024, 1536], P('fsdp', 'seq'), may hold values from -6 to 6
- attn_gain: bfloat16 [1536], P('fsdp'), may hold values from 0.5 to 1.5
- w_query: bfloat16 [1536, 1536], P('fsdp'), may hold values from -0.15625 to 0.15625
- key_projection: bfloat16 [1536, 512], P('fsdp'), may hold values from -0.15625 to 0.15625
- value_projection: bfloat16 [1536, 512], P('fsdp'), may hold values from -0.15625 to 0.15625
- query_gain: bfloat16 [64], P('fsdp'), may hold values from 0.5 to 1.5
- key_norm_gain: bfloat16 [64], P('fsdp'), may hold values from 0.5 to 1.5
- w_out: bfloat16 [1536, 1536], P(None, 'fsdp'), may hold values from -0.875 to 0.875
- mlp_gain: bfloat16 [1536], P('fsdp'), may hold values from 0.5 to 1.5
- w_gate: bfloat16 [1536, 6912], P('fsdp', 'seq'), may hold values from -0.15625 to 0.15625
- w_up: bfloat16 [1536, 6912], P('fsdp', 'seq'), may hold values from -0.15625 to 0.15625
- w_down: bfloat16 [6912, 1536], P('seq', 'fsdp'), may hold values from -0.15625 to 0.15625
Outputs:
- layer_out: bfloat16 [16, 1024, 1536], P('fsdp', 'seq')
- grad_tokens: float32 [16, 1024, 1536], P('fsdp', 'seq')
- grad_attn_gain: float32 [1536], P('fsdp')
- grad_w_query: float32 [1536, 1536], P('fsdp')
- grad_w_key: float32 [1536, 512], P('fsdp')
- grad_w_value: float32 [1536, 512], P('fsdp')
- grad_query_gain: float32 [64], P('fsdp')
- grad_key_gain: float32 [64], P('fsdp')
- grad_w_out: float32 [1536, 1536], P(None, 'fsdp')
- grad_mlp_gain: float32 [1536], P('fsdp')
- grad_w_gate: float32 [1536, 6912], P('fsdp', 'seq')
- grad_w_up: float32 [1536, 6912], P('fsdp', 'seq')
- grad_w_down: float32 [6912, 1536], P('seq', 'fsdp')
Inputs may be any that keep to these rules, and one draw needn't show every extreme that they name: `segments`: within a sequence segment numbers start at 0, never fall and rise by one where a document starts; a sequence holds at most three documents, each of 64 tokens or more; of the 1 sequence of each index of fsdp, one drawn from the seed has three documents, the middle one starting within the first 128 tokens and ending within the last 128.
All inputs are finite; a program needn't handle non-finite values.
Results may differ from a plain program's by a relative error of at most 0.02.
Values may be sent and summed in bfloat16 or wider, within the bound.
No kernel may reach another device: no remote copies, remote signals or barrier semaphores. Data moves between devices by JAX's collectives and lax.ppermute only.
A program may use at most 192 MiB of HBM per device.

v0:
```python
from functools import partial

import jax
import jax.numpy as jnp
from jax import lax
from jax.sharding import PartitionSpec as P

HEAD_SIZE = 64


eps = 1e-05
rope_base = 1000000.0


def apply_norm(values, norm_gain):
    inverse = lax.rsqrt(jnp.mean(values * values, axis=-1, keepdims=True) + eps)
    return values * inverse * norm_gain


def apply_rotary(values, token_position):
    halfway = values.shape[-1] // 2
    frequency = rope_base ** (-2.0 * jnp.arange(halfway, dtype=jnp.float32) / values.shape[-1])
    angles = token_position[..., None, None] * frequency
    cosine = jnp.cos(angles)
    sine_part = jnp.sin(angles)
    leading = values[..., :halfway]
    trailing = values[..., halfway:]
    return jnp.concatenate(
        [leading * cosine - trailing * sine_part, trailing * cosine + leading * sine_part], axis=-1
    )


def prep_heads(query_in, key_in, query_scale, key_scale, token_position):
    query_shaped = query_in.reshape(query_in.shape[:-1] + (-1, HEAD_SIZE))
    key_shaped = key_in.reshape(key_in.shape[:-1] + (-1, HEAD_SIZE))
    query_done = apply_rotary(apply_norm(query_shaped, query_scale), token_position)
    key_done = apply_rotary(apply_norm(key_shaped, key_scale), token_position)
    return (query_done.reshape(query_in.shape), key_done.reshape(key_in.shape))


def scores_for(query_block, key_block, id_block):
    length_total = query_block.shape[0]
    head_groups = key_block.shape[-1] // HEAD_SIZE
    grouped = query_block.reshape(length_total, head_groups, -1, HEAD_SIZE)
    key_split = key_block.reshape(length_total, head_groups, HEAD_SIZE)
    raw_scores = jnp.einsum(
        "qhgd,khd->hgqk", grouped, key_split, preferred_element_type=jnp.float32
    ) * HEAD_SIZE ** (-0.5)
    indices = jnp.arange(length_total)
    allowed = (indices[None, :] <= indices[:, None]) & (id_block[None, :] == id_block[:, None])
    return (grouped, key_split, jnp.where(allowed, raw_scores, -1e30))


def attend_forward(element):
    query_block, key_block, value_block, id_block = element
    grouped, key_split, scores = scores_for(query_block, key_block, id_block)
    row_peak = jnp.max(scores, axis=-1, keepdims=True)
    exponent = jnp.exp(scores - row_peak)
    row_total = jnp.sum(exponent, axis=-1, keepdims=True)
    weights = (exponent / row_total).astype(jnp.bfloat16)
    value_split = value_block.reshape(value_block.shape[0], -1, HEAD_SIZE)
    mixed_out = jnp.einsum(
        "hgqk,khd->qhgd", weights, value_split, preferred_element_type=jnp.float32
    )
    return (
        mixed_out.reshape(mixed_out.shape[0], -1).astype(jnp.bfloat16),
        row_peak + jnp.log(row_total),
    )


def attend_backward(element):
    query_block, key_block, value_block, id_block, lse_block, grad_block = element
    grouped, key_split, scores = scores_for(query_block, key_block, id_block)
    probability = jnp.exp(scores - lse_block)
    value_split = value_block.reshape(value_block.shape[0], -1, HEAD_SIZE)
    grad_split = grad_block.reshape(grouped.shape)
    grad_probs = jnp.einsum(
        "qhgd,khd->hgqk", grad_split, value_split, preferred_element_type=jnp.float32
    )
    inner_sum = jnp.sum(probability * grad_probs, axis=-1, keepdims=True)
    grad_scores = (probability * (grad_probs - inner_sum)).astype(jnp.bfloat16)
    grad_query = jnp.einsum(
        "hgqk,khd->qhgd", grad_scores, key_split, preferred_element_type=jnp.float32
    ) * HEAD_SIZE ** (-0.5)
    grad_key = jnp.einsum(
        "hgqk,qhgd->khd", grad_scores, grouped, preferred_element_type=jnp.float32
    ) * HEAD_SIZE ** (-0.5)
    grad_value = jnp.einsum(
        "hgqk,qhgd->khd",
        probability.astype(jnp.bfloat16),
        grad_split,
        preferred_element_type=jnp.float32,
    )
    length_total = query_block.shape[0]
    return (
        grad_query.reshape(length_total, -1).astype(jnp.bfloat16),
        grad_key.reshape(length_total, -1).astype(jnp.bfloat16),
        grad_value.reshape(length_total, -1).astype(jnp.bfloat16),
    )


def on_device(
    tokens,
    segments,
    out_grad,
    attn_gain,
    w_query,
    key_projection,
    value_projection,
    query_gain,
    key_norm_gain,
    w_out,
    mlp_gain,
    w_gate,
    w_up,
    w_down,
):
    gathered = (
        lax.all_gather(attn_gain, "fsdp", axis=0, tiled=True),
        lax.all_gather(w_query, "fsdp", axis=0, tiled=True),
        lax.all_gather(key_projection, "fsdp", axis=0, tiled=True),
        lax.all_gather(value_projection, "fsdp", axis=0, tiled=True),
        lax.all_gather(query_gain, "fsdp", axis=0, tiled=True),
        lax.all_gather(key_norm_gain, "fsdp", axis=0, tiled=True),
        lax.all_gather(w_out, "fsdp", axis=1, tiled=True),
        lax.all_gather(mlp_gain, "fsdp", axis=0, tiled=True),
        lax.all_gather(w_gate, "fsdp", axis=0, tiled=True),
        lax.all_gather(w_up, "fsdp", axis=0, tiled=True),
        lax.all_gather(w_down, "fsdp", axis=1, tiled=True),
    )
    (
        full_gain,
        complete_query_weight,
        complete_key_weight,
        complete_value_weight,
        full_qgain,
        full_kgain,
        complete_output_weight,
        full_mgain,
        complete_gate_weight,
        complete_up_weight,
        complete_down_weight,
    ) = gathered
    gain_attn = full_gain.astype(jnp.float32)
    gain_query = full_qgain.astype(jnp.float32)
    gain_key = full_kgain.astype(jnp.float32)
    gain_mlp = full_mgain.astype(jnp.float32)
    local_len = tokens.shape[1]
    all_ids = lax.all_gather(segments, "seq", axis=1, tiled=True)
    offset = lax.axis_index("seq") * local_len
    local_index = offset + jnp.arange(local_len, dtype=jnp.int32)
    earlier = jnp.sum((all_ids[:, None, :] < segments[:, :, None]).astype(jnp.int32), axis=-1)
    token_position = (local_index[None, :] - earlier).astype(jnp.float32)
    hidden_in = tokens.astype(jnp.float32)
    normed_f, attn_back = jax.vjp(apply_norm, hidden_in, gain_attn)
    normed_input = normed_f.astype(jnp.bfloat16)
    query_unnormed = jnp.einsum(
        "fxq,qm->fxm", normed_input, complete_query_weight, preferred_element_type=jnp.float32
    )
    key_unnormed = jnp.einsum(
        "fxq,qm->fxm", normed_input, complete_key_weight, preferred_element_type=jnp.float32
    )
    value_send = jnp.einsum(
        "fxq,qm->fxm", normed_input, complete_value_weight, preferred_element_type=jnp.float32
    ).astype(jnp.bfloat16)
    (query_rot, key_rot), prep_back = jax.vjp(
        partial(prep_heads, token_position=token_position),
        query_unnormed,
        key_unnormed,
        gain_query,
        gain_key,
    )
    query_send = query_rot.astype(jnp.bfloat16)
    key_outgoing = key_rot.astype(jnp.bfloat16)
    query_heads, key_head_rows, value_heads = (
        lax.all_to_all(query_send, "seq", split_axis=2, concat_axis=1, tiled=True),
        lax.all_to_all(key_outgoing, "seq", split_axis=2, concat_axis=1, tiled=True),
        lax.all_to_all(value_send, "seq", split_axis=2, concat_axis=1, tiled=True),
    )
    attended, log_total = lax.map(
        attend_forward, (query_heads, key_head_rows, value_heads, all_ids)
    )
    attended_token_rows = lax.all_to_all(attended, "seq", split_axis=1, concat_axis=2, tiled=True)
    branch_output = jnp.einsum(
        "jmu,uc->jmc",
        attended_token_rows,
        complete_output_weight,
        preferred_element_type=jnp.float32,
    )
    middle = hidden_in + branch_output
    second_f, mlp_back = jax.vjp(apply_norm, middle, gain_mlp)
    second = second_f.astype(jnp.bfloat16)
    second_gathered = lax.all_gather(second, "seq", axis=1, tiled=True)
    gate_before_activation = jnp.einsum(
        "tov,vr->tor", second_gathered, complete_gate_weight, preferred_element_type=jnp.float32
    )
    upward_projection = jnp.einsum(
        "tov,vr->tor", second_gathered, complete_up_weight, preferred_element_type=jnp.float32
    )
    sigmoid_gate = jax.nn.sigmoid(gate_before_activation)
    hidden_activation = (gate_before_activation * sigmoid_gate * upward_projection).astype(
        jnp.bfloat16
    )
    partial_out = jnp.einsum(
        "ohy,yp->ohp", hidden_activation, complete_down_weight, preferred_element_type=jnp.float32
    )
    mlp_out = lax.psum_scatter(partial_out, "seq", scatter_dimension=1, tiled=True)
    layer_out = (middle + mlp_out).astype(jnp.bfloat16)
    gathered_gradient = lax.all_gather(out_grad, "seq", axis=1, tiled=True)
    hidden_gradient = jnp.einsum(
        "woq,pq->wop", gathered_gradient, complete_down_weight, preferred_element_type=jnp.float32
    )
    gate_gradient = (
        hidden_gradient
        * upward_projection
        * sigmoid_gate
        * (1.0 + gate_before_activation * (1.0 - sigmoid_gate))
    ).astype(jnp.bfloat16)
    up_gradient = (hidden_gradient * gate_before_activation * sigmoid_gate).astype(jnp.bfloat16)
    grad_second_part = jnp.einsum(
        "hcg,rg->hcr", gate_gradient, complete_gate_weight, preferred_element_type=jnp.float32
    ) + jnp.einsum(
        "hcg,rg->hcr", up_gradient, complete_up_weight, preferred_element_type=jnp.float32
    )
    grad_wgate = jnp.einsum(
        "aic,aiq->cq", second_gathered, gate_gradient, preferred_element_type=jnp.float32
    )
    up_weight_gradient = jnp.einsum(
        "aic,aiq->cq", second_gathered, up_gradient, preferred_element_type=jnp.float32
    )
    down_weight_gradient = jnp.einsum(
        "uoi,uok->ik", hidden_activation, gathered_gradient, preferred_element_type=jnp.float32
    )
    grad_second = lax.psum_scatter(grad_second_part, "seq", scatter_dimension=1, tiled=True)
    grad_middle_norm, grad_mgain = mlp_back(grad_second)
    grad_middle = out_grad.astype(jnp.float32) + grad_middle_norm
    branch_gradient = grad_middle.astype(jnp.bfloat16)
    grad_attended = jnp.einsum(
        "wxi,fi->wxf", branch_gradient, complete_output_weight, preferred_element_type=jnp.float32
    ).astype(jnp.bfloat16)
    grad_heads = lax.all_to_all(grad_attended, "seq", split_axis=2, concat_axis=1, tiled=True)
    grad_query_h, grad_key_h, grad_value_h = lax.map(
        attend_backward, (query_heads, key_head_rows, value_heads, all_ids, log_total, grad_heads)
    )
    token_first, token_second, value_gradient_transposed = (
        lax.all_to_all(grad_query_h, "seq", split_axis=1, concat_axis=2, tiled=True),
        lax.all_to_all(grad_key_h, "seq", split_axis=1, concat_axis=2, tiled=True),
        lax.all_to_all(grad_value_h, "seq", split_axis=1, concat_axis=2, tiled=True),
    )
    grad_query_raw, grad_key_raw, grad_qgain, grad_kgain = prep_back(
        (token_first.astype(jnp.float32), token_second.astype(jnp.float32))
    )
    query_reduced_precision = grad_query_raw.astype(jnp.bfloat16)
    key_reduced_precision = grad_key_raw.astype(jnp.bfloat16)
    grad_normed = (
        jnp.einsum(
            "aoj,uj->aou",
            query_reduced_precision,
            complete_query_weight,
            preferred_element_type=jnp.float32,
        )
        + jnp.einsum(
            "aoj,uj->aou",
            key_reduced_precision,
            complete_key_weight,
            preferred_element_type=jnp.float32,
        )
        + jnp.einsum(
            "aoj,uj->aou",
            value_gradient_transposed,
            complete_value_weight,
            preferred_element_type=jnp.float32,
        )
    )
    grad_input_norm, grad_again = attn_back(grad_normed)
    grad_tokens = grad_middle + grad_input_norm
    grad_wout = jnp.einsum(
        "gzq,gzk->qk", attended_token_rows, branch_gradient, preferred_element_type=jnp.float32
    )
    query_weight_gradient = jnp.einsum(
        "fuo,fub->ob", normed_input, query_reduced_precision, preferred_element_type=jnp.float32
    )
    key_weight_gradient = jnp.einsum(
        "fuo,fub->ob", normed_input, key_reduced_precision, preferred_element_type=jnp.float32
    )
    grad_wvalue = jnp.einsum(
        "fuo,fub->ob", normed_input, value_gradient_transposed, preferred_element_type=jnp.float32
    )
    owned = (
        lax.psum_scatter(grad_again, "fsdp", scatter_dimension=0, tiled=True),
        lax.psum_scatter(query_weight_gradient, "fsdp", scatter_dimension=0, tiled=True),
        lax.psum_scatter(key_weight_gradient, "fsdp", scatter_dimension=0, tiled=True),
        lax.psum_scatter(grad_wvalue, "fsdp", scatter_dimension=0, tiled=True),
        lax.psum_scatter(grad_qgain, "fsdp", scatter_dimension=0, tiled=True),
        lax.psum_scatter(grad_kgain, "fsdp", scatter_dimension=0, tiled=True),
        lax.psum_scatter(grad_wout, "fsdp", scatter_dimension=1, tiled=True),
        lax.psum_scatter(grad_mgain, "fsdp", scatter_dimension=0, tiled=True),
        lax.psum_scatter(grad_wgate, "fsdp", scatter_dimension=0, tiled=True),
        lax.psum_scatter(up_weight_gradient, "fsdp", scatter_dimension=0, tiled=True),
        lax.psum_scatter(down_weight_gradient, "fsdp", scatter_dimension=1, tiled=True),
    )
    summed = lax.psum(
        (owned[0], owned[1], owned[2], owned[3], owned[4], owned[5], owned[6], owned[7]), "seq"
    )
    return (
        layer_out,
        grad_tokens,
        summed[0],
        summed[1],
        summed[2],
        summed[3],
        summed[4],
        summed[5],
        summed[6],
        summed[7],
        owned[8],
        owned[9],
        owned[10],
    )


def solution(mesh):
    in_specs = (
        P("fsdp", "seq", None),
        P("fsdp", "seq"),
        P("fsdp", "seq", None),
        P("fsdp"),
        P("fsdp", None),
        P("fsdp", None),
        P("fsdp", None),
        P("fsdp"),
        P("fsdp"),
        P(None, "fsdp"),
        P("fsdp"),
        P("fsdp", "seq"),
        P("fsdp", "seq"),
        P("seq", "fsdp"),
    )
    out_specs = (
        P("fsdp", "seq", None),
        P("fsdp", "seq", None),
        P("fsdp"),
        P("fsdp", None),
        P("fsdp", None),
        P("fsdp", None),
        P("fsdp"),
        P("fsdp"),
        P(None, "fsdp"),
        P("fsdp"),
        P("fsdp", "seq"),
        P("fsdp", "seq"),
        P("seq", "fsdp"),
    )
    return jax.shard_map(
        on_device, mesh=mesh, in_specs=in_specs, out_specs=out_specs, check_vma=False
    )
```

profile of v0, /device:TPU:0, one launch (start us, length us, event | category | flops | bytes accessed | tf_op | source)
XLA Modules:
  0.0 1615.4 jit_solution(8532526279055252222)
XLA Ops:
  15.0 19.2 %all_gather.44 = s32[1,1024]{1,0:T(1,128)S(1)} all-gather(s32[1,128]{1,0:T(1,128)} %param.15), channel_id=1, replica_groups=mesh['seq'=8,'fsdp'=16] {'seq'}, dimensions={1}, use_global_device_ids=true | all-gather | bytes 4608 | tf_op jit(solution)/shard_map/all_gather | solution.py:149
  37.5 36.0 %all-reduce.15 = (bf16[1536]{0:T(1024)(128)(2,1)S(1)}, bf16[64]{0:T(256)(128)(2,1)S(1)}, bf16[64]{0:T(256)(128)(2,1)S(1)}, bf16[1536]{0:T(1024)(128)(2,1)S(1)}) all-reduce(bf16[1536]{0:T(1024)(128)(2,1)S(1)} %dynamic-update-slice, bf16[64]{0:T(256)(128)(2,1)S(1)} %dynamic-update-slice.1, ...), channel_id=1, replica_groups=mesh['seq'=8,'fsdp'=16] {'fsdp'}, use_global_device_ids=true, to_apply=%add.4 | all-reduce | flops 3200 | bytes 12800
  82.8 24.2 %all-gather.12.cloned.1.call-done = bf16[1536,512]{1,0:T(8,128)(2,1)} async-done(((bf16[96,512]{1,0:T(8,128)(2,1)}), bf16[1536,512]{1,0:T(8,128)(2,1)}) %all-gather.12.cloned.1.call-update) | async-done | bytes 1572880 | tf_op jit(solution)/shard_map/all_gather | solution.py:121
  111.8 54.3 %all-gather.14.cloned.1.call-done = bf16[1536,1536]{1,0:T(8,128)(2,1)} async-done(((bf16[96,1536]{1,0:T(8,128)(2,1)}), bf16[1536,1536]{1,0:T(8,128)(2,1)}) %all-gather.14.cloned.1.call-update) | async-done | bytes 4718608 | tf_op jit(solution)/shard_map/all_gather | solution.py:120
  182.1 8.8 reduce.18
  199.9 10.6 all-to-all-done.2
  232.0 7.9 all-to-all-done.3
  249.1 26.9 %all-gather.22.cloned.1.call-done = bf16[1536,864]{1,0:T(8,128)(2,1)} async-done(((bf16[96,864]{1,0:T(8,128)(2,1)}), bf16[1536,864]{1,0:T(8,128)(2,1)}) %all-gather.22.cloned.1.call-update) | async-done | bytes 2654224 | tf_op jit(solution)/shard_map/all_gather | solution.py:128
  276.0 72.3 %all-gather.18.cloned.1.call-done = bf16[1,1024,1536]{2,1,0:T(8,128)(2,1)} async-done(((bf16[1,128,1536]{2,1,0:T(8,128)(2,1)}), bf16[1,1024,1536]{2,1,0:T(8,128)(2,1)}) %all-gather.18.cloned.1.call-update) | async-done | bytes 3145744 | tf_op jit(solution)/shard_map/all_gather | solution.py:193
  355.7 44.3 %all-gather.20.cloned.1.call-done = bf16[1536,864]{1,0:T(8,128)(2,1)} async-done(((bf16[96,864]{1,0:T(8,128)(2,1)}), bf16[1536,864]{1,0:T(8,128)(2,1)}) %all-gather.20.cloned.1.call-update) | async-done | bytes 2654224 | tf_op jit(solution)/shard_map/all_gather | solution.py:127
  407.5 43.5 %all-gather.24.cloned.1.call-done = bf16[864,1536]{0,1:T(8,128)(2,1)} async-done(((bf16[864,96]{0,1:T(8,128)(2,1)}), bf16[864,1536]{0,1:T(8,128)(2,1)}) %all-gather.24.cloned.1.call-update) | async-done | bytes 2654224 | tf_op jit(solution)/shard_map/all_gather | solution.py:129
  450.9 71.9 %all-gather.26.cloned.1.call-done = bf16[1,1024,1536]{2,1,0:T(8,128)(2,1)} async-done(((bf16[1,128,1536]{2,1,0:T(8,128)(2,1)}), bf16[1,1024,1536]{2,1,0:T(8,128)(2,1)}) %all-gather.26.cloned.1.call-update) | async-done | bytes 3145744 | tf_op jit(solution)/shard_map/all_gather | solution.py:209
  522.8 10.6 multiply_convert_fusion
  542.9 8.4 convolution_bitcast_fusion
  551.3 121.3 %reduce-scatter.12.cloned.1.call-done = f32[1,128,1536]{2,1,0:T(8,128)} async-done(((f32[1,1024,1536]{2,1,0:T(8,128)}), f32[1,128,1536]{2,1,0:T(8,128)}) %reduce-scatter.12.cloned.1.call-update) | async-done | bytes 786448 | tf_op jit(solution)/shard_map/reduce_scatter | solution.py:234
  674.5 131.2 %reduce-scatter.10.cloned.1.call-done = f32[1,128,1536]{2,1,0:T(8,128)} async-done(((f32[1,1024,1536]{2,1,0:T(8,128)}), f32[1,128,1536]{2,1,0:T(8,128)}) %reduce-scatter.10.cloned.1.call-update) | async-done | bytes 786448 | tf_op jit(solution)/shard_map/reduce_scatter | solution.py:207
  814.2 9.6 reduce.20
  830.5 8.5 all-to-all-done.4
  853.2 9.2 all_to_all.108
  887.7 9.5 all_to_all.109
  920.8 10.5 all_to_all.110
  942.1 8.3 fusion.13
  950.4 8.3 fusion.17
  958.8 8.5 fusion.19
  968.9 51.7 %reduce-scatter.16.cloned.1.call-done = f32[96,512]{1,0:T(8,128)} async-done(((f32[1536,512]{1,0:T(8,128)}), f32[96,512]{1,0:T(8,128)}) %reduce-scatter.16.cloned.1.call-update) | async-done | bytes 196624 | tf_op jit(solution)/shard_map/reduce_scatter | solution.py:292
  1020.5 110.3 %reduce-scatter.20.cloned.1.call-done = f32[1536,96]{0,1:T(8,128)} async-done(((f32[1536,1536]{0,1:T(8,128)}), f32[1536,96]{0,1:T(8,128)}) %reduce-scatter.20.cloned.1.call-update) | async-done | bytes 589840 | tf_op jit(solution)/shard_map/reduce_scatter | solution.py:296
  1130.8 110.9 %reduce-scatter.14.cloned.1.call-done = f32[96,1536]{1,0:T(8,128)} async-done(((f32[1536,1536]{1,0:T(8,128)}), f32[96,1536]{1,0:T(8,128)}) %reduce-scatter.14.cloned.1.call-update) | async-done | bytes 589840 | tf_op jit(solution)/shard_map/reduce_scatter | solution.py:291
  1247.5 65.5 %all-reduce.12 = (f32[1536]{0:T(1024)S(1)}, f32[64]{0:T(128)S(1)}, f32[64]{0:T(128)S(1)}, f32[1536]{0:T(1024)S(1)}) all-reduce(f32[1536]{0:T(1024)S(1)} %get-tuple-element.68, f32[64]{0:T(128)S(1)} %get-tuple-element.56, f32[64]{0:T(128)S(1)} %copy-done.29, f32[1536]{0:T(1024)S(1)} %copy-done.25), channel_id=4, replica_groups=mesh['seq'=8,'fsdp'=16] {'fsdp'}, use_global_device_ids=true, to_apply=%region_15.16.clone | all-reduce | flops 3200 | bytes 25600
  1313.3 20.2 %all-reduce.13 = (f32[96]{0:T(128)}, f32[4]{0:T(128)}, f32[4]{0:T(128)}, f32[96]{0:T(128)}) all-reduce(f32[96]{0:T(128)S(1)} %dynamic-slice.6, f32[4]{0:T(128)S(1)} %dynamic-slice.8, f32[4]{0:T(128)S(1)} %dynamic-slice.10, f32[96]{0:T(128)S(1)} %dynamic-slice.12), channel_id=1, replica_groups=mesh['seq'=8,'fsdp'=16] {'seq'}, use_global_device_ids=true, to_apply=%region_16.17 | all-reduce | flops 200 | bytes 1600 | tf_op jit(solution)/shard_map/psum | solution.py:302
  1334.6 86.9 %reduce-scatter.24.cloned.1.call-done = f32[96,864]{1,0:T(8,128)} async-done(((f32[1536,864]{1,0:T(8,128)}), f32[96,864]{1,0:T(8,128)}) %reduce-scatter.24.cloned.1.call-update) | async-done | bytes 331792 | tf_op jit(solution)/shard_map/reduce_scatter | solution.py:299
  1421.5 89.6 %reduce-scatter.22.cloned.1.call-done = f32[96,864]{1,0:T(8,128)} async-done(((f32[1536,864]{1,0:T(8,128)}), f32[96,864]{1,0:T(8,128)}) %reduce-scatter.22.cloned.1.call-update) | async-done | bytes 331792 | tf_op jit(solution)/shard_map/reduce_scatter | solution.py:298
  1511.1 90.5 %all-reduce.18.cloned.1.call-done = (f32[96,1536]{1,0:T(8,128)}, f32[96,512]{1,0:T(8,128)}, f32[96,512]{1,0:T(8,128)}, f32[1536,96]{0,1:T(8,128)}) async-done(((f32[96,1536]{1,0:T(8,128)}, f32[96,512]{1,0:T(8,128)}, f32[96,512]{1,0:T(8,128)}, f32[1536,96]{0,1:T(8,128)}), (f32[96,1536]{1,0:T(8,128)}, f32[96,512]{1,0:T(8,128)}, f32[96,512]{1,0:T(8,128)}, f32[1536,96]{0,1:T(8,128)})) %all-reduce.18.cloned.1.call-update) | async-done | bytes 1572880 | tf_op jit(solution)/shard_map/psum | solution.py:302
  (256 shorter events, 208.4 us)
Async XLA Ops:
  7.2 99.9 %copy-start.2 = (bf16[1,128,1536]{2,1,0:T(8,128)(2,1)S(1)}, bf16[1,128,1536]{2,1,0:T(8,128)(2,1)}, u32[]{:S(2)}) copy-start(bf16[1,128,1536]{2,1,0:T(8,128)(2,1)} %param.14) | copy-start | bytes 1179652
  7.2 67.5 %all-gather.10.cloned.1.call-start = ((), (), s32[]{:S(2)}) async-start(), calls=%async_computation.17 | async-start | bytes 1671168 | tf_op jit(solution)/shard_map/all_gather | solution.py:122
  7.9 99.1 %all-gather.12.cloned.1.call-start = ((), (), s32[]{:S(2)}) async-start(), calls=%async_computation.18 | async-start | bytes 1671168 | tf_op jit(solution)/shard_map/all_gather | solution.py:121
  8.7 157.4 %all-gather.14.cloned.1.call-start = ((), (), s32[]{:S(2)}) async-start(), calls=%async_computation.19 | async-start | bytes 5013504 | tf_op jit(solution)/shard_map/all_gather | solution.py:120
  9.4 232.0 %all-gather.16.cloned.1.call-start = ((), (), s32[]{:S(2)}) async-start(), calls=%async_computation.20 | async-start | bytes 5013504 | tf_op jit(solution)/shard_map/all_gather | solution.py:125
  10.0 266.0 %all-gather.22.cloned.1.call-start = ((), (), s32[]{:S(2)}) async-start(), calls=%async_computation.23 | async-start | bytes 2924544 | tf_op jit(solution)/shard_map/all_gather | solution.py:128
  73.6 35.9 %copy-start.28 = (f32[64]{0:T(128)}, f32[64]{0:T(128)S(1)}, u32[]{:S(2)}) copy-start(f32[64]{0:T(128)S(1)} %convert_element_type.250) | copy-start | bytes 772
  73.6 96.9 %copy-start.26 = (f32[64]{0:T(128)}, f32[64]{0:T(128)S(1)}, u32[]{:S(2)}) copy-start(f32[64]{0:T(128)S(1)} %convert_element_type.254) | copy-start | bytes 772
  74.6 96.1 %copy-start.15 = (f32[128,32]{0,1:T(8,128)}, f32[128,32]{0,1:T(8,128)S(1)}, u32[]{:S(2)}) copy-start(f32[128,32]{0,1:T(8,128)S(1)} %get-tuple-element.101) | copy-start | bytes 49156
  74.7 96.0 %copy-start.17 = (f32[128,32]{0,1:T(8,128)}, f32[128,32]{0,1:T(8,128)S(1)}, u32[]{:S(2)}) copy-start(f32[128,32]{0,1:T(8,128)S(1)} %get-tuple-element.102) | copy-start | bytes 49156
  79.5 91.4 %all-to-all-start = ((bf16[8,2,4096]{2,1,0:T(2,128)(2,1)}), bf16[8,2,4096]{2,1,0:T(2,128)(2,1)S(1)}, u32[]{:S(2)}, u32[]{:S(2)}) async-start(bf16[8,2,4096]{2,1,0:T(2,128)(2,1)} %reshape.784), calls=%async_computation | async-start | bytes 262144 | tf_op jit(solution)/shard_map/all_to_all | solution.py:178
  109.3 61.1 %copy-start.23 = (f32[128,8]{0,1:T(8,128)}, f32[128,8]{0,1:T(8,128)S(1)}, u32[]{:S(2)}) copy-start(f32[128,8]{0,1:T(8,128)S(1)} %multiply_reduce_fusion.8) | copy-start | bytes 12292
  171.1 20.7 %all-to-all-start.1 = ((bf16[8,2,4096]{2,1,0:T(2,128)(2,1)}), bf16[8,2,4096]{2,1,0:T(2,128)(2,1)S(1)}, u32[]{:S(2)}, u32[]{:S(2)}) async-start(bf16[8,2,4096]{2,1,0:T(2,128)(2,1)} %reshape.786), calls=%async_computation.1 | async-start | bytes 262144 | tf_op jit(solution)/shard_map/all_to_all | solution.py:177
  191.8 18.7 %all-to-all-start.2 = ((bf16[8,2,12288]{2,1,0:T(2,128)(2,1)}), bf16[8,2,12288]{2,1,0:T(2,128)(2,1)S(1)}, u32[]{:S(2)}, u32[]{:S(2)}) async-start(bf16[8,2,12288]{2,1,0:T(2,128)(2,1)} %reshape.788), calls=%async_computation.2 | async-start | bytes 786432 | tf_op jit(solution)/shard_map/all_to_all | solution.py:176
  228.4 11.4 all-to-all-start.3
  231.9 116.4 %all-gather.18.cloned.1.call-start = ((), (), s32[]{:S(2)}) async-start(), calls=%async_computation.21 | async-start | bytes 3538944 | tf_op jit(solution)/shard_map/all_gather | solution.py:193
  246.4 153.6 %all-gather.20.cloned.1.call-start = ((), (), s32[]{:S(2)}) async-start(), calls=%async_computation.22 | async-start | bytes 2924544 | tf_op jit(solution)/shard_map/all_gather | solution.py:127
  247.2 203.8 %all-gather.24.cloned.1.call-start = ((), (), s32[]{:S(2)}) async-start(), calls=%async_computation.24 | async-start | bytes 2924544 | tf_op jit(solution)/shard_map/all_gather | solution.py:129
  247.9 274.9 %all-gather.26.cloned.1.call-start = ((), (), s32[]{:S(2)}) async-start(), calls=%async_computation.26 | async-start | bytes 3538944 | tf_op jit(solution)/shard_map/all_gather | solution.py:209
  248.6 423.9 %reduce-scatter.12.cloned.1.call-start = ((), (), s32[]{:S(2)}) async-start(), calls=%async_computation.27 | async-start | bytes 7077888 | tf_op jit(solution)/shard_map/reduce_scatter | solution.py:234
  542.8 262.9 %reduce-scatter.10.cloned.1.call-start = ((), (), s32[]{:S(2)}) async-start(), calls=%async_computation.25 | async-start | bytes 7077888 | tf_op jit(solution)/shard_map/reduce_scatter | solution.py:207
  825.6 13.5 all-to-all-start.4
  830.2 138.7 %reduce-scatter.18.cloned.1.call-start = ((), (), s32[]{:S(2)}) async-start(), calls=%async_computation.30 | async-start | bytes 3342336 | tf_op jit(solution)/shard_map/reduce_scatter | solution.py:293
  830.5 18.3 %copy-start.9 = (f32[3,1024]{1,0:T(4,128)}, f32[3,1024]{1,0:T(4,128)S(1)}, u32[]{:S(2)}) copy-start(f32[3,1024]{1,0:T(4,128)S(1)} %log_add_fusion) | copy-start | bytes 36868
  867.1 153.5 %reduce-scatter.16.cloned.1.call-start = ((), (), s32[]{:S(2)}) async-start(), calls=%async_computation.29 | async-start | bytes 3342336 | tf_op jit(solution)/shard_map/reduce_scatter | solution.py:292
  903.3 227.6 %reduce-scatter.20.cloned.1.call-start = ((), (), s32[]{:S(2)}) async-start(), calls=%async_computation.31 | async-start | bytes 10027008 | tf_op jit(solution)/shard_map/reduce_scatter | solution.py:296
  908.4 333.3 %reduce-scatter.14.cloned.1.call-start = ((), (), s32[]{:S(2)}) async-start(), calls=%async_computation.28 | async-start | bytes 10027008 | tf_op jit(solution)/shard_map/reduce_scatter | solution.py:291
  941.8 392.8 %reduce-scatter.26.cloned.1.call-start = ((), (), s32[]{:S(2)}) async-start(), calls=%async_computation.34 | async-start | bytes 5849088 | tf_op jit(solution)/shard_map/reduce_scatter | solution.py:300
  950.4 471.2 %reduce-scatter.24.cloned.1.call-start = ((), (), s32[]{:S(2)}) async-start(), calls=%async_computation.33 | async-start | bytes 5849088 | tf_op jit(solution)/shard_map/reduce_scatter | solution.py:299
  958.8 552.4 %reduce-scatter.22.cloned.1.call-start = ((), (), s32[]{:S(2)}) async-start(), calls=%async_computation.32 | async-start | bytes 5849088 | tf_op jit(solution)/shard_map/reduce_scatter | solution.py:298
  967.3 634.3 %all-reduce.18.cloned.1.call-start = ((), (), s32[]{:S(2)}) async-start(), calls=%async_computation.35 | async-start | bytes 3145728 | tf_op jit(solution)/shard_map/psum | solution.py:302
  1246.0 87.5 %copy-start.31 = (f32[128]{0:T(128)S(1)}, f32[128]{0:T(128)}, u32[]{:S(2)}) copy-start(f32[128]{0:T(128)} %copy-done.30) | copy-start | bytes 1540
  (28 other events, 135.3 us)
Sparse Core Ops, SparseCore 0:
  10.5 48.8 all-gather.9
  61.8 45.1 all-gather.11
  109.5 56.4 all-gather.13
  168.4 55.5 all-gather.15
  226.3 49.6 all-gather.21
  278.1 70.1 all-gather.17
  350.7 49.2 all-gather.19
  402.5 48.3 all-gather.23
  452.6 70.1 all-gather.25
  542.9 129.5 reduce-scatter.11
  675.0 130.6 reduce-scatter.9
  867.2 74.9 reduce-scatter.17
  946.2 74.2 reduce-scatter.15
  1024.7 106.0 reduce-scatter.19
  1135.7 106.0 reduce-scatter.13
  1246.3 85.1 reduce-scatter.25
  1336.6 84.8 reduce-scatter.23
  1426.1 84.9 reduce-scatter.21
  1514.1 87.4 all-reduce.17
where the time goes:
time: 1620 us
  waiting for transfers between devices  1160 us (72%)
  blocking collectives  170 us (10%)
  matrix products  130 us (8%)
  other arithmetic  58.7 us (4%)
  local copies, waits for them, and re-layouts  52.8 us (3%)
  starting transfers between devices  24 us (1%)
  between operations  17.9 us (1%)
    reduce_scatter x1, waiting for transfers between devices, on_device(): lax.psum_scatter(partial_out, 'seq', scatter_dimension=1, tiled=True)  131 us
    reduce_scatter x1, waiting for transfers between devices, on_device(): lax.psum_scatter(grad_second_part, 'seq', scatter_dimension=1, tiled=True)  121 us
    reduce_scatter x1, waiting for transfers between devices, on_device(): lax.psum_scatter(query_weight_gradient, 'fsdp', scatter_dimension=0, tile...  111 us
    reduce_scatter x1, waiting for transfers between devices, on_device(): lax.psum_scatter(grad_wout, 'fsdp', scatter_dimension=1, tiled=True)  110 us
    unnamed x2, blocking collectives  102 us
    psum x1, waiting for transfers between devices, on_device(): lax.psum((owned[0], owned[1], owned[2], owned[3], owned[4], owned[5], own...  90.5 us
    reduce_scatter x1, waiting for transfers between devices, on_device(): lax.psum_scatter(grad_wgate, 'fsdp', scatter_dimension=0, tiled=True)  89.6 us
    reduce_scatter x1, waiting for transfers between devices, on_device(): lax.psum_scatter(up_weight_gradient, 'fsdp', scatter_dimension=0, tiled=T...  86.9 us
  transfers between devices with their start and end apart: 24, of which 18 were waited for; matrix products, arithmetic and copies ran while one was open for 10% of the time, Pallas kernels for 0%

commit v1 on v0

v1 whole, which is shorter than its diff:
```python
from functools import partial

import jax
import jax.numpy as jnp
from jax import lax
from jax.sharding import PartitionSpec as P

HEAD = 64
EPS = 1e-05
ROPE_BASE = 1000000.0
F32 = jnp.float32
BF16 = jnp.bfloat16
PAD = 896


def rms_norm(values, gain):
    inverse = lax.rsqrt(jnp.mean(values * values, axis=-1, keepdims=True) + EPS)
    return values * inverse * gain


def shift(size, by):
    return [(i, (i + by) % size) for i in range(size)]


def gather_seq(block):
    n = lax.axis_size("seq")
    me = lax.axis_index("seq")
    whole = jnp.zeros((n,) + block.shape, block.dtype)
    whole = lax.dynamic_update_index_in_dim(whole, block, me, 0)
    for by in range(1, n):
        got = lax.ppermute(block, "seq", shift(n, by))
        whole = lax.dynamic_update_index_in_dim(whole, got, (me - by) % n, 0)
    return whole


def scatter_sum_seq(blocks):
    n = lax.axis_size("seq")
    me = lax.axis_index("seq")
    got = [
        lax.ppermute(
            lax.dynamic_index_in_dim(blocks, (me + by) % n, 0, keepdims=False), "seq", shift(n, by)
        )
        for by in range(1, n)
    ]
    total = lax.dynamic_index_in_dim(blocks, me, 0, keepdims=False).astype(F32)
    for block in got:
        total = total + block.astype(F32)
    return total


def gather_fsdp(block):
    n = lax.axis_size("fsdp")
    me = lax.axis_index("fsdp")
    held = block[None]
    for bit in (1, 2):
        other = lax.ppermute(held, "fsdp", [(i, i ^ bit) for i in range(n)])
        low = (me & bit) == 0
        held = jnp.concatenate([jnp.where(low, held, other), jnp.where(low, other, held)], axis=0)
    quad = held.shape[0]
    whole = jnp.zeros((n,) + block.shape, block.dtype)
    whole = lax.dynamic_update_slice_in_dim(whole, held, me // quad * quad, 0)
    for by in range(quad, n, quad):
        got = lax.ppermute(held, "fsdp", shift(n, by))
        whole = lax.dynamic_update_slice_in_dim(whole, got, (me - by) % n // quad * quad, 0)
    return whole.reshape((n * block.shape[0],) + block.shape[1:])


def rotary(values, cosine, sine):
    half = values.shape[-1] // 2
    a, b = values[..., :half], values[..., half:]
    return jnp.concatenate([a * cosine - b * sine, b * cosine + a * sine], axis=-1)


def prep(raw, gain, cosine, sine):
    shaped = raw.reshape(raw.shape[0], -1, HEAD)
    return rotary(rms_norm(shaped, gain), cosine[:, None, :], sine[:, None, :]).reshape(raw.shape)


def mm(a, b):
    return jnp.dot(a, b, preferred_element_type=F32)


def mm_nt(a, b):
    return lax.dot_general(a, b, (((1,), (1,)), ((), ())), preferred_element_type=F32)


def mm_tn(a, b):
    return lax.dot_general(a, b, (((0,), (0,)), ((), ())), preferred_element_type=F32)


def masked_scores(q, k, allowed):
    scores = jnp.einsum("qhd,kd->hqk", q, k, preferred_element_type=F32) * HEAD**-0.5
    return jnp.where(allowed, scores, -1e30)


def attend(q, k, v, allowed):
    grouped = q.reshape(q.shape[0], -1, HEAD)
    scores = masked_scores(grouped, k, allowed)
    peak = jnp.max(scores, axis=-1, keepdims=True)
    exps = jnp.exp(scores - peak)
    total = jnp.sum(exps, axis=-1, keepdims=True)
    probs = (exps / total).astype(BF16)
    mixed = jnp.einsum("hqk,kd->qhd", probs, v, preferred_element_type=F32)
    return mixed.reshape(q.shape).astype(BF16), peak + jnp.log(total)


def attend_back(q, k, v, allowed, lse, grad):
    grouped = q.reshape(q.shape[0], -1, HEAD)
    probs = jnp.exp(masked_scores(grouped, k, allowed) - lse)
    grads = grad.reshape(grouped.shape)
    grad_probs = jnp.einsum("qhd,kd->hqk", grads, v, preferred_element_type=F32)
    inner = jnp.sum(probs * grad_probs, axis=-1, keepdims=True)
    grad_scores = (probs * (grad_probs - inner)).astype(BF16)
    gq = jnp.einsum("hqk,kd->qhd", grad_scores, k, preferred_element_type=F32) * HEAD**-0.5
    gk = jnp.einsum("hqk,qhd->kd", grad_scores, grouped, preferred_element_type=F32) * HEAD**-0.5
    gv = jnp.einsum("hqk,qhd->kd", probs.astype(BF16), grads, preferred_element_type=F32)
    return gq.reshape(q.shape).astype(BF16), gk.astype(BF16), gv.astype(BF16)


def lanes(array, width):
    return jnp.pad(array, ((0, 0), (0, width - array.shape[1])))


def rows(vector, count):
    return jnp.pad(vector, (0, count - vector.shape[0]))


def on_device(
    tokens,
    segments,
    out_grad,
    attn_gain,
    w_query,
    w_key,
    w_value,
    query_gain,
    key_gain,
    w_out,
    mlp_gain,
    w_gate,
    w_up,
    w_down,
):
    n_seq = lax.axis_size("seq")
    n_fsdp = lax.axis_size("fsdp")
    me = lax.axis_index("seq")
    local, width = tokens.shape[1:]
    length = local * n_seq
    shard = attn_gain.shape[0]
    q_all, kv_all = w_query.shape[1], w_key.shape[1]
    q_own, kv_own = q_all // n_seq, kv_all // n_seq
    hidden_own = w_gate.shape[1]
    gain_own = query_gain.shape[0]

    mlp_pack = jnp.concatenate(
        [w_out.T, lanes(w_gate, PAD), lanes(w_up, PAD), lanes(w_down.T, PAD)], axis=1
    )
    mlp_full = lax.all_gather(mlp_pack, "fsdp", axis=0, tiled=True)
    own = lax.dynamic_slice_in_dim
    head_pack = jnp.concatenate(
        [
            own(w_query, me * q_own, q_own, 1),
            own(w_key, me * kv_own, kv_own, 1),
            own(w_value, me * kv_own, kv_own, 1),
            attn_gain[:, None],
            mlp_gain[:, None],
            rows(query_gain, shard)[:, None],
            rows(key_gain, shard)[:, None],
        ],
        axis=1,
    )
    qkv_own = q_own + 2 * kv_own
    head_pack = lanes(head_pack, 384)

    segs = gather_seq(segments).reshape(length)
    x = tokens[0]
    x_all = gather_seq(x).reshape(length, width)
    head_full = gather_fsdp(head_pack)
    g_all = gather_seq(out_grad[0]).reshape(length, width)

    w_own = head_full[:, :qkv_own]
    gains = head_full[:, qkv_own : qkv_own + 4].astype(F32)
    attn_g, mlp_g = gains[:, 0], gains[:, 1]
    query_g = gains[:, 2].reshape(n_fsdp, shard)[:, :gain_own].reshape(-1)
    key_g = gains[:, 3].reshape(n_fsdp, shard)[:, :gain_own].reshape(-1)

    index = jnp.arange(length, dtype=jnp.int32)
    first = jnp.sum((segs == 0).astype(jnp.int32))
    second_ = jnp.sum((segs == 1).astype(jnp.int32))
    earlier = jnp.where(segs >= 1, first, 0) + jnp.where(segs >= 2, second_, 0)
    position = (index - earlier).astype(F32)
    frequency = ROPE_BASE ** (-2.0 * jnp.arange(HEAD // 2, dtype=F32) / HEAD)
    angles = position[:, None] * frequency
    cosine, sine = jnp.cos(angles), jnp.sin(angles)
    allowed = (index[None, :] <= index[:, None]) & (segs[None, :] == segs[:, None])

    normed_all = rms_norm(x_all.astype(F32), attn_g).astype(BF16)
    raw = mm(normed_all, w_own)
    q_raw, k_raw = raw[:, :q_own], raw[:, q_own : q_own + kv_own]
    v = raw[:, q_own + kv_own :].astype(BF16)
    prep_pos = partial(prep, cosine=cosine, sine=sine)
    q_f, q_back = jax.vjp(prep_pos, q_raw, query_g)
    k_f, k_back = jax.vjp(prep_pos, k_raw, key_g)
    q, k = q_f.astype(BF16), k_f.astype(BF16)
    attended, lse = attend(q, k, v, allowed)

    att_all = gather_seq(attended).transpose(1, 0, 2).reshape(length, q_all)
    w_out_t = mlp_full[:, :q_all]
    gate_w = mlp_full[:, q_all : q_all + PAD]
    up_w = mlp_full[:, q_all + PAD : q_all + 2 * PAD]
    down_t = mlp_full[:, q_all + 2 * PAD :]
    middle = x_all.astype(F32) + mm_nt(att_all, w_out_t)
    second = rms_norm(middle, mlp_g).astype(BF16)
    middle_own = lax.dynamic_slice_in_dim(middle, me * local, local, 0)

    gate_pre = mm(second, gate_w)
    upward = mm(second, up_w)
    sig = jax.nn.sigmoid(gate_pre)
    hidden = (gate_pre * sig * upward).astype(BF16)
    grad_hidden = mm(g_all, down_t)
    grad_gate = (grad_hidden * upward * sig * (1.0 + gate_pre * (1.0 - sig))).astype(BF16)
    grad_up = (grad_hidden * gate_pre * sig).astype(BF16)
    second_part = (mm_nt(grad_gate, gate_w) + mm_nt(grad_up, up_w)).astype(BF16)
    grad_second = scatter_sum_seq(second_part.reshape(n_seq, local, width))
    out_part = mm_nt(hidden, down_t).astype(BF16)
    mlp_out = scatter_sum_seq(out_part.reshape(n_seq, local, width))
    layer_out = (middle_own + mlp_out).astype(BF16)

    mlp_grads = jnp.concatenate(
        [mm_tn(second, grad_gate), mm_tn(second, grad_up), mm_tn(g_all, hidden)], axis=1
    ).astype(BF16)
    mlp_owned = lax.psum_scatter(mlp_grads, "fsdp", scatter_dimension=0, tiled=True).astype(F32)
    proj = lax.all_gather(
        jnp.concatenate([w_query, w_key, w_value], axis=1), "fsdp", axis=0, tiled=True
    )

    _, mlp_back = jax.vjp(rms_norm, middle_own, mlp_g)
    grad_middle_norm, grad_mlp_g = mlp_back(grad_second)
    grad_middle = out_grad[0].astype(F32) + grad_middle_norm
    branch = grad_middle.astype(BF16)
    grad_att = mm(branch, w_out_t).astype(BF16)
    grad_att_h = lax.all_to_all(
        grad_att.reshape(local, n_seq, q_own), "seq", split_axis=1, concat_axis=0, tiled=True
    ).reshape(length, q_own)
    branch_all = gather_seq(branch).reshape(length, width)
    gq, gk, gv = attend_back(q, k, v, allowed, lse, grad_att_h)
    gq_raw, grad_query_g = q_back(gq.astype(F32))
    gk_raw, grad_key_g = k_back(gk.astype(F32))
    g_qkv = jnp.concatenate([gq_raw.astype(BF16), gk_raw.astype(BF16), gv], axis=1)

    tok_qkv = lax.all_to_all(
        g_qkv.reshape(n_seq, local, qkv_own), "seq", split_axis=0, concat_axis=0, tiled=True
    )
    cut = (q_own, q_own + kv_own)
    tok_g = jnp.concatenate(
        [
            tok_qkv[:, :, : cut[0]].transpose(1, 0, 2).reshape(local, q_all),
            tok_qkv[:, :, cut[0] : cut[1]].transpose(1, 0, 2).reshape(local, kv_all),
            tok_qkv[:, :, cut[1] :].transpose(1, 0, 2).reshape(local, kv_all),
        ],
        axis=1,
    )
    grad_normed = mm_nt(tok_g, proj)
    _, attn_back = jax.vjp(rms_norm, x.astype(F32), attn_g)
    grad_x_norm, grad_attn_g = attn_back(grad_normed)
    grad_tokens = grad_middle + grad_x_norm

    def spread(vector):
        grid = vector.reshape(n_fsdp, gain_own)
        return jnp.pad(grid, ((0, 0), (0, shard - gain_own))).reshape(-1)

    att_grads = jnp.concatenate(
        [
            mm_tn(normed_all, g_qkv),
            mm_tn(branch_all, attended),
            grad_attn_g[:, None],
            grad_mlp_g[:, None],
            spread(grad_query_g)[:, None],
            spread(grad_key_g)[:, None],
        ],
        axis=1,
    )
    att_grads = lanes(att_grads.astype(BF16), 640)
    got = lax.all_to_all(
        att_grads.reshape(n_fsdp, shard, 640), "fsdp", split_axis=0, concat_axis=0, tiled=True
    )
    att_owned = jnp.sum(got.astype(F32), axis=0).astype(BF16)
    att_seq = gather_seq(att_owned).astype(F32)

    def side(start, stop):
        return att_seq[:, :, start:stop].transpose(1, 0, 2).reshape(shard, -1)

    gain_at = qkv_own + q_own
    gain_sums = jnp.sum(att_seq[:, :, gain_at : gain_at + 4], axis=0)
    return (
        layer_out[None],
        grad_tokens[None],
        gain_sums[:, 0],
        side(0, cut[0]),
        side(cut[0], cut[1]),
        side(cut[1], qkv_own),
        gain_sums[:gain_own, 2],
        gain_sums[:gain_own, 3],
        side(qkv_own, gain_at).T,
        gain_sums[:, 1],
        mlp_owned[:, :hidden_own],
        mlp_owned[:, PAD : PAD + hidden_own],
        mlp_owned[:, 2 * PAD : 2 * PAD + hidden_own].T,
    )


def solution(mesh):
    in_specs = (
        P("fsdp", "seq", None),
        P("fsdp", "seq"),
        P("fsdp", "seq", None),
        P("fsdp"),
        P("fsdp", None),
        P("fsdp", None),
        P("fsdp", None),
        P("fsdp"),
        P("fsdp"),
        P(None, "fsdp"),
        P("fsdp"),
        P("fsdp", "seq"),
        P("fsdp", "seq"),
        P("seq", "fsdp"),
    )
    out_specs = (
        P("fsdp", "seq", None),
        P("fsdp", "seq", None),
        P("fsdp"),
        P("fsdp", None),
        P("fsdp", None),
        P("fsdp", None),
        P("fsdp"),
        P("fsdp"),
        P(None, "fsdp"),
        P("fsdp"),
        P("fsdp", "seq"),
        P("fsdp", "seq"),
        P("seq", "fsdp"),
    )
    return jax.shard_map(
        on_device, mesh=mesh, in_specs=in_specs, out_specs=out_specs, check_vma=False
    )
```

time: 1620 us -> 614 us (0.38)
  waiting for transfers between devices: 1160 us -> 147 us
  blocking collectives: 170 us -> 44.9 us
  starting transfers between devices: 24 us -> 148 us
  local copies, waits for them, and re-layouts: 52.8 us -> 91.9 us
  matrix products: 130 us -> 102 us
    reduce_scatter x9 -> x0, waiting for transfers between devices: 702 us -> none  [the longest x1 131 us: on_device(): lax.psum_scatter(partial_out, 'seq', scatter_dimension=1, tiled=True)]
    all_gather x9 -> x2, waiting for transfers between devices: 337 us -> 0.02 us  [the longest x1 0.02 us: on_device(): lax.all_gather(jnp.concatenate([w_query, w_key, w_value], axis=1), 'fsdp'...]
    ppermute x0 -> x61, waiting for transfers between devices: none -> 147 us  [the longest x42 78 us: gather_seq(): got = lax.ppermute(block, 'seq', shift(n, by))]
    ppermute x0 -> x61, starting transfers between devices: none -> 138 us  [the longest x42 109 us: gather_seq(): got = lax.ppermute(block, 'seq', shift(n, by))]
    unnamed x2 -> x0, blocking collectives: 102 us -> none
    psum x1 -> x0, waiting for transfers between devices: 90.5 us -> none  [on_device(): lax.psum((owned[0], owned[1], owned[2], owned[3], owned[4], owned[5], own...]
    unnamed x10 -> x2, other arithmetic: 35.6 us -> 0.01 us
    dot_general x27 -> x21, matrix products: 130 us -> 102 us  [the longest x5 32.8 us: mm_nt(): lax.dot_general(a, b, (((1,), (1,)), ((), ())), preferred_element_type=F32)]
  transfers between devices with their start and end apart: 24 -> 66, of which waited for: 18 -> 27; matrix products, arithmetic and copies ran while one was open for 10% -> 39% of each run, Pallas kernels for 0% -> 0%
where the time goes in v1:
time: 614 us; the launch traced here: 603 us
  starting transfers between devices  148 us (24%)
  waiting for transfers between devices  147 us (24%)
  matrix products  102 us (17%)
  local copies, waits for them, and re-layouts  91.9 us (15%)
  other arithmetic  52.3 us (9%)
  blocking collectives  44.9 us (7%)
  between operations  16 us (3%)
    ppermute x42, starting transfers between devices, gather_seq(): got = lax.ppermute(block, 'seq', shift(n, by))  109 us
    ppermute x42, waiting for transfers between devices, gather_seq(): got = lax.ppermute(block, 'seq', shift(n, by))  78 us
    ppermute x14, waiting for transfers between devices, scatter_sum_seq(): lax.ppermute(lax.dynamic_index_in_dim(blocks, (me + by) % n, 0, keepdims=...  54.5 us
    all_to_all x1, blocking collectives, on_device(): lax.all_to_all(att_grads.reshape(n_fsdp, shard, 640), 'fsdp', split_axis=...  44.9 us
    dot_general x5, matrix products, mm_nt(): lax.dot_general(a, b, (((1,), (1,)), ((), ())), preferred_element_type=F32)  32.8 us
    dot_general x5, matrix products, mm(): return jnp.dot(a, b, preferred_element_type=F32)  28.8 us
    unnamed x152, local copies, waits for them, and re-layouts  26.6 us
    dynamic_update_slice x42, local copies, waits for them, and re-layouts, gather_seq(): whole = lax.dynamic_update_index_in_dim(whole, got, (me - by) % n, 0)  22.2 us
  transfers between devices with their start and end apart: 66, of which 27 were waited for; matrix products, arithmetic and copies ran while one was open for 39% of the time, Pallas kernels for 0%

profile of v1, /device:TPU:0, one launch (start us, length us, event | category | flops | bytes accessed | tf_op | source)
XLA Modules:
  0.0 602.7 jit_solution(1428305956190648583)
XLA Ops:
  28.1 7.7 %collective-permute-done.12 = s32[1,128]{1,0:T(1,128)} collective-permute-done((s32[1,128]{1,0:T(1,128)}, s32[1,128]{1,0:T(1,128)}, u32[]{:S(2)}, u32[]{:S(2)}) %collective-permute-start.12) | collective-permute-done | bytes 544 | tf_op jit(solution)/shard_map/ppermute | solution.py:31
  38.0 8.3 %collective-permute-done.13 = s32[1,128]{1,0:T(1,128)S(1)} collective-permute-done((s32[1,128]{1,0:T(1,128)S(1)}, s32[1,128]{1,0:T(1,128)S(1)}, u32[]{:S(2)}, u32[]{:S(2)}) %collective-permute-start.13) | collective-permute-done | bytes 544 | tf_op jit(solution)/shard_map/ppermute | solution.py:31
  46.3 5.9 collective-permute-done.14
  80.4 6.9 %collective-permute-done.8 = bf16[2,96,384]{2,1,0:T(8,128)(2,1)S(1)} collective-permute-done((bf16[2,96,384]{2,1,0:T(8,128)(2,1)S(1)}, bf16[2,96,384]{2,1,0:T(8,128)(2,1)S(1)}, u32[]{:S(2)}, u32[]{:S(2)}) %collective-permute-start.8) | collective-permute-done | bytes 147488 | tf_op jit(solution)/shard_map/ppermute | solution.py:56
  99.8 7.4 %collective-permute-done.4 = bf16[128,1536]{1,0:T(8,128)(2,1)S(1)} collective-permute-done((bf16[128,1536]{1,0:T(8,128)(2,1)}, bf16[128,1536]{1,0:T(8,128)(2,1)S(1)}, u32[]{:S(2)}, u32[]{:S(2)}) %collective-permute-start.4) | collective-permute-done | bytes 393248 | tf_op jit(solution)/shard_map/ppermute | solution.py:31
  114.8 8.0 %collective-permute-start.37 = (bf16[128,1536]{1,0:T(8,128)(2,1)S(1)}, bf16[128,1536]{1,0:T(8,128)(2,1)S(1)}, u32[]{:S(2)}, u32[]{:S(2)}) collective-permute-start(bf16[128,1536]{1,0:T(8,128)(2,1)S(1)} %bitcast.319), channel_id=1, source_target_pairs={{0,80},{16,96},{32,112},{48,0},{64,16},{80,32},{96,48},{112,64},{1... | collective-permute-start | bytes 1179656 | tf_op jit(solution)/shard_map/ppermute | solution.py:31
  151.6 5.1 collective-permute-done.10
  189.1 16.7 %collective-permute-start.19 = (bf16[1024,192]{0,1:T(8,128)(2,1)S(1)}, bf16[1024,192]{0,1:T(8,128)(2,1)S(1)}, u32[]{:S(2)}, u32[]{:S(2)}) collective-permute-start(bf16[1024,192]{0,1:T(8,128)(2,1)S(1)} %bitcast.341), channel_id=1, source_target_pairs={{0,16},{16,32},{32,48},{48,64},{64,80},{80,96},{96,112},{112,0},{1... | collective-permute-start | bytes 1179656 | tf_op jit(solution)/shard_map/ppermute | solution.py:31
  219.2 9.6 %collective-permute-done.20 = bf16[1024,192]{0,1:T(8,128)(2,1)S(1)} collective-permute-done((bf16[1024,192]{0,1:T(8,128)(2,1)S(1)}, bf16[1024,192]{0,1:T(8,128)(2,1)S(1)}, u32[]{:S(2)}, u32[]{:S(2)}) %collective-permute-start.20) | collective-permute-done | bytes 393248 | tf_op jit(solution)/shard_map/ppermute | solution.py:31
  228.8 13.1 %collective-permute-start.25 = (bf16[1024,192]{0,1:T(8,128)(2,1)S(1)}, bf16[1024,192]{0,1:T(8,128)(2,1)S(1)}, u32[]{:S(2)}, u32[]{:S(2)}) collective-permute-start(bf16[1024,192]{0,1:T(8,128)(2,1)S(1)} %bitcast.348), channel_id=1, source_target_pairs={{0,112},{16,0},{32,16},{48,32},{64,48},{80,64},{96,80},{112,96},{1... | collective-permute-start | bytes 1179656 | tf_op jit(solution)/shard_map/ppermute | solution.py:31
  249.5 8.5 %multiply_reduce_fusion = (f32[1024]{0:T(1024)S(1)}, f32[1024,1536]{1,0:T(8,128)S(1)}) fusion(bf16[1024,1536]{0,1:T(8,128)(2,1)} %bitcast.43, bf16[1536,4224]{1,0:T(8,128)(2,1)} %all-gather.3.cloned.1.call-done, bf16[8,128,1536]{2,1,0:T(8,128)(2,1)S(1)} %bitcast_dynamic-update-slice_fusion.22), kind=kOutput, calls=%fused_computation.22 | convolution fusion | flops 4838128640 | bytes 17305600 | tf_op jit(solution)/shard_map/dot_general | solution.py:84
  258.7 9.5 %fusion.20 = f32[1024,896]{1,0:T(8,128)} fusion(bf16[1024,1536]{1,0:T(8,128)(2,1)S(1)} %multiply_convert_fusion, bf16[1536,4224]{1,0:T(8,128)(2,1)} %all-gather.3.cloned.1.call-done), kind=kOutput, calls=%fused_computation.47 | convolution fusion | flops 2818572288 | bytes 9568256 | tf_op jit(solution)/shard_map/dot_general | solution.py:80
  268.2 5.3 fusion.24
  273.6 9.6 %multiply_convert_fusion.1 = (bf16[1024,896]{1,0:T(8,128)(2,1)}, bf16[1024,896]{1,0:T(8,128)(2,1)S(1)}, bf16[1024,896]{1,0:T(8,128)(2,1)}) fusion(f32[1024,896]{1,0:T(8,128)} %fusion.24, f32[1024,896]{1,0:T(8,128)} %fusion.20, bf16[1024,1536]{1,0:T(8,128)(2,1)} %bitcast.64, bf16[1536,4224]{1,0:T(8,128)(2,1)S(1)} %bitcast.367), kind=kOutput, calls=%fused_computation.30 | convolution fusion | flops 2833252352 | bytes 18743296 | tf_op jit(solution)/shard_map/dot_general | solution.py:80
  283.2 5.4 fusion.22
  288.5 6.1 %add_convert_fusion = bf16[1024,1536]{1,0:T(8,128)(2,1)S(1)} fusion(f32[1024,1536]{1,0:T(8,128)} %fusion.22, bf16[1024,896]{1,0:T(8,128)(2,1)} %get-tuple-element.82, bf16[1536,4224]{1,0:T(8,128)(2,1)S(1)} %bitcast.367), kind=kOutput, calls=%fused_computation.20 | convolution fusion | flops 2821718016 | bytes 14024704 | tf_op jit(solution)/shard_map/dot_general | solution.py:84
  298.3 5.2 convolution_convert_fusion
  304.0 5.4 collective-permute-start.28
  318.5 11.9 %collective-permute-done.41 = bf16[128,1536]{1,0:T(8,128)(2,1)S(1)} collective-permute-done((bf16[128,1536]{1,0:T(8,128)(2,1)S(1)}, bf16[128,1536]{1,0:T(8,128)(2,1)S(1)}, u32[]{:S(2)}, u32[]{:S(2)}) %collective-permute-start.41) | collective-permute-done | bytes 393248 | tf_op jit(solution)/shard_map/ppermute | solution.py:40
  330.5 16.3 %collective-permute-done.27 = bf16[128,1536]{1,0:T(8,128)(2,1)S(1)} collective-permute-done((bf16[128,1536]{1,0:T(8,128)(2,1)S(1)}, bf16[128,1536]{1,0:T(8,128)(2,1)S(1)}, u32[]{:S(2)}, u32[]{:S(2)}) %collective-permute-start.27) | collective-permute-done | bytes 393248 | tf_op jit(solution)/shard_map/ppermute | solution.py:40
  346.7 6.6 %convolution_convert_fusion.1 = bf16[1536,896]{0,1:T(8,128)(2,1)} fusion(bf16[1024,1536]{1,0:T(8,128)(2,1)} %bitcast.64, bf16[1024,896]{1,0:T(8,128)(2,1)S(1)} %copy-done.63), kind=kOutput, calls=%fused_computation.34 | convolution fusion | flops 2819948544 | bytes 7733248 | tf_op jit(solution)/shard_map/dot_general | solution.py:88
  367.8 6.1 %collective-permute-done.43 = bf16[128,1536]{1,0:T(8,128)(2,1)S(1)} collective-permute-done((bf16[128,1536]{1,0:T(8,128)(2,1)S(1)}, bf16[128,1536]{1,0:T(8,128)(2,1)S(1)}, u32[]{:S(2)}, u32[]{:S(2)}) %collective-permute-start.43) | collective-permute-done | bytes 393248 | tf_op jit(solution)/shard_map/ppermute | solution.py:40
  374.0 15.9 %collective-permute-done.45 = bf16[128,1536]{1,0:T(8,128)(2,1)S(1)} collective-permute-done((bf16[128,1536]{1,0:T(8,128)(2,1)S(1)}, bf16[128,1536]{1,0:T(8,128)(2,1)S(1)}, u32[]{:S(2)}, u32[]{:S(2)}) %collective-permute-start.45) | collective-permute-done | bytes 393248 | tf_op jit(solution)/shard_map/ppermute | solution.py:40
  396.8 5.5 all-to-all-start
  402.3 7.1 %pad_maximum_fusion = bf16[1536,2688]{0,1:T(8,128)(2,1)} fusion(bf16[1536,896]{0,1:T(8,128)(2,1)} %convolution_convert_fusion.1, bf16[1536,896]{0,1:T(8,128)(2,1)} %convolution_convert_fusion.2, bf16[1536,896]{0,1:T(8,128)(2,1)} %convolution_convert_fusion.3), kind=kLoop, calls=%fused_computation.11 | loop fusion | flops 24772608 | bytes 16515072 | tf_op jit(solution)/shard_map/concatenate | solution.py:229
  409.4 11.2 %copy.134 = bf16[1536,2688]{1,0:T(8,128)(2,1)} copy(bf16[1536,2688]{0,1:T(8,128)(2,1)} %pad_maximum_fusion) | data formatting | bytes 16515072
  434.7 6.3 %fusion = (f32[3,1024]{1,0:T(4,128)S(1)}, f32[1024,1024,3]{1,0,2:T(8,128)S(1)}) fusion(f32[3,1024,1024]{1,2,0:T(8,128)} %copy-done, f32[3,1024]{1,0:T(4,128)S(1)} %log_add_fusion, bf16[1024,3,64]{0,2,1:T(8,128)(2,1)S(1)} %reshape_reshape.3, f32[1024,320]{0,1:T(8,128)} %copy-done.10), kind=kOutput, calls=%fused_computation.2 | convolution fusion | flops 412087296 | bytes 25714688 | tf_op jit(solution)/shard_map/qhd,kd->hqk/dot_general | solution.py:111
  441.1 8.9 %fusion.2 = bf16[3,1024,1024]{1,2,0:T(8,128)(2,1)S(1)} fusion(f32[1024,1024,3]{1,0,2:T(8,128)S(1)} %get-tuple-element.134, f32[3,1024,1024]{1,2,0:T(8,128)} %copy-done, f32[3,1024]{1,0:T(4,128)S(1)} %get-tuple-element.133, f32[3,1024]{1,0:T(4,128)S(1)} %log_add_fusion), kind=kLoop, calls=%fused_computation.4 | loop fusion | flops 12582912 | bytes 31481856 | tf_op jit(solution)/shard_map/convert_element_type | solution.py:113
  483.7 8.1 %collective-permute-done.53 = bf16[128,1536]{1,0:T(8,128)(2,1)S(1)} collective-permute-done((bf16[128,1536]{1,0:T(8,128)(2,1)S(1)}, bf16[128,1536]{1,0:T(8,128)(2,1)S(1)}, u32[]{:S(2)}, u32[]{:S(2)}) %collective-permute-start.53) | collective-permute-done | bytes 393248 | tf_op jit(solution)/shard_map/ppermute | solution.py:31
  495.6 7.6 %fusion.60 = (bf16[1536]{0:T(1024)(128)(2,1)S(1)}, f32[128]{0:T(128)}, f32[128,1536]{1,0:T(8,128)}) fusion(f32[128]{0:T(128)} %fusion.110, bf16[1,128,1536]{2,1,0:T(8,128)(2,1)S(1)} %copy-done.9, f32[1536]{0:T(1024)S(1)} %copy-done.38, bf16[1536,2560]{1,0:T(8,128)(2,1)} %all-gather.5.cloned.1.call-done, bf16[128,512]{0,1:T(8,128)(2,1)S(1)} %bitcast.358, ...), kind=kOutput, calls=%fused_computation.91 | convolution fusion | flops 1009973632 | bytes 9709568 | tf_op jit(solution)/shard_map/dot_general | solution.py:84
  503.3 5.4 concatenate.46
  511.7 44.9 %all_to_all.25 = bf16[16,96,640]{2,1,0:T(8,128)(2,1)S(1)} all-to-all(bf16[16,96,640]{2,1,0:T(8,128)(2,1)S(1)} %bitcast.314), channel_id=1, replica_groups=mesh['seq'=8,'fsdp'=16] {'fsdp'}, dimensions={0} | all-to-all | bytes 3932160 | tf_op jit(solution)/shard_map/all_to_all | solution.py:284
  (436 shorter events, 281.0 us)
Async XLA Ops:
  7.2 242.3 %all-gather.3.cloned.1.call-start = ((), (), s32[]{:S(2)}) async-start(), calls=%async_computation.4 | async-start | bytes 13787136 | tf_op jit(solution)/shard_map/all_gather | solution.py:158
  9.6 486.0 %all-gather.5.cloned.1.call-start = ((), (), s32[]{:S(2)}) async-start(), calls=%async_computation.5 | async-start | bytes 8355840 | tf_op jit(solution)/shard_map/all_gather | solution.py:233
  9.6 81.7 %collective-permute-start = (bf16[128,1536]{1,0:T(8,128)(2,1)}, bf16[128,1536]{1,0:T(8,128)(2,1)}, u32[]{:S(2)}, u32[]{:S(2)}) collective-permute-start(bf16[128,1536]{1,0:T(8,128)(2,1)} %bitcast.322), channel_id=1, source_target_pairs={{0,16},{16,32},{32,48},{48,64},{64,80},{80,96},{96,112},{112,0},{1... | collective-permute-start | bytes 1179656 | tf_op jit(solution)/shard_map/ppermute | solution.py:31
  11.3 81.2 %collective-permute-start.1 = (bf16[128,1536]{1,0:T(8,128)(2,1)}, bf16[128,1536]{1,0:T(8,128)(2,1)}, u32[]{:S(2)}, u32[]{:S(2)}) collective-permute-start(bf16[128,1536]{1,0:T(8,128)(2,1)} %bitcast.323), channel_id=1, source_target_pairs={{0,32},{16,48},{32,64},{48,80},{64,96},{80,112},{96,0},{112,16},{1... | collective-permute-start | bytes 1179656 | tf_op jit(solution)/shard_map/ppermute | solution.py:31
  12.9 81.3 %collective-permute-start.2 = (bf16[128,1536]{1,0:T(8,128)(2,1)}, bf16[128,1536]{1,0:T(8,128)(2,1)}, u32[]{:S(2)}, u32[]{:S(2)}) collective-permute-start(bf16[128,1536]{1,0:T(8,128)(2,1)} %bitcast.324), channel_id=1, source_target_pairs={{0,48},{16,64},{32,80},{48,96},{64,112},{80,0},{96,16},{112,32},{1... | collective-permute-start | bytes 1179656 | tf_op jit(solution)/shard_map/ppermute | solution.py:31
  15.1 81.6 %collective-permute-start.3 = (bf16[128,1536]{1,0:T(8,128)(2,1)}, bf16[128,1536]{1,0:T(8,128)(2,1)}, u32[]{:S(2)}, u32[]{:S(2)}) collective-permute-start(bf16[128,1536]{1,0:T(8,128)(2,1)} %bitcast.325), channel_id=1, source_target_pairs={{0,64},{16,80},{32,96},{48,112},{64,0},{80,16},{96,32},{112,48},{1... | collective-permute-start | bytes 1179656 | tf_op jit(solution)/shard_map/ppermute | solution.py:31
  94.2 31.5 %collective-permute-start.33 = (bf16[128,1536]{1,0:T(8,128)(2,1)S(1)}, bf16[128,1536]{1,0:T(8,128)(2,1)S(1)}, u32[]{:S(2)}, u32[]{:S(2)}) collective-permute-start(bf16[128,1536]{1,0:T(8,128)(2,1)S(1)} %bitcast.315), channel_id=1, source_target_pairs={{0,16},{16,32},{32,48},{48,64},{64,80},{80,96},{96,112},{112,0},{1... | collective-permute-start | bytes 1179656 | tf_op jit(solution)/shard_map/ppermute | solution.py:31
  96.7 30.2 %collective-permute-start.34 = (bf16[128,1536]{1,0:T(8,128)(2,1)S(1)}, bf16[128,1536]{1,0:T(8,128)(2,1)S(1)}, u32[]{:S(2)}, u32[]{:S(2)}) collective-permute-start(bf16[128,1536]{1,0:T(8,128)(2,1)S(1)} %bitcast.316), channel_id=1, source_target_pairs={{0,32},{16,48},{32,64},{48,80},{64,96},{80,112},{96,0},{112,16},{1... | collective-permute-start | bytes 1179656 | tf_op jit(solution)/shard_map/ppermute | solution.py:31
  107.3 26.8 %collective-permute-start.35 = (bf16[128,1536]{1,0:T(8,128)(2,1)S(1)}, bf16[128,1536]{1,0:T(8,128)(2,1)S(1)}, u32[]{:S(2)}, u32[]{:S(2)}) collective-permute-start(bf16[128,1536]{1,0:T(8,128)(2,1)S(1)} %bitcast.317), channel_id=1, source_target_pairs={{0,48},{16,64},{32,80},{48,96},{64,112},{80,0},{96,16},{112,32},{1... | collective-permute-start | bytes 1179656 | tf_op jit(solution)/shard_map/ppermute | solution.py:31
  110.0 28.1 %collective-permute-start.36 = (bf16[128,1536]{1,0:T(8,128)(2,1)S(1)}, bf16[128,1536]{1,0:T(8,128)(2,1)S(1)}, u32[]{:S(2)}, u32[]{:S(2)}) collective-permute-start(bf16[128,1536]{1,0:T(8,128)(2,1)S(1)} %bitcast.318), channel_id=1, source_target_pairs={{0,64},{16,80},{32,96},{48,112},{64,0},{80,16},{96,32},{112,48},{1... | collective-permute-start | bytes 1179656 | tf_op jit(solution)/shard_map/ppermute | solution.py:31
  114.8 31.6 %collective-permute-start.37 = (bf16[128,1536]{1,0:T(8,128)(2,1)S(1)}, bf16[128,1536]{1,0:T(8,128)(2,1)S(1)}, u32[]{:S(2)}, u32[]{:S(2)}) collective-permute-start(bf16[128,1536]{1,0:T(8,128)(2,1)S(1)} %bitcast.319), channel_id=1, source_target_pairs={{0,80},{16,96},{32,112},{48,0},{64,16},{80,32},{96,48},{112,64},{1... | collective-permute-start | bytes 1179656 | tf_op jit(solution)/shard_map/ppermute | solution.py:31
  127.0 78.8 %collective-permute-start.39 = (bf16[128,1536]{1,0:T(8,128)(2,1)S(1)}, bf16[128,1536]{1,0:T(8,128)(2,1)}, u32[]{:S(2)}, u32[]{:S(2)}) collective-permute-start(bf16[128,1536]{1,0:T(8,128)(2,1)S(1)} %bitcast.321), channel_id=1, source_target_pairs={{0,112},{16,0},{32,16},{48,32},{64,48},{80,64},{96,80},{112,96},{1... | collective-permute-start | bytes 1179656 | tf_op jit(solution)/shard_map/ppermute | solution.py:31
  189.1 26.8 %collective-permute-start.19 = (bf16[1024,192]{0,1:T(8,128)(2,1)S(1)}, bf16[1024,192]{0,1:T(8,128)(2,1)S(1)}, u32[]{:S(2)}, u32[]{:S(2)}) collective-permute-start(bf16[1024,192]{0,1:T(8,128)(2,1)S(1)} %bitcast.341), channel_id=1, source_target_pairs={{0,16},{16,32},{32,48},{48,64},{64,80},{80,96},{96,112},{112,0},{1... | collective-permute-start | bytes 1179656 | tf_op jit(solution)/shard_map/ppermute | solution.py:31
  207.6 35.2 %collective-permute-start.21 = (bf16[1024,192]{0,1:T(8,128)(2,1)S(1)}, bf16[1024,192]{0,1:T(8,128)(2,1)S(1)}, u32[]{:S(2)}, u32[]{:S(2)}) collective-permute-start(bf16[1024,192]{0,1:T(8,128)(2,1)S(1)} %bitcast.343), channel_id=1, source_target_pairs={{0,48},{16,64},{32,80},{48,96},{64,112},{80,0},{96,16},{112,32},{1... | collective-permute-start | bytes 1179656 | tf_op jit(solution)/shard_map/ppermute | solution.py:31
  208.0 35.5 %collective-permute-start.22 = (bf16[1024,192]{0,1:T(8,128)(2,1)S(1)}, bf16[1024,192]{0,1:T(8,128)(2,1)S(1)}, u32[]{:S(2)}, u32[]{:S(2)}) collective-permute-start(bf16[1024,192]{0,1:T(8,128)(2,1)S(1)} %bitcast.344), channel_id=1, source_target_pairs={{0,64},{16,80},{32,96},{48,112},{64,0},{80,16},{96,32},{112,48},{1... | collective-permute-start | bytes 1179656 | tf_op jit(solution)/shard_map/ppermute | solution.py:31
  211.8 32.5 %collective-permute-start.23 = (bf16[1024,192]{0,1:T(8,128)(2,1)S(1)}, bf16[1024,192]{0,1:T(8,128)(2,1)S(1)}, u32[]{:S(2)}, u32[]{:S(2)}) collective-permute-start(bf16[1024,192]{0,1:T(8,128)(2,1)S(1)} %bitcast.345), channel_id=1, source_target_pairs={{0,80},{16,96},{32,112},{48,0},{64,16},{80,32},{96,48},{112,64},{1... | collective-permute-start | bytes 1179656 | tf_op jit(solution)/shard_map/ppermute | solution.py:31
  215.8 29.9 %collective-permute-start.24 = (bf16[1024,192]{0,1:T(8,128)(2,1)S(1)}, bf16[1024,192]{0,1:T(8,128)(2,1)S(1)}, u32[]{:S(2)}, u32[]{:S(2)}) collective-permute-start(bf16[1024,192]{0,1:T(8,128)(2,1)S(1)} %bitcast.347), channel_id=1, source_target_pairs={{0,96},{16,112},{32,0},{48,16},{64,32},{80,48},{96,64},{112,80},{1... | collective-permute-start | bytes 1179656 | tf_op jit(solution)/shard_map/ppermute | solution.py:31
  297.9 32.5 %collective-permute-start.41 = (bf16[128,1536]{1,0:T(8,128)(2,1)S(1)}, bf16[128,1536]{1,0:T(8,128)(2,1)S(1)}, u32[]{:S(2)}, u32[]{:S(2)}) collective-permute-start(bf16[128,1536]{1,0:T(8,128)(2,1)S(1)} %get-tuple-element.93), channel_id=1, source_target_pairs={{0,32},{16,48},{32,64},{48,80},{64,96},{80,112},{96,0},{112,16},{1... | collective-permute-start | bytes 1179656 | tf_op jit(solution)/shard_map/ppermute | solution.py:40
  304.0 42.7 %collective-permute-start.27 = (bf16[128,1536]{1,0:T(8,128)(2,1)S(1)}, bf16[128,1536]{1,0:T(8,128)(2,1)S(1)}, u32[]{:S(2)}, u32[]{:S(2)}) collective-permute-start(bf16[128,1536]{1,0:T(8,128)(2,1)S(1)} %get-tuple-element.100), channel_id=1, source_target_pairs={{0,32},{16,48},{32,64},{48,80},{64,96},{80,112},{96,0},{112,16},{1... | collective-permute-start | bytes 1179656 | tf_op jit(solution)/shard_map/ppermute | solution.py:40
  304.0 49.4 %collective-permute-start.28 = (bf16[128,1536]{1,0:T(8,128)(2,1)S(1)}, bf16[128,1536]{1,0:T(8,128)(2,1)S(1)}, u32[]{:S(2)}, u32[]{:S(2)}) collective-permute-start(bf16[128,1536]{1,0:T(8,128)(2,1)S(1)} %get-tuple-element.99), channel_id=1, source_target_pairs={{0,48},{16,64},{32,80},{48,96},{64,112},{80,0},{96,16},{112,32},{1... | collective-permute-start | bytes 1179656 | tf_op jit(solution)/shard_map/ppermute | solution.py:40
  318.5 34.9 %collective-permute-start.29 = (bf16[128,1536]{1,0:T(8,128)(2,1)S(1)}, bf16[128,1536]{1,0:T(8,128)(2,1)S(1)}, u32[]{:S(2)}, u32[]{:S(2)}) collective-permute-start(bf16[128,1536]{1,0:T(8,128)(2,1)S(1)} %get-tuple-element.98), channel_id=1, source_target_pairs={{0,64},{16,80},{32,96},{48,112},{64,0},{80,16},{96,32},{112,48},{1... | collective-permute-start | bytes 1179656 | tf_op jit(solution)/shard_map/ppermute | solution.py:40
  330.5 28.0 %collective-permute-start.31 = (bf16[128,1536]{1,0:T(8,128)(2,1)S(1)}, bf16[128,1536]{1,0:T(8,128)(2,1)S(1)}, u32[]{:S(2)}, u32[]{:S(2)}) collective-permute-start(bf16[128,1536]{1,0:T(8,128)(2,1)S(1)} %get-tuple-element.96), channel_id=1, source_target_pairs={{0,96},{16,112},{32,0},{48,16},{64,32},{80,48},{96,64},{112,80},{1... | collective-permute-start | bytes 1179656 | tf_op jit(solution)/shard_map/ppermute | solution.py:40
  358.5 31.4 %collective-permute-start.45 = (bf16[128,1536]{1,0:T(8,128)(2,1)S(1)}, bf16[128,1536]{1,0:T(8,128)(2,1)S(1)}, u32[]{:S(2)}, u32[]{:S(2)}) collective-permute-start(bf16[128,1536]{1,0:T(8,128)(2,1)S(1)} %get-tuple-element.89), channel_id=1, source_target_pairs={{0,96},{16,112},{32,0},{48,16},{64,32},{80,48},{96,64},{112,80},{1... | collective-permute-start | bytes 1179656 | tf_op jit(solution)/shard_map/ppermute | solution.py:40
  358.8 31.1 %collective-permute-start.46 = (bf16[128,1536]{1,0:T(8,128)(2,1)S(1)}, bf16[128,1536]{1,0:T(8,128)(2,1)S(1)}, u32[]{:S(2)}, u32[]{:S(2)}) collective-permute-start(bf16[128,1536]{1,0:T(8,128)(2,1)S(1)} %get-tuple-element.88), channel_id=1, source_target_pairs={{0,112},{16,0},{32,16},{48,32},{64,48},{80,64},{96,80},{112,96},{1... | collective-permute-start | bytes 1179656 | tf_op jit(solution)/shard_map/ppermute | solution.py:40
  396.8 35.7 %all-to-all-start = ((bf16[128,8,192]{0,2,1:T(8,128)(2,1)}), bf16[128,8,192]{0,2,1:T(8,128)(2,1)S(1)}, u32[]{:S(2)}, u32[]{:S(2)}) async-start(bf16[128,8,192]{0,2,1:T(8,128)(2,1)} %bitcast.338), calls=%async_computation | async-start | bytes 786432 | tf_op jit(solution)/shard_map/all_to_all | solution.py:242
  402.3 189.2 %reduce-scatter.4.cloned.1.call-start = ((), (), s32[]{:S(2)}) async-start(), calls=%async_computation.6 | async-start | bytes 8773632
  420.7 52.5 %collective-permute-start.47 = (bf16[128,1536]{1,0:T(8,128)(2,1)}, bf16[128,1536]{1,0:T(8,128)(2,1)}, u32[]{:S(2)}, u32[]{:S(2)}) collective-permute-start(bf16[128,1536]{1,0:T(8,128)(2,1)} %copy-done.27), channel_id=1, source_target_pairs={{0,16},{16,32},{32,48},{48,64},{64,80},{80,96},{96,112},{112,0},{1... | collective-permute-start | bytes 1179656 | tf_op jit(solution)/shard_map/ppermute | solution.py:31
  422.9 54.5 %collective-permute-start.48 = (bf16[128,1536]{1,0:T(8,128)(2,1)}, bf16[128,1536]{1,0:T(8,128)(2,1)}, u32[]{:S(2)}, u32[]{:S(2)}) collective-permute-start(bf16[128,1536]{1,0:T(8,128)(2,1)} %copy-done.27), channel_id=1, source_target_pairs={{0,32},{16,48},{32,64},{48,80},{64,96},{80,112},{96,0},{112,16},{1... | collective-permute-start | bytes 1179656 | tf_op jit(solution)/shard_map/ppermute | solution.py:31
  424.2 56.3 %collective-permute-start.49 = (bf16[128,1536]{1,0:T(8,128)(2,1)}, bf16[128,1536]{1,0:T(8,128)(2,1)}, u32[]{:S(2)}, u32[]{:S(2)}) collective-permute-start(bf16[128,1536]{1,0:T(8,128)(2,1)} %copy-done.27), channel_id=1, source_target_pairs={{0,48},{16,64},{32,80},{48,96},{64,112},{80,0},{96,16},{112,32},{1... | collective-permute-start | bytes 1179656 | tf_op jit(solution)/shard_map/ppermute | solution.py:31
  426.3 55.3 %collective-permute-start.50 = (bf16[128,1536]{1,0:T(8,128)(2,1)}, bf16[128,1536]{1,0:T(8,128)(2,1)}, u32[]{:S(2)}, u32[]{:S(2)}) collective-permute-start(bf16[128,1536]{1,0:T(8,128)(2,1)} %copy-done.27), channel_id=1, source_target_pairs={{0,64},{16,80},{32,96},{48,112},{64,0},{80,16},{96,32},{112,48},{1... | collective-permute-start | bytes 1179656 | tf_op jit(solution)/shard_map/ppermute | solution.py:31
  428.3 54.3 %collective-permute-start.51 = (bf16[128,1536]{1,0:T(8,128)(2,1)}, bf16[128,1536]{1,0:T(8,128)(2,1)}, u32[]{:S(2)}, u32[]{:S(2)}) collective-permute-start(bf16[128,1536]{1,0:T(8,128)(2,1)} %copy-done.27), channel_id=1, source_target_pairs={{0,80},{16,96},{32,112},{48,0},{64,16},{80,32},{96,48},{112,64},{1... | collective-permute-start | bytes 1179656 | tf_op jit(solution)/shard_map/ppermute | solution.py:31
  461.7 31.7 %all-to-all-start.1 = ((bf16[8,128,320]{1,2,0:T(8,128)(2,1)}), bf16[8,128,320]{1,2,0:T(8,128)(2,1)}, u32[]{:S(2)}, u32[]{:S(2)}) async-start(bf16[8,128,320]{1,2,0:T(8,128)(2,1)} %copy_bitcast_fusion), calls=%async_computation.1 | async-start | bytes 1310720 | tf_op jit(solution)/shard_map/all_to_all | solution.py:251
  (106 other events, 1549.4 us)
Sparse Core Ops, SparseCore 0:
  10.5 106.2 all-gather.2
  119.9 82.5 all-gather.4
  420.8 136.3 reduce-scatter.3

commit v2 on v1

v2 whole, which is shorter than its diff:
```python
import functools

import jax
import jax.numpy as jnp
from jax import lax
from jax.experimental import pallas as pl
from jax.experimental.pallas import tpu as pltpu
from jax.sharding import PartitionSpec as P

HEAD = 64
EPS = 1e-05
ROPE_BASE = 1000000.0
F32 = jnp.float32
BF16 = jnp.bfloat16
PAD = 896
HALVES = 2
VMEM = 56 * 2**20


def dot(a, b, ca, cb):
    return lax.dot_general(a, b, (((ca,), (cb,)), ((), ())), preferred_element_type=F32)


def shape(*dims, dtype=BF16):
    return jax.ShapeDtypeStruct(dims, dtype)


def cost(micros):
    return pl.CostEstimate(flops=int(micros * 1.15e9), bytes_accessed=2**10, transcendentals=0)


def angles_of(freq_ref, position):
    turn = freq_ref[...] * position
    return jnp.cos(turn), jnp.sin(turn)


def mask_of(rows, start, index, heads):
    row = lax.broadcasted_iota(jnp.int32, (rows, start.shape[1]), 0).astype(F32)
    allowed = (row >= start) & (row <= index)
    return jnp.concatenate([allowed] * heads, axis=1)


PIECES = (
    (0, 0, 0, 1),
    (0, 1, 0, 1),
    (-1, 0, 0, 1),
    (1, 0, 0, 1),
    (-1, 1, 0, 1),
    (1, 1, 0, 1),
    (2, 0, 0, 2),
    (2, 0, 1, 2),
    (2, 1, 0, 2),
    (2, 1, 1, 2),
)


STEPS = (0, -1, 1, 2)


def block_at(me_ref, dy, dx, n_seq):
    y, x = me_ref[0] // 2, me_ref[0] % 2
    return (y + dy + n_seq // 2) % (n_seq // 2) * 2 + (x + dx) % 2


def first_row(me_ref, piece, n_seq, rows):
    dy, dx, part, parts = piece
    block = block_at(me_ref, dy, dx, n_seq)
    return pl.multiple_of(block * rows + part * (rows // parts), rows // parts)


def owners(width, per):
    lane = lax.broadcasted_iota(jnp.int32, (HEAD, width), 1)
    row = lax.broadcasted_iota(jnp.int32, (HEAD, width), 0)
    shard = width * per // HEAD
    owner, place = lane // shard, lane % shard
    return jnp.where((place < per) & (owner * per + place == row), 1.0, 0.0).astype(BF16)


def forward_kernel(
    me_ref, *refs, pieces, heads, block, n_seq, per,
):
    x_refs, refs = refs[:pieces], refs[pieces:]
    w_ref, freq_ref = refs[:2]
    (
        x_ref, normed_ref, raw_ref, qt_ref, kt_ref, vt_ref, att_ref, parts_ref, lse_ref, pos_ref,
        rows_ref, gains_ref, k_rows, segs_ref,
    ) = refs[2:]
    local = x_refs[0].shape[0]
    width = w_ref.shape[0]
    at = (heads + 2) * HEAD
    slab = w_ref[:, at // 128 * 128 :]
    rows = slab.astype(F32).T
    at = at % 128
    rows_ref[...] = rows[at : at + 8]
    gain = rows[at : at + 1]
    gains_ref[...] = dot(owners(width, per), slab, 1, 0)
    qg, kg = gains_ref[:, at + 2 : at + 3], gains_ref[:, at + 3 : at + 4]
    length = n_seq * local
    q_own = heads * HEAD
    for piece, ref in zip(PIECES, x_refs):
        at = first_row(me_ref, piece, n_seq, local)
        here = pl.ds(at, ref.shape[0])
        x = ref[:, :width]
        x_ref[here, :] = x
        x = x.astype(F32)
        inverse = lax.rsqrt(jnp.mean(x * x, axis=1, keepdims=True) + EPS)
        normed_ref[here, :] = (x * inverse * gain).astype(BF16)
        if piece[2] == 0:
            segs_ref[0:1, pl.ds(pl.multiple_of(at, 128), local)] = ref[
                0:1, width : width + local
            ].astype(F32)
    segs = segs_ref[0:1, :]
    index = lax.broadcasted_iota(jnp.int32, (1, length), 1).astype(F32)
    first = jnp.sum(jnp.where(segs == 0.0, 1.0, 0.0), axis=1, keepdims=True)
    middle = jnp.sum(jnp.where(segs == 1.0, 1.0, 0.0), axis=1, keepdims=True)
    start = jnp.where(segs >= 1.0, first, 0.0) + jnp.where(segs >= 2.0, middle, 0.0)
    position = index - start
    pos_ref[0:1, :] = position
    cosine, sine = angles_of(freq_ref, position)
    raw = dot(normed_ref[...], w_ref[...], 1, 0).T
    raw_ref[...] = raw[: q_own + HEAD]
    for h in range(heads + 1):
        values = raw[h * HEAD : (h + 1) * HEAD]
        inverse = lax.rsqrt(jnp.mean(values * values, axis=0, keepdims=True) + EPS)
        values = values * inverse * (qg if h < heads else kg)
        a, b = values[: HEAD // 2], values[HEAD // 2 :]
        turned = jnp.concatenate([a * cosine - b * sine, b * cosine + a * sine], axis=0)
        if h < heads:
            qt_ref[h * HEAD : (h + 1) * HEAD, :] = turned.astype(BF16)
        else:
            kt_ref[...] = turned.astype(BF16)
            k_rows[...] = turned.T.astype(BF16)
    vt_ref[...] = raw[q_own + HEAD : q_own + 2 * HEAD].astype(BF16)
    part = local // HALVES
    for c in range(length // block):
        stop = (c + 1) * block
        lanes = slice(c * block, stop)
        q = jnp.concatenate(
            [qt_ref[h * HEAD : (h + 1) * HEAD, lanes] for h in range(heads)], axis=1
        )
        scores = dot(k_rows[:stop, :], q, 1, 0) * HEAD**-0.5
        allowed = mask_of(stop, start[:, lanes], index[:, lanes], heads)
        scores = jnp.where(allowed, scores, -1e30)
        peak = jnp.max(scores, axis=0, keepdims=True)
        exps = jnp.exp(scores - peak)
        total = jnp.sum(exps, axis=0, keepdims=True)
        probs = (exps * (1.0 / total)).astype(BF16)
        mixed = dot(vt_ref[:, :stop], probs, 1, 0).astype(BF16)
        lse = peak + jnp.log(total)
        for h in range(heads):
            own = mixed[:, h * block : (h + 1) * block]
            rows = slice(h * HEAD, (h + 1) * HEAD)
            att_ref[rows, lanes] = own
            lse_ref[h : h + 1, lanes] = lse[:, h * block : (h + 1) * block]
            for k in range(HALVES):
                cut = [
                    own[:, t * local + k * part : t * local + (k + 1) * part]
                    for t in range(block // local)
                ]
                at = c * (block // HALVES)
                parts_ref[k, rows, at : at + block // HALVES] = jnp.concatenate(cut, axis=1)


def smem():
    return pl.BlockSpec(memory_space=pltpu.SMEM)


def vmem(count):
    return [pl.BlockSpec(memory_space=pltpu.VMEM)] * count


def attend_forward(me, x_pieces, w_own, freq, heads, n_seq, per, block=256):
    local = x_pieces[0].shape[0]
    width = w_own.shape[0]
    length = n_seq * local
    q_own = heads * HEAD
    return pl.pallas_call(
        functools.partial(
            forward_kernel,
            pieces=len(x_pieces),
            heads=heads,
            block=block,
            n_seq=n_seq,
            per=per,
        ),
        in_specs=[smem()] + vmem(len(x_pieces) + 2),
        out_shape=(
            shape(length, width),
            shape(length, width),
            shape(q_own + HEAD, length, dtype=F32),
            shape(q_own, length),
            shape(HEAD, length),
            shape(HEAD, length),
            shape(q_own, length),
            shape(HALVES, q_own, length // HALVES),
            shape(8, length, dtype=F32),
            shape(8, length, dtype=F32),
            shape(8, width, dtype=F32),
            shape(HEAD, 128, dtype=F32),
        ),
        scratch_shapes=[pltpu.VMEM((length, HEAD), BF16), pltpu.VMEM((8, length), F32)],
        compiler_params=pltpu.CompilerParams(vmem_limit_bytes=VMEM),
        cost_estimate=cost(0.1),
        name="attend_forward",
    )(me, *x_pieces, w_own, freq)


def backward_kernel(
    me_ref, qt_ref, kt_ref, vt_ref, raw_ref, lse_ref, pos_ref, g_ref, gains_ref, freq_ref, w_ref,
    gt_ref, back0_ref, back1_ref, back2_ref, back3_ref, gain_ref,
    k_rows, v_rows, q_rows, g_rows, dk, dv, dq, *, heads, block,
):
    length = kt_ref.shape[1]
    blocks, _, local = g_ref.shape
    q_own = heads * HEAD
    at = (heads + 2) * HEAD % 128 + 2
    qg, kg = gains_ref[:, at : at + 1], gains_ref[:, at + 1 : at + 2]
    position = pos_ref[0:1, :]
    index = lax.broadcasted_iota(jnp.int32, (1, length), 1).astype(F32)
    start = index - position
    cosine, sine = angles_of(freq_ref, position)
    k_rows[...] = kt_ref[...].astype(F32).T.astype(BF16)
    v_rows[...] = vt_ref[...].astype(F32).T.astype(BF16)
    dk[...] = jnp.zeros_like(dk)
    dv[...] = jnp.zeros_like(dv)
    scale = HEAD**-0.5
    per = block // local
    for c in range(length // block):
        stop = (c + 1) * block
        lanes = slice(c * block, stop)
        q = jnp.concatenate(
            [qt_ref[h * HEAD : (h + 1) * HEAD, lanes] for h in range(heads)], axis=1
        )
        g = jnp.concatenate(
            [
                g_ref[c * per + t, h * HEAD : (h + 1) * HEAD, :]
                for h in range(heads)
                for t in range(per)
            ],
            axis=1,
        )
        lse = jnp.concatenate([lse_ref[h : h + 1, lanes] for h in range(heads)], axis=1)
        q_rows[...] = q.astype(F32).T.astype(BF16)
        g_rows[...] = g.astype(F32).T.astype(BF16)
        scores = dot(k_rows[:stop, :], q, 1, 0) * scale
        allowed = mask_of(stop, start[:, lanes], index[:, lanes], heads)
        probs = jnp.where(allowed, jnp.exp(scores - lse), 0.0)
        grad_probs = dot(v_rows[:stop, :], g, 1, 0)
        inner = jnp.sum(probs * grad_probs, axis=0, keepdims=True)
        grad_scores = (probs * (grad_probs - inner)).astype(BF16)
        dv[:stop, :] += dot(probs.astype(BF16), g_rows[...], 1, 0)
        dk[:stop, :] += dot(grad_scores, q_rows[...], 1, 0)
        part = dot(kt_ref[:, :stop], grad_scores, 1, 0) * scale
        for h in range(heads):
            dq[h * HEAD : (h + 1) * HEAD, lanes] = part[:, h * block : (h + 1) * block]

    def back(grad, raw, gain):
        grad = grad.astype(BF16).astype(F32)
        a, b = grad[: HEAD // 2], grad[HEAD // 2 :]
        grad = jnp.concatenate([a * cosine + b * sine, b * cosine - a * sine], axis=0)
        inverse = lax.rsqrt(jnp.mean(raw * raw, axis=0, keepdims=True) + EPS)
        u = grad * gain
        pull = jnp.mean(u * raw, axis=0, keepdims=True)
        out = inverse * u - raw * (inverse * inverse * inverse) * pull
        return out.astype(BF16), jnp.sum(grad * raw * inverse, axis=1, keepdims=True)

    gain_q = jnp.zeros((HEAD, 1), F32)
    for h in range(heads):
        rows = slice(h * HEAD, (h + 1) * HEAD)
        gt_ref[rows, :], more = back(dq[rows, :], raw_ref[rows, :], qg)
        gain_q += more
    k_at = slice(q_own, q_own + HEAD)
    gt_ref[k_at, :], gain_k = back((dk[...] * scale).T, raw_ref[k_at, :], kg)
    gt_ref[q_own + HEAD : q_own + 2 * HEAD, :] = dv[...].T.astype(BF16)
    w = w_ref[:, : q_own + 2 * HEAD]
    for dy, ref in zip(STEPS, (back0_ref, back1_ref, back2_ref, back3_ref)):
        for dx in range(2):
            at = pl.multiple_of(block_at(me_ref, dy, dx, blocks) * local, local)
            ref[dx] = dot(gt_ref[:, pl.ds(at, local)], w, 0, 1).astype(BF16)
    lane = lax.broadcasted_iota(jnp.int32, (HEAD, 128), 1)
    gain_ref[...] = jnp.where(lane == 0, gain_q, jnp.where(lane == 1, gain_k, 0.0))


def attend_backward(me, qt, kt, vt, raw, lse, pos, grads, gains, freq, w_own, block=256):
    blocks, q_own, local = grads.shape
    length = blocks * local
    heads = q_own // HEAD
    rows = q_own + 2 * HEAD
    return pl.pallas_call(
        functools.partial(backward_kernel, heads=heads, block=block),
        out_shape=(
            shape(rows, length),
            *[shape(2, local, w_own.shape[0])] * 4,
            shape(HEAD, 128, dtype=F32),
        ),
        in_specs=[smem()] + vmem(10),
        scratch_shapes=[
            pltpu.VMEM((length, HEAD), BF16),
            pltpu.VMEM((length, HEAD), BF16),
            pltpu.VMEM((heads * block, HEAD), BF16),
            pltpu.VMEM((heads * block, HEAD), BF16),
            pltpu.VMEM((length, HEAD), F32),
            pltpu.VMEM((length, HEAD), F32),
            pltpu.VMEM((q_own, length), F32),
        ],
        compiler_params=pltpu.CompilerParams(vmem_limit_bytes=VMEM),
        cost_estimate=cost(0.1),
        name="attend_backward",
    )(me, qt, kt, vt, raw, lse, pos, grads, gains, freq, w_own)


def mlp_kernel(me_ref, *refs, pieces, width, pad, n_seq):
    att_refs, refs = refs[:pieces], refs[pieces:]
    x_ref, g_ref, gain_ref, w_ref = refs[:4]
    (
        mid_ref, second_ref, hid_ref, gate_grad_ref, up_grad_ref, back_ref, out_ref,
        w_out, w_gate, w_up, w_down, sems, att_all,
    ) = refs[4:]
    places = (
        (0, width, w_out),
        (width, pad, w_gate),
        (width + pad, pad, w_up),
        (width + 2 * pad, pad, w_down),
    )
    copies = [
        pltpu.make_async_copy(w_ref.at[:, at : at + n], to, sems.at[i])
        for i, (at, n, to) in enumerate(places)
    ]
    first = pl.program_id(0) == 0

    @pl.when(first)
    def _():
        for copy in copies:
            copy.start()

    def ready(i):
        @pl.when(first)
        def _():
            copies[i].wait()

    n, rows, _ = g_ref.shape
    count = n * rows
    x = x_ref[...].reshape(count, width).astype(F32)
    if pieces == 1:
        att = att_refs[0][...].reshape(width, count)
    else:
        part = width // n_seq
        for dy, ref in zip(STEPS, att_refs):
            for dx in range(2):
                at = pl.multiple_of(block_at(me_ref, dy, dx, n_seq) * part, part)
                att_all[pl.ds(at, part), :] = ref[dx]
        att = att_all[...]
    ready(0)
    middle = x + dot(att, w_out[...], 0, 1)
    mid_ref[...] = middle.reshape(n, rows, width)
    inverse = lax.rsqrt(jnp.mean(middle * middle, axis=1, keepdims=True) + EPS)
    second = (middle * inverse * gain_ref[1:2, :]).astype(BF16)
    second_ref[...] = second
    ready(1)
    gate = dot(second, w_gate[...], 1, 0)
    ready(2)
    up = dot(second, w_up[...], 1, 0)
    sig = lax.logistic(gate)
    act = gate * sig
    hidden = (act * up).astype(BF16)
    hid_ref[...] = hidden
    ready(3)
    grad_hidden = dot(g_ref[...].reshape(count, width), w_down[...], 1, 0)
    gate_grad = (grad_hidden * up * sig * (1.0 + gate * (1.0 - sig))).astype(BF16)
    up_grad = (grad_hidden * act).astype(BF16)
    gate_grad_ref[...] = gate_grad
    up_grad_ref[...] = up_grad
    back = dot(gate_grad, w_gate[...], 1, 1) + dot(up_grad, w_up[...], 1, 1)
    back_ref[...] = back.astype(BF16).reshape(n, rows, width)
    out_ref[...] = dot(hidden, w_down[...], 1, 1).astype(BF16).reshape(n, rows, width)


def mlp(me, att, x_all, g_all, gain, weights, half, per=4):
    count = att[0].shape[-1]
    n_seq, local, width = x_all.shape
    rows = local // HALVES
    pad = (weights.shape[1] - width) // 3
    step = per * rows
    spec = pl.BlockSpec
    flat = spec((step, pad), lambda i: (i, 0))
    stack = spec((per, rows, width), lambda i: (i, 0, 0))
    return pl.pallas_call(
        functools.partial(mlp_kernel, pieces=len(att), width=width, pad=pad, n_seq=n_seq),
        grid=(n_seq // per,),
        in_specs=[smem()]
        + [
            spec(a.shape[:-1] + (step,), lambda i, lead=(0,) * (a.ndim - 1): lead + (i,))
            for a in att
        ]
        + [
            spec((per, rows, width), lambda i: (i, half, 0)),
            spec((per, rows, width), lambda i: (i, half, 0)),
            spec((8, width), lambda i: (0, 0)),
            spec(memory_space=pl.ANY),
        ],
        out_specs=[
            stack,
            spec((step, width), lambda i: (i, 0)),
            flat,
            flat,
            flat,
            stack,
            stack,
        ],
        out_shape=(
            shape(n_seq, rows, width, dtype=F32),
            shape(count, width),
            shape(count, pad),
            shape(count, pad),
            shape(count, pad),
            shape(n_seq, rows, width),
            shape(n_seq, rows, width),
        ),
        scratch_shapes=[
            pltpu.VMEM((width, width), BF16),
            pltpu.VMEM((width, pad), BF16),
            pltpu.VMEM((width, pad), BF16),
            pltpu.VMEM((width, pad), BF16),
            pltpu.SemaphoreType.DMA((4,)),
            pltpu.VMEM((width, step), BF16),
        ],
        compiler_params=pltpu.CompilerParams(vmem_limit_bytes=VMEM),
        cost_estimate=cost(1),
        name="mlp_part",
    )(me, *att, x_all, g_all, gain, weights)


def mlp_grads_kernel(core_ref, *refs, shard):
    seconds, cotangents = refs[:HALVES], refs[HALVES : 2 * HALVES]
    rest, own_ref, other_ref = refs[2 * HALVES : -2], refs[-2], refs[-1]
    pad = rest[0].shape[1]
    core = core_ref[0]
    for k in range(3):
        total = None
        for h in range(HALVES):
            left = (seconds if k < 2 else cotangents)[h][...]
            left = left.reshape(-1, left.shape[-1])
            term = dot(left, rest[k * HALVES + h][...], 0, 0)
            total = term if total is None else total + term
        total = total.astype(BF16)
        lanes = slice(k * pad, (k + 1) * pad)
        for i in range(total.shape[0] // shard):
            part = total[i * shard : (i + 1) * shard]

            @pl.when(core == i % 2)
            def _(part=part, i=i, lanes=lanes):
                own_ref[i // 2, :, lanes] = part

            @pl.when(core != i % 2)
            def _(part=part, i=i, lanes=lanes):
                other_ref[i // 2, :, lanes] = part


def mlp_grads(core, seconds, g_all, gates, ups, hiddens, shard, tile=384):
    count, width = seconds[0].shape
    pad = gates[0].shape[1]
    n_seq, local, _ = g_all.shape
    rows = local // HALVES
    spec = pl.BlockSpec
    return pl.pallas_call(
        functools.partial(mlp_grads_kernel, shard=shard),
        grid=(width // tile,),
        in_specs=[smem()]
        + [spec((count, tile), lambda r: (0, r))] * HALVES
        + [spec((n_seq, rows, tile), lambda r, h=h: (0, h, r)) for h in range(HALVES)]
        + [spec((count, pad), lambda r: (0, 0))] * (3 * HALVES),
        out_specs=[spec((tile // shard // 2, shard, 3 * pad), lambda r: (r, 0, 0))] * 2,
        out_shape=(shape(width // shard // 2, shard, 3 * pad),) * 2,
        compiler_params=pltpu.CompilerParams(vmem_limit_bytes=VMEM),
        cost_estimate=cost(0.1),
        name="mlp_grads",
    )(core, *seconds, *([g_all] * HALVES), *gates, *ups, *hiddens)


def middle_kernel(
    me_ref, back0_ref, back1_ref, mid0_ref, mid1_ref, g_ref, gain_ref, w_ref,
    branch_ref, grad_ref, att_ref, gain_grad_ref, mid_out_ref,
    mid, w, sems, *, width,
):
    half = back0_ref.shape[1]
    me = me_ref[0]
    copies = [
        pltpu.make_async_copy(mid0_ref.at[me], mid.at[pl.ds(0, half)], sems.at[0]),
        pltpu.make_async_copy(mid1_ref.at[me], mid.at[pl.ds(half, half)], sems.at[1]),
        pltpu.make_async_copy(w_ref.at[:, :width], w, sems.at[2]),
    ]
    for copy in copies:
        copy.start()
    grad = jnp.concatenate(
        [jnp.sum(ref[...].astype(F32), axis=0) for ref in (back0_ref, back1_ref)], axis=0
    )
    copies[0].wait()
    copies[1].wait()
    middle = mid[...]
    mid_out_ref[...] = middle
    inverse = lax.rsqrt(jnp.mean(middle * middle, axis=1, keepdims=True) + EPS)
    u = grad * gain_ref[1:2, :]
    pull = jnp.mean(u * middle, axis=1, keepdims=True)
    grad_middle = (
        g_ref[...].astype(F32) + inverse * u - middle * (inverse * inverse * inverse) * pull
    )
    gain_grad_ref[...] = jnp.sum(grad * middle * inverse, axis=0, keepdims=True)
    grad_ref[...] = grad_middle
    branch = grad_middle.astype(BF16)
    branch_ref[...] = branch
    copies[2].wait()
    att_ref[...] = dot(branch, w[...], 1, 0).T.astype(BF16)


def middle_back(me, backs, mids, g_own, gain, weights):
    local, width = g_own.shape
    anywhere = pl.BlockSpec(memory_space=pl.ANY)
    return pl.pallas_call(
        functools.partial(middle_kernel, width=width),
        in_specs=[smem()] + vmem(2) + [anywhere] * 2 + vmem(2) + [anywhere],
        out_shape=(
            shape(local, width),
            shape(local, width, dtype=F32),
            shape(width, local),
            shape(1, width, dtype=F32),
            shape(local, width, dtype=F32),
        ),
        scratch_shapes=[
            pltpu.VMEM((local, width), F32),
            pltpu.VMEM((width, width), BF16),
            pltpu.SemaphoreType.DMA((3,)),
        ],
        compiler_params=pltpu.CompilerParams(vmem_limit_bytes=VMEM),
        cost_estimate=cost(0.1),
        name="middle_back",
    )(me, *backs, *mids, g_own, gain, weights)


def qkv_grads_kernel(gt_ref, normed_ref, gains_ref, mlp_gain_ref, out_ref, *, per):
    qkv = dot(gt_ref[...], normed_ref[...], 1, 0)
    width = normed_ref.shape[1]
    gains = dot(gains_ref[:, :HEAD].astype(BF16), owners(width, per), 0, 0)
    row = lax.broadcasted_iota(jnp.int32, gains.shape, 0)
    gains = jnp.where(row == 2, mlp_gain_ref[...], gains)
    out_ref[...] = jnp.concatenate([qkv, gains], axis=0).T.astype(BF16)


def qkv_grads(gt, normed, gains, mlp_gain, per):
    count, width = normed.shape
    return pl.pallas_call(
        functools.partial(qkv_grads_kernel, per=per),
        out_shape=shape(width, gt.shape[0] + HEAD),
        compiler_params=pltpu.CompilerParams(vmem_limit_bytes=VMEM),
        cost_estimate=cost(0.1),
        name="qkv_grads",
    )(gt, normed, gains, mlp_gain)


def out_grads_kernel(me_ref, att_ref, *refs, n_seq):
    branch_refs, out_ref, whole = refs[:-2], refs[-2], refs[-1]
    local = branch_refs[0].shape[1]
    for dy, ref in zip(STEPS, branch_refs):
        for dx in range(2):
            at = pl.multiple_of(block_at(me_ref, dy, dx, n_seq) * local, local)
            whole[pl.ds(at, local), :] = ref[dx]
    out_ref[...] = dot(att_ref[...], whole[...], 1, 0).T.astype(BF16)


def out_grads(me, att, branch, n_seq):
    q_own, length = att.shape
    width = branch[0].shape[2]
    return pl.pallas_call(
        functools.partial(out_grads_kernel, n_seq=n_seq),
        in_specs=[smem()] + vmem(1 + len(branch)),
        out_shape=shape(width, q_own),
        scratch_shapes=[pltpu.VMEM((length, width), BF16)],
        compiler_params=pltpu.CompilerParams(vmem_limit_bytes=VMEM),
        cost_estimate=cost(1),
        name="out_grads",
    )(me, att, *branch)


def shards_kernel(
    in_ref, wq_ref, wk_ref, wv_ref, gain_ref,
    gq_ref, gk_ref, gv_ref, go_ref, gains_ref, *, q_own, kv_own,
):
    n = in_ref.shape[0]

    def side(start, stop):
        return jnp.concatenate([in_ref[j][:, start:stop] for j in range(n)], axis=1).astype(F32)

    k_at, v_at, end = q_own, q_own + kv_own, q_own + 2 * kv_own
    gq, gk, gv = side(0, k_at), side(k_at, v_at), side(v_at, end)
    gq_ref[...], gk_ref[...], gv_ref[...] = gq, gk, gv
    go_ref[...] = side(end + HEAD, end + HEAD + q_own)
    attn = sum(
        jnp.sum(w[...].astype(F32) * g, axis=1, keepdims=True)
        for w, g in ((wq_ref, gq), (wk_ref, gk), (wv_ref, gv))
    ) / gain_ref[...].astype(F32)
    sums = jnp.sum(in_ref[:, :, 256:384].astype(F32), axis=0)
    lane = lax.broadcasted_iota(jnp.int32, sums.shape, 1)
    gains_ref[...] = jnp.where(lane == 0, attn, sums)


def own_shards(parts, w_query, w_key, w_value, attn_gain, q_own, kv_own):
    shard, q_all = w_query.shape
    return pl.pallas_call(
        functools.partial(shards_kernel, q_own=q_own, kv_own=kv_own),
        out_shape=(
            shape(shard, q_all, dtype=F32),
            shape(shard, w_key.shape[1], dtype=F32),
            shape(shard, w_value.shape[1], dtype=F32),
            shape(shard, q_all, dtype=F32),
            shape(shard, 128, dtype=F32),
        ),
        compiler_params=pltpu.CompilerParams(vmem_limit_bytes=VMEM),
        cost_estimate=cost(200),
        name="own_shards",
    )(parts, w_query, w_key, w_value, attn_gain)


def mlp_shards_kernel(x_ref, grads_ref, got_ref, gate_ref, up_ref, down_ref):
    width = gate_ref.shape[1]
    total = grads_ref[x_ref[0]].astype(F32) + got_ref[...].astype(F32)
    for k, ref in enumerate((gate_ref, up_ref, down_ref)):
        ref[...] = total[:, k * PAD : k * PAD + width]


def mlp_shards(x_hi, grads, got, width):
    return pl.pallas_call(
        mlp_shards_kernel,
        in_specs=[smem()] + vmem(2),
        out_shape=(shape(got.shape[0], width, dtype=F32),) * 3,
        compiler_params=pltpu.CompilerParams(vmem_limit_bytes=VMEM),
        cost_estimate=cost(1),
        name="mlp_shards",
    )(x_hi, grads, got)


def shift(size, by):
    return [(i, (i + by) % size) for i in range(size)]


def to_all(block):
    n = lax.axis_size("seq")
    return lax.all_to_all(jnp.broadcast_to(block[None], (n,) + block.shape), "seq", 0, 0, tiled=True)


def exchange(blocks):
    return lax.all_to_all(blocks, "seq", 0, 0, tiled=True)


def total_of(blocks):
    return jnp.sum(blocks.astype(F32), axis=0)


def step_seq(block, dy, dx=0):
    n = lax.axis_size("seq")
    to = [(i, (i + 2 * dy) % n ^ dx) for i in range(n)]
    return lax.ppermute(block, "seq", to)


def gather_pieces(block):
    half = block.shape[0] // 2
    up, down = step_seq(block, 1), step_seq(block, -1)
    beside = step_seq(block, 0, 1)
    beside_up, beside_down = step_seq(beside, 1), step_seq(beside, -1)
    return (
        block,
        beside,
        up,
        down,
        beside_up,
        beside_down,
        step_seq(up[:half], 1),
        step_seq(down[half:], -1),
        step_seq(beside_up[:half], 1),
        step_seq(beside_down[half:], -1),
    )


def along_y(pair):
    return (pair,) + tuple(step_seq(pair, -dy) for dy in STEPS[1:])


def send_along(parts):
    return (parts[0],) + tuple(step_seq(part, dy) for dy, part in zip(STEPS[1:], parts[1:]))


def sum_pairs(pairs):
    total = sum(pair.astype(F32) for pair in pairs)
    return total[0] + step_seq(total[1].astype(pairs[0].dtype), 0, 1).astype(F32)


def pairs_for(blocks):
    n = lax.axis_size("seq")
    me = lax.axis_index("seq")
    y, x = me // 2, me % 2
    grid = blocks.reshape((n // 2, 2) + blocks.shape[1:])
    grid = jnp.where(x == 0, grid, grid[:, ::-1])
    pick = functools.partial(lax.dynamic_index_in_dim, grid, axis=0, keepdims=False)
    return [pick((y + dy) % (n // 2)) for dy in STEPS]


def in_order_kernel(me_ref, *refs, n_seq):
    out_ref = refs[-1]
    for dy, ref in zip(STEPS, refs[:-1]):
        for dx in range(2):
            out_ref[block_at(me_ref, dy, dx, n_seq)] = ref[dx]


def in_order(me, pairs, n_seq):
    return pl.pallas_call(
        functools.partial(in_order_kernel, n_seq=n_seq),
        in_specs=[smem()] + vmem(len(pairs)),
        out_shape=shape(n_seq, *pairs[0].shape[1:]),
        compiler_params=pltpu.CompilerParams(vmem_limit_bytes=VMEM),
        cost_estimate=cost(0.1),
        name="in_order",
    )(me, *pairs)


def swap(held, bit):
    n = lax.axis_size("fsdp")
    return lax.ppermute(held, "fsdp", [(i, i ^ bit) for i in range(n)])


def scatter_sum_fsdp(blocks):
    n = lax.axis_size("fsdp")
    me = lax.axis_index("fsdp")
    core, x_hi, z = me % 2, me // 2 % 2, me // 4
    rest = blocks.shape[1:]
    grid = blocks.reshape((n // 2, 2) + rest)
    pick = lax.dynamic_index_in_dim
    got = swap(pick(grid, 1 - core, 1, keepdims=False), 1)
    held = (pick(grid, core, 1, keepdims=False).astype(F32) + got.astype(F32)).astype(blocks.dtype)
    grid = held.reshape((n // 4, 2) + rest)
    got = [
        lax.ppermute(pick(grid, (z + by) % (n // 4), 0, keepdims=False), "fsdp", shift(n, 4 * by))
        for by in range(1, n // 4)
    ]
    held = pick(grid, z, 0, keepdims=False).astype(F32)
    for block in got:
        held = held + block.astype(F32)
    held = held.astype(blocks.dtype)
    got = swap(pick(held, 1 - x_hi, 0, keepdims=False), 2)
    return pick(held, x_hi, 0, keepdims=False).astype(F32) + got.astype(F32)


def pair(mine, other, low):
    return jnp.concatenate([jnp.where(low, mine, other), jnp.where(low, other, mine)], axis=0)


def gather_fsdp(block, first, second):
    n = lax.axis_size("fsdp")
    me = lax.axis_index("fsdp")
    held = block[None]
    held = pair(held, swap(held, 2), me // 2 % 2 == 0)
    held, _ = lax.optimization_barrier((held, first))
    other = swap(held, 1)
    low = me % 2 == 0
    held = jnp.stack([jnp.where(low, held, other), jnp.where(low, other, held)], axis=1)
    held = held.reshape((1, 4) + block.shape)
    held, _ = lax.optimization_barrier((held, second))
    whole = jnp.zeros((n // 4,) + held.shape[1:], block.dtype)
    z = me // 4
    whole = lax.dynamic_update_slice_in_dim(whole, held, z, 0)
    for by in range(1, n // 4):
        got = lax.ppermute(held, "fsdp", shift(n, 4 * by))
        whole = lax.dynamic_update_slice_in_dim(whole, got, (z - by) % (n // 4), 0)
    return whole.reshape((n * block.shape[0],) + block.shape[1:])


def lanes(array, width):
    return jnp.pad(array, ((0, 0), (0, width - array.shape[1])))


def rows(vector, count):
    return jnp.pad(vector, (0, count - vector.shape[0]))


def on_device(
    tokens,
    segments,
    out_grad,
    attn_gain,
    w_query,
    w_key,
    w_value,
    query_gain,
    key_gain,
    w_out,
    mlp_gain,
    w_gate,
    w_up,
    w_down,
):
    n_seq = lax.axis_size("seq")
    n_fsdp = lax.axis_size("fsdp")
    me = lax.axis_index("seq")
    here = me.astype(jnp.int32).reshape(1)
    core = (lax.axis_index("fsdp") % 2).astype(jnp.int32).reshape(1)
    x_hi = (lax.axis_index("fsdp") // 2 % 2).astype(jnp.int32).reshape(1)
    local, width = tokens.shape[1:]
    shard = attn_gain.shape[0]
    q_all, kv_all = w_query.shape[1], w_key.shape[1]
    q_own, kv_own = q_all // n_seq, kv_all // n_seq
    heads = q_own // HEAD
    qkv_own = q_own + 2 * kv_own
    hidden_own = w_gate.shape[1]
    gain_own = query_gain.shape[0]

    x = tokens[0]
    numbers = lax.pad(
        segments.astype(BF16), jnp.zeros((), BF16), ((0, local - 1, 0), (0, 128 - local, 0))
    )
    x_pieces = gather_pieces(jnp.concatenate([x, numbers], axis=1))

    mlp_pack = jnp.concatenate(
        [w_out.T, lanes(w_gate, PAD), lanes(w_up, PAD), lanes(w_down.T, PAD)], axis=1
    )
    mlp_full = lax.all_gather(mlp_pack, "fsdp", axis=0, tiled=True)

    mlp_pack = jnp.concatenate(
        [w_out.T, lanes(w_gate, PAD), lanes(w_up, PAD), lanes(w_down.T, PAD)], axis=1
    )
    mlp_full = lax.all_gather(mlp_pack, "fsdp", axis=0, tiled=True)

    own = lax.dynamic_slice_in_dim
    head_pack = jnp.concatenate(
        [
            own(w_query, me * q_own, q_own, 1),
            own(w_key, me * kv_own, kv_own, 1),
            own(w_value, me * kv_own, kv_own, 1),
            attn_gain[:, None],
            mlp_gain[:, None],
            rows(query_gain, shard)[:, None],
            rows(key_gain, shard)[:, None],
        ],
        axis=1,
    )
    head_full = gather_fsdp(lanes(head_pack, 384), x_pieces[1], x_pieces[2:4])

    freq = (ROPE_BASE ** (-2.0 * jnp.arange(HEAD // 2, dtype=F32) / HEAD)).reshape(-1, 1)

    after = lax.optimization_barrier
    g_pair = jnp.stack([out_grad[0], step_seq(out_grad[0], 0, 1)])
    g_pair, x_pieces = after((g_pair, x_pieces))
    g_pairs = along_y(g_pair)

    x_all, normed, raw, qt, kt, vt, att, att_parts, lse, pos, gain_rows, gains = attend_forward(
        here, x_pieces, head_full, freq, heads, n_seq, gain_own
    )
    x_all = x_all.reshape(n_seq, local, width)
    att_beside = step_seq(att_parts, 0, 1)
    att_pair, g_pairs = after((jnp.stack([att_parts[0], att_beside[0]]), g_pairs))
    att_first = along_y(att_pair)
    att_sent, att_first = after((att_parts[1], att_first))
    att_second = (to_all(att_sent),)
    g_all = in_order(here, g_pairs, n_seq)
    done = [mlp(here, att_first, x_all, g_all, gain_rows, mlp_full, 0)]
    back_first = exchange(done[0][5])
    att_second, done[0] = after((att_second, done[0]))
    done.append(mlp(here, att_second, x_all, g_all, gain_rows, mlp_full, 1))
    middle_parts, seconds, hiddens, gate_grads, up_grads, back_parts, out_parts = zip(*done)
    back_sent, back_first = after((back_parts[1], back_first))
    backs = (back_first, exchange(back_sent))
    mine, other = mlp_grads(core, seconds, g_all, gate_grads, up_grads, hiddens, shard)
    mine, other, backs = after((mine, other, backs))
    got = swap(other, 1)
    out_sent = pairs_for(jnp.concatenate(out_parts, axis=1))
    out_near = [step_seq(pair, dy) for pair, dy in zip(out_sent[1:3], STEPS[1:3])]
    backs, out_near = after((backs, out_near))

    branch, grad_middle, grad_att, grad_mlp_g, middle = middle_back(
        here, backs, middle_parts, out_grad[0], gain_rows, mlp_full
    )
    mine, got, branch = after((mine, got, branch))
    chip_sums = (mine.astype(F32) + got.astype(F32)).astype(BF16)
    mlp_sums = lax.psum_scatter(
        chip_sums.reshape(n_fsdp // 4, 2, shard, -1),
        "fsdp",
        scatter_dimension=0,
        tiled=True,
        axis_index_groups=[list(range(i, n_fsdp, 4)) for i in range(4)],
    ).reshape(2, shard, -1)
    grad_heads = exchange(grad_att.reshape(n_seq, q_own, local))
    branch_pair = jnp.stack([branch, step_seq(branch, 0, 1)])
    branch_pair, grad_heads, _ = after((branch_pair, grad_heads, chip_sums))
    branch_pairs = along_y(branch_pair)

    gt, *back, gain_grads = attend_backward(
        here, qt, kt, vt, raw, lse, pos, grad_heads, gains, freq, head_full
    )
    back, branch_pairs = after((back, branch_pairs))
    back_pairs = send_along(back)
    grad_normed = sum_pairs(back_pairs)
    out_far, back_pairs = after((out_sent[3], back_pairs))
    out_pairs = [out_sent[0], *out_near, step_seq(out_far, STEPS[3])]
    layer_out = (middle + sum_pairs(out_pairs)).astype(BF16)
    xf = x.astype(F32)
    inverse_x = lax.rsqrt(jnp.mean(xf * xf, axis=-1, keepdims=True) + EPS)
    ux = grad_normed * gain_rows[:1]
    grad_tokens = (
        grad_middle
        + inverse_x * ux
        - xf * inverse_x**3 * jnp.mean(ux * xf, axis=-1, keepdims=True)
    )

    own_grads = jnp.concatenate(
        [
            qkv_grads(gt, normed, gain_grads, grad_mlp_g, gain_own),
            out_grads(here, att, branch_pairs, n_seq),
        ],
        axis=1,
    )
    att_owned = scatter_sum_fsdp(own_grads.reshape(n_fsdp, shard, -1)).astype(BF16)
    att_owned, grad_normed = after((att_owned, grad_normed))
    gw_query, gw_key, gw_value, gw_out, gain_sums = own_shards(
        to_all(att_owned), w_query, w_key, w_value, attn_gain[:, None], q_own, kv_own
    )
    far = lax.dynamic_index_in_dim(mlp_sums, 1 - x_hi[0], 0, keepdims=False)
    gw_gate, gw_up, gw_down = mlp_shards(x_hi, mlp_sums, swap(far, 2), hidden_own)
    at = qkv_own - 256
    return (
        layer_out[None],
        grad_tokens[None],
        gain_sums[:, 0],
        gw_query,
        gw_key,
        gw_value,
        gain_sums[:gain_own, at],
        gain_sums[:gain_own, at + 1],
        gw_out.T,
        gain_sums[:, at + 2],
        gw_gate,
        gw_up,
        gw_down.T,
    )


def solution(mesh):
    in_specs = (
        P("fsdp", "seq", None),
        P("fsdp", "seq"),
        P("fsdp", "seq", None),
        P("fsdp"),
        P("fsdp", None),
        P("fsdp", None),
        P("fsdp", None),
        P("fsdp"),
        P("fsdp"),
        P(None, "fsdp"),
        P("fsdp"),
        P("fsdp", "seq"),
        P("fsdp", "seq"),
        P("seq", "fsdp"),
    )
    out_specs = (
        P("fsdp", "seq", None),
        P("fsdp", "seq", None),
        P("fsdp"),
        P("fsdp", None),
        P("fsdp", None),
        P("fsdp", None),
        P("fsdp"),
        P("fsdp"),
        P(None, "fsdp"),
        P("fsdp"),
        P("fsdp", "seq"),
        P("fsdp", "seq"),
        P("seq", "fsdp"),
    )
    return jax.shard_map(
        on_device, mesh=mesh, in_specs=in_specs, out_specs=out_specs, check_vma=False
    )
```

time: 614 us -> 397 us (0.65)
  Pallas kernels: 0 us -> 106 us
  matrix products: 102 us -> 0 us
  local copies, waits for them, and re-layouts: 91.9 us -> 21 us
  starting transfers between devices: 148 us -> 79.9 us
  blocking collectives: 44.9 us -> 0 us
  other arithmetic: 52.3 us -> 24.7 us
    pallas_call x0 -> x11, Pallas kernels: none -> 106 us  [the longest x2 40.1 us: mlp(): pl.pallas_call(functools.partial(mlp_kernel, pieces=len(att), width=width...]
    dot_general x21 -> x0, matrix products: 102 us -> none  [the longest x5 32.8 us: mm_nt(): lax.dot_general(a, b, (((1,), (1,)), ((), ())), preferred_element_type=F32)]
    ppermute x61 -> x41, starting transfers between devices: 138 us -> 58.6 us  [the longest x29 41.9 us: step_seq(): return lax.ppermute(block, 'seq', to)]
    all_to_all x1 -> x0, blocking collectives: 44.9 us -> none  [on_device(): lax.all_to_all(att_grads.reshape(n_fsdp, shard, 640), 'fsdp', split_axis=...]
    dynamic_update_slice x50 -> x4, local copies, waits for them, and re-layouts: 25 us -> 0.2 us  [the longest x3 0.15 us: gather_fsdp(): whole = lax.dynamic_update_slice_in_dim(whole, got, (z - by) % (n // 4), 0)]
    ppermute x61 -> x41, waiting for transfers between devices: 147 us -> 125 us  [the longest x29 110 us: step_seq(): return lax.ppermute(block, 'seq', to)]
    unnamed x152 -> x86, local copies, waits for them, and re-layouts: 26.6 us -> 5.78 us
    all_to_all x2 -> x5, waiting for transfers between devices: 0.01 us -> 13.9 us  [the longest x2 7.47 us: to_all(): lax.all_to_all(jnp.broadcast_to(block[None], (n,) + block.shape), 'seq',...]
  transfers between devices with their start and end apart: 66 -> 48, of which waited for: 27 -> 25; matrix products, arithmetic and copies ran while one was open for 39% -> 8% of each run, Pallas kernels for 0% -> 27%
where the time goes in v2:
time: 397 us; the launch traced here: 390 us
  waiting for transfers between devices  143 us (36%)
  Pallas kernels  106 us (27%)
  starting transfers between devices  79.9 us (20%)
  other arithmetic  24.7 us (6%)
  local copies, waits for them, and re-layouts  21 us (5%)
  between operations  15 us (4%)
    ppermute x29, waiting for transfers between devices, step_seq(): return lax.ppermute(block, 'seq', to)  110 us
    ppermute x29, starting transfers between devices, step_seq(): return lax.ppermute(block, 'seq', to)  41.9 us
    pallas_call x2, Pallas kernels, mlp(): pl.pallas_call(functools.partial(mlp_kernel, pieces=len(att), width=width...  40.1 us
    pallas_call x1, Pallas kernels, mlp_grads(): pl.pallas_call(functools.partial(mlp_grads_kernel, shard=shard), grid=(wi...  17.6 us
    pallas_call x1, Pallas kernels, attend_backward(): pl.pallas_call(functools.partial(backward_kernel, heads=heads, block=bloc...  13.3 us
    all_to_all x3, starting transfers between devices, exchange(): return lax.all_to_all(blocks, 'seq', 0, 0, tiled=True)  12.3 us
    pallas_call x1, Pallas kernels, attend_forward(): pl.pallas_call(functools.partial(forward_kernel, pieces=len(x_pieces), he...  11.3 us
    all_to_all x2, starting transfers between devices, to_all(): lax.all_to_all(jnp.broadcast_to(block[None], (n,) + block.shape), 'seq',...  8.92 us
  transfers between devices with their start and end apart: 48, of which 25 were waited for; matrix products, arithmetic and copies ran while one was open for 8% of the time, Pallas kernels for 27%

profile of v2, /device:TPU:0, one launch (start us, length us, event | category | flops | bytes accessed | tf_op | source)
XLA Modules:
  0.0 389.9 jit_solution(16489138635125416415)
XLA Ops:
  19.9 5.3 %collective-permute-done.10 = bf16[1,96,384]{2,1,0:T(8,128)(2,1)S(1)} collective-permute-done((bf16[1,96,384]{2,1,0:T(8,128)(2,1)S(1)}, bf16[1,96,384]{2,1,0:T(8,128)(2,1)S(1)}, u32[]{:S(2)}, u32[]{:S(2)}) %collective-permute-start.10) | collective-permute-done | bytes 73760 | tf_op jit(solution)/shard_map/ppermute | solution.py:725
  35.7 3.8 collective-permute-done.4.refs_4_
  41.5 3.9 collective-permute-start.13
  58.9 3.7 collective-permute-done.13
  63.8 11.3 %attend_forward.1 = (bf16[1024,1536]{1,0:T(8,128)(2,1)}, bf16[1024,1536]{1,0:T(8,128)(2,1)}, f32[256,1024]{1,0:T(8,128)}, bf16[192,1024]{1,0:T(8,128)(2,1)}, bf1...) custom-call(s32[1]{0:T(128)} %bitcast.me_ref, ...), custom_call_target="tpu_custom_call" | custom-call | flops 115000000 | bytes 1024 | tf_op jit(solution)/shard_map/attend_forward/pallas_call | solution.py:177
  77.8 17.0 %collective-permute-done.15 = bf16[2,192,512]{2,1,0:T(8,128)(2,1)S(1)} collective-permute-done((bf16[2,192,512]{2,1,0:T(8,128)(2,1)}, bf16[2,192,512]{2,1,0:T(8,128)(2,1)S(1)}, u32[]{:S(2)}, u32[]{:S(2)}) %collective-permute-start.15) | collective-permute-done | bytes 393248 | tf_op jit(solution)/shard_map/ppermute | solution.py:660
  99.4 7.7 %collective-permute-done.19.refs_1_ = bf16[2,192,512]{2,1,0:T(8,128)(2,1)S(1)} collective-permute-done((bf16[2,192,512]{2,1,0:T(8,128)(2,1)S(1)}, bf16[2,192,512]{2,1,0:T(8,128)(2,1)S(1)}, u32[]{:S(2)}, u32[]{:S(2)}) %collective-permute-start.19) | collective-permute-done | bytes 393248 | tf_op jit(solution)/shard_map/ppermute | solution.py:660
  107.2 5.2 %collective-permute-done.20.refs_2_ = bf16[2,192,512]{2,1,0:T(8,128)(2,1)S(1)} collective-permute-done((bf16[2,192,512]{2,1,0:T(8,128)(2,1)S(1)}, bf16[2,192,512]{2,1,0:T(8,128)(2,1)S(1)}, u32[]{:S(2)}, u32[]{:S(2)}) %collective-permute-start.20) | collective-permute-done | bytes 393248 | tf_op jit(solution)/shard_map/ppermute | solution.py:660
  115.9 5.0 %all-to-all-start = ((bf16[8,192,512]{2,1,0:T(8,128)(2,1)}), bf16[8,192,512]{2,1,0:T(8,128)(2,1)S(1)}, u32[]{:S(2)}, u32[]{:S(2)}) async-start(bf16[8,192,512]{2,1,0:T(8,128)(2,1)} %broadcast_in_dim.45), calls=%async_computation | async-start | bytes 3145728 | tf_op jit(solution)/shard_map/all_to_all | solution.py:646
  120.9 4.0 %in_order.1.refs_5_.refs_2_.refs_3_ = bf16[8,128,1536]{2,1,0:T(8,128)(2,1)} custom-call(s32[1]{0:T(128)} %bitcast.me_ref, bf16[2,128,1536]{2,1,0:T(8,128)(2,1)} %copy-done.11, bf16[2,128,1536]{2,1,0:T(8,128)(2,1)} %copy-done.24, bf16[2,128,1536]{2,1,0:T(8,128)(2,1)} %copy-done.25, bf16[2,128,1536]{2,1,0:T(8,128)(2,1)} %copy-done.26), custom_call_target="tpu_custom_call" | custom-call | flops 115000000 | bytes 1024 | tf_op jit(solution)/shard_map/in_order/pallas_call | solution.py:713
  124.9 4.5 %all-gather.2.cloned.1.call-done.refs_7_.refs_4_.w_ref = bf16[1536,4224]{1,0:T(8,128)(2,1)} async-done(((bf16[96,4224]{1,0:T(8,128)(2,1)}), bf16[1536,4224]{1,0:T(8,128)(2,1)}) %all-gather.2.cloned.1.call-update) | async-done | bytes 12976144 | tf_op jit(solution)/shard_map/all_gather | solution.py:827
  129.3 20.1 %mlp_part.2 = (f32[8,64,1536]{2,1,0:T(8,128)}, bf16[512,1536]{1,0:T(8,128)(2,1)}, bf16[512,896]{1,0:T(8,128)(2,1)}, bf16[512,896]{1,0:T(8,128)(2,1)}, bf16[512,8...) custom-call(s32[1]{0:T(128)} %bitcast.me_ref, bf16[2,192,512]{2,1,0:T(8,128)(2,1)} %copy-done.13, ...), custom_call_target="tpu_custom_call" | custom-call | flops 1150000000 | bytes 1024 | tf_op jit(solution)/shard_map/mlp_part/pallas_call | solution.py:387
  149.5 4.3 %all-to-all-start.1 = ((bf16[8,64,1536]{2,1,0:T(8,128)(2,1)}), bf16[8,64,1536]{2,1,0:T(8,128)(2,1)S(1)}, u32[]{:S(2)}, u32[]{:S(2)}) async-start(bf16[8,64,1536]{2,1,0:T(8,128)(2,1)} %get-tuple-element.146), calls=%async_computation.1 | async-start | bytes 3145728 | tf_op jit(solution)/shard_map/all_to_all | solution.py:650
  153.8 19.9 %mlp_part.3 = (f32[8,64,1536]{2,1,0:T(8,128)}, bf16[512,1536]{1,0:T(8,128)(2,1)}, bf16[512,896]{1,0:T(8,128)(2,1)}, bf16[512,896]{1,0:T(8,128)(2,1)}, bf16[512,8...) custom-call(s32[1]{0:T(128)} %bitcast.me_ref, bf16[8,192,512]{2,1,0:T(8,128)(2,1)} %copy-done.5, ...), custom_call_target="tpu_custom_call" | custom-call | flops 1150000000 | bytes 1024 | tf_op jit(solution)/shard_map/mlp_part/pallas_call | solution.py:387
  175.6 3.9 %all-to-all-start.2 = ((bf16[8,64,1536]{2,1,0:T(8,128)(2,1)}), bf16[8,64,1536]{2,1,0:T(8,128)(2,1)S(1)}, u32[]{:S(2)}, u32[]{:S(2)}) async-start(bf16[8,64,1536]{2,1,0:T(8,128)(2,1)} %get-tuple-element.161), calls=%async_computation.2 | async-start | bytes 3145728 | tf_op jit(solution)/shard_map/all_to_all | solution.py:650
  179.5 17.6 %mlp_grads.1 = (bf16[8,96,2688]{2,1,0:T(8,128)(2,1)}, bf16[8,96,2688]{2,1,0:T(8,128)(2,1)}) custom-call(s32[1]{0:T(128)} %bitcast.1.core_ref, bf16[512,1536]{1,0:T(8,128)(2,1)} %get-tuple-element.148.refs_0_, bf16[512,1536]{1,0:T(8,128)(2,1)} %get-tuple-element.150.refs_1_, bf16[8,128,1536]{2,1,0:T(8,128)(2,1)} %in_order.1.refs_5_.refs_2_.refs_3_, ...), custom_call_target="tpu_custom_call" | custom-call | flops 115000000 | bytes 1024 | tf_op jit(solution)/shard_map/mlp_grads/pallas_call | solution.py:465
  197.1 3.6 all-to-all-done.2.back1_ref
  207.2 17.4 %collective-permute-done.22 = bf16[2,128,1536]{2,1,0:T(8,128)(2,1)S(1)} collective-permute-done((bf16[2,128,1536]{2,1,0:T(8,128)(2,1)S(1)}, bf16[2,128,1536]{2,1,0:T(8,128)(2,1)S(1)}, u32[]{:S(2)}, u32[]{:S(2)}) %collective-permute-start.22) | collective-permute-done | bytes 786464 | tf_op jit(solution)/shard_map/ppermute | solution.py:660
  227.5 6.5 %middle_back.1 = (bf16[128,1536]{1,0:T(8,128)(2,1)}, f32[128,1536]{1,0:T(8,128)}, bf16[1536,128]{1,0:T(8,128)(2,1)}, f32[1,1536]{1,0:T(1,128)}, f32[128,1536]{1,0:T(8,128)}) custom-call(s32[1]{0:T(128)} %bitcast.me_ref, bf16[8,64,1536]{2,1,0:T(8,128)(2,1)} %copy-done.3, bf16[8,64,1536]{2,1,0:T(8,128)(2,1)} %copy-done.4, ...), custom_call_target="tpu_custom_call" | custom-call | flops 115000000 | bytes 1024 | tf_op jit(solution)/shard_map/middle_back/pallas_call | solution.py:518
  234.1 5.2 %add_convert_fusion = bf16[8,96,2688]{2,1,0:T(8,128)(2,1)} fusion(bf16[8,96,2688]{2,1,0:T(8,128)(2,1)} %collective-permute-done.24, bf16[8,96,2688]{2,1,0:T(8,128)(2,1)S(1)} %copy-done.9), kind=kLoop, calls=%fused_computation | loop fusion | flops 8257536 | bytes 12386304 | tf_op jit(solution)/shard_map/convert_element_type | solution.py:879
  240.2 4.1 %all-to-all-start.3 = ((bf16[8,192,128]{2,1,0:T(8,128)(2,1)}), bf16[8,192,128]{2,1,0:T(8,128)(2,1)}, u32[]{:S(2)}, u32[]{:S(2)}) async-start(bf16[8,192,128]{2,1,0:T(8,128)(2,1)} %bitcast.114), calls=%async_computation.3 | async-start | bytes 786432 | tf_op jit(solution)/shard_map/all_to_all | solution.py:650
  244.3 7.2 %collective-permute-done.25 = bf16[128,1536]{1,0:T(8,128)(2,1)} collective-permute-done((bf16[128,1536]{1,0:T(8,128)(2,1)}, bf16[128,1536]{1,0:T(8,128)(2,1)}, u32[]{:S(2)}, u32[]{:S(2)}) %collective-permute-start.25) | collective-permute-done | bytes 393248 | tf_op jit(solution)/shard_map/ppermute | solution.py:660
  258.3 13.3 %attend_backward.1 = (bf16[320,1024]{1,0:T(8,128)(2,1)}, bf16[2,128,1536]{2,1,0:T(8,128)(2,1)}, bf16[2,128,1536]{2,1,0:T(8,128)(2,1)}, bf16[2,128,1536]{2,1,0:T(...) custom-call(s32[1]{0:T(128)} %bitcast.me_ref, bf16[192,1024]{1,0:T(8,128)(2,1)} %get-tuple-element.173.qt_ref, ...), custom_call_target="tpu_custom_call" | custom-call | flops 115000000 | bytes 1024 | tf_op jit(solution)/shard_map/attend_backward/pallas_call | solution.py:289
  271.5 4.4 %qkv_grads.1 = bf16[1536,384]{1,0:T(8,128)(2,1)} custom-call(bf16[320,1024]{1,0:T(8,128)(2,1)} %get-tuple-element.199.gt_ref, bf16[1024,1536]{1,0:T(8,128)(2,1)} %get-tuple-element.200.normed_ref, f32[64,128]{1,0:T(8,128)} %get-tuple-element.201.gains_ref, f32[1,1536]{1,0:T(1,128)} %get-tuple-element.202.mlp_gain_ref), custom_call_target="tpu_custom_call" | custom-call | flops 115000000 | bytes 1024 | tf_op jit(solution)/shard_map/qkv_grads/pallas_call | solution.py:550
  276.0 14.4 %collective-permute-done.26.refs_1_ = bf16[2,128,1536]{2,1,0:T(8,128)(2,1)} collective-permute-done((bf16[2,128,1536]{2,1,0:T(8,128)(2,1)}, bf16[2,128,1536]{2,1,0:T(8,128)(2,1)}, u32[]{:S(2)}, u32[]{:S(2)}) %collective-permute-start.26) | collective-permute-done | bytes 786464 | tf_op jit(solution)/shard_map/ppermute | solution.py:660
  290.3 3.4 collective-permute-start.29
  295.4 4.1 %out_grads.1 = bf16[1536,192]{1,0:T(8,128)(2,1)} custom-call(s32[1]{0:T(128)} %bitcast.me_ref, bf16[192,1024]{1,0:T(8,128)(2,1)} %get-tuple-element.203.att_ref, bf16[2,128,1536]{2,1,0:T(8,128)(2,1)} %pad_maximum_fusion.3.refs_0_, bf16[2,128,1536]{2,1,0:T(8,128)(2,1)} %collective-permute-done.26.refs_1_, ...), custom_call_target="tpu_custom_call" | custom-call | flops 1150000000 | bytes 1024 | tf_op jit(solution)/shard_map/out_grads/pallas_call | solution.py:572
  303.2 20.1 %collective-permute-done.29 = bf16[2,128,1536]{2,1,0:T(8,128)(2,1)} collective-permute-done((bf16[2,128,1536]{2,1,0:T(8,128)(2,1)}, bf16[2,128,1536]{2,1,0:T(8,128)(2,1)}, u32[]{:S(2)}, u32[]{:S(2)}) %collective-permute-start.29) | collective-permute-done | bytes 786464 | tf_op jit(solution)/shard_map/ppermute | solution.py:660
  343.8 3.6 collective-permute-done.32
  352.9 3.9 %all-to-all-start.4 = ((bf16[8,96,576]{2,1,0:T(8,128)(2,1)}), bf16[8,96,576]{2,1,0:T(8,128)(2,1)S(1)}, u32[]{:S(2)}, u32[]{:S(2)}) async-start(bf16[8,96,576]{2,1,0:T(8,128)(2,1)} %broadcast_in_dim.48), calls=%async_computation.4 | async-start | bytes 1966080 | tf_op jit(solution)/shard_map/all_to_all | solution.py:646
  356.8 3.6 collective-permute-done.33
  366.4 7.5 %all-to-all-done.4.in_ref = bf16[8,96,576]{2,1,0:T(8,128)(2,1)S(1)} async-done(((bf16[8,96,576]{2,1,0:T(8,128)(2,1)}), bf16[8,96,576]{2,1,0:T(8,128)(2,1)S(1)}, u32[]{:S(2)}, u32[]{:S(2)}) %all-to-all-start.4) | async-done | bytes 884768 | tf_op jit(solution)/shard_map/all_to_all | solution.py:646
  (221 shorter events, 115.5 us)
Async XLA Ops:
  7.2 122.1 %all-gather.2.cloned.1.call-start = ((), (), s32[]{:S(2)}) async-start(), calls=%async_computation.6 | async-start | bytes 13787136 | tf_op jit(solution)/shard_map/all_gather | solution.py:827
  9.7 15.6 %collective-permute-start.1 = (bf16[128,1664]{1,0:T(8,128)(2,1)S(1)}, bf16[128,1664]{1,0:T(8,128)(2,1)S(1)}, u32[]{:S(2)}, u32[]{:S(2)}) collective-permute-start(bf16[128,1664]{1,0:T(8,128)(2,1)S(1)} %fusion.24.refs_0_), channel_id=1, source_target_pairs={{0,16},{16,0},{32,48},{48,32},{64,80},{80,64},{96,112},{112,96},{1... | collective-permute-start | bytes 1277960 | tf_op jit(solution)/shard_map/ppermute | solution.py:660
  25.3 20.0 %collective-permute-start = (bf16[128,1536]{1,0:T(8,128)(2,1)S(1)}, bf16[128,1536]{1,0:T(8,128)(2,1)}, u32[]{:S(2)}, u32[]{:S(2)}) collective-permute-start(bf16[128,1536]{1,0:T(8,128)(2,1)S(1)} %bitcast.109), channel_id=1, source_target_pairs={{0,16},{16,0},{32,48},{48,32},{64,80},{80,64},{96,112},{112,96},{1... | collective-permute-start | bytes 1179656 | tf_op jit(solution)/shard_map/ppermute | solution.py:660
  25.7 13.9 %collective-permute-start.4 = (bf16[128,1664]{1,0:T(8,128)(2,1)S(1)}, bf16[128,1664]{1,0:T(8,128)(2,1)S(1)}, u32[]{:S(2)}, u32[]{:S(2)}) collective-permute-start(bf16[128,1664]{1,0:T(8,128)(2,1)S(1)} %collective-permute-done.1.refs_1_), channel_id=1, source_target_pairs={{0,32},{16,48},{32,64},{48,80},{64,96},{80,112},{96,0},{112,16},{1... | collective-permute-start | bytes 1277960 | tf_op jit(solution)/shard_map/ppermute | solution.py:660
  31.3 14.6 %collective-permute-start.6 = (bf16[64,1664]{1,0:T(8,128)(2,1)S(1)}, bf16[64,1664]{1,0:T(8,128)(2,1)S(1)}, u32[]{:S(2)}, u32[]{:S(2)}) collective-permute-start(bf16[64,1664]{1,0:T(8,128)(2,1)S(1)} %slice.66), channel_id=1, source_target_pairs={{0,32},{16,48},{32,64},{48,80},{64,96},{80,112},{96,0},{112,16},{1... | collective-permute-start | bytes 638984 | tf_op jit(solution)/shard_map/ppermute | solution.py:660
  31.7 18.1 %collective-permute-start.7 = (bf16[64,1664]{1,0:T(8,128)(2,1)S(1)}, bf16[64,1664]{1,0:T(8,128)(2,1)S(1)}, u32[]{:S(2)}, u32[]{:S(2)}) collective-permute-start(bf16[64,1664]{1,0:T(8,128)(2,1)S(1)} %slice.67), channel_id=1, source_target_pairs={{0,96},{16,112},{32,0},{48,16},{64,32},{80,48},{96,64},{112,80},{1... | collective-permute-start | bytes 638984 | tf_op jit(solution)/shard_map/ppermute | solution.py:660
  39.5 17.0 %collective-permute-start.12 = (bf16[1,4,96,384]{3,2,1,0:T(8,128)(2,1)S(1)}, bf16[1,4,96,384]{3,2,1,0:T(8,128)(2,1)S(1)}, u32[]{:S(2)}, u32[]{:S(2)}) collective-permute-start(bf16[1,4,96,384]{3,2,1,0:T(8,128)(2,1)S(1)} %bitcast.110), channel_id=1, source_target_pairs={{0,4},{1,5},{2,6},{3,7},{4,8},{5,9},{6,10},{7,11},{8,12},{9,13},{1... | collective-permute-start | bytes 884744 | tf_op jit(solution)/shard_map/ppermute | solution.py:769
  41.5 21.2 %collective-permute-start.13 = (bf16[1,4,96,384]{3,2,1,0:T(8,128)(2,1)S(1)}, bf16[1,4,96,384]{3,2,1,0:T(8,128)(2,1)S(1)}, u32[]{:S(2)}, u32[]{:S(2)}) collective-permute-start(bf16[1,4,96,384]{3,2,1,0:T(8,128)(2,1)S(1)} %bitcast.111), channel_id=1, source_target_pairs={{0,8},{1,9},{2,10},{3,11},{4,12},{5,13},{6,14},{7,15},{8,0},{9,1},... | collective-permute-start | bytes 884744 | tf_op jit(solution)/shard_map/ppermute | solution.py:769
  53.2 41.7 %collective-permute-start.16 = (bf16[2,128,1536]{2,1,0:T(8,128)(2,1)S(1)}, bf16[2,128,1536]{2,1,0:T(8,128)(2,1)S(1)}, u32[]{:S(2)}, u32[]{:S(2)}) collective-permute-start(bf16[2,128,1536]{2,1,0:T(8,128)(2,1)S(1)} %pad_maximum_fusion.2.refs_0_), channel_id=1, source_target_pairs={{0,32},{16,48},{32,64},{48,80},{64,96},{80,112},{96,0},{112,16},{1... | collective-permute-start | bytes 2359304 | tf_op jit(solution)/shard_map/ppermute | solution.py:660
  54.3 40.7 %collective-permute-start.17 = (bf16[2,128,1536]{2,1,0:T(8,128)(2,1)S(1)}, bf16[2,128,1536]{2,1,0:T(8,128)(2,1)S(1)}, u32[]{:S(2)}, u32[]{:S(2)}) collective-permute-start(bf16[2,128,1536]{2,1,0:T(8,128)(2,1)S(1)} %pad_maximum_fusion.2.refs_0_), channel_id=1, source_target_pairs={{0,96},{16,112},{32,0},{48,16},{64,32},{80,48},{96,64},{112,80},{1... | collective-permute-start | bytes 2359304 | tf_op jit(solution)/shard_map/ppermute | solution.py:660
  56.5 38.5 %collective-permute-start.18 = (bf16[2,128,1536]{2,1,0:T(8,128)(2,1)S(1)}, bf16[2,128,1536]{2,1,0:T(8,128)(2,1)S(1)}, u32[]{:S(2)}, u32[]{:S(2)}) collective-permute-start(bf16[2,128,1536]{2,1,0:T(8,128)(2,1)S(1)} %pad_maximum_fusion.2.refs_0_), channel_id=1, source_target_pairs={{0,64},{16,80},{32,96},{48,112},{64,0},{80,16},{96,32},{112,48},{1... | collective-permute-start | bytes 2359304 | tf_op jit(solution)/shard_map/ppermute | solution.py:660
  75.1 19.7 %collective-permute-start.15 = (bf16[2,192,512]{2,1,0:T(8,128)(2,1)}, bf16[2,192,512]{2,1,0:T(8,128)(2,1)S(1)}, u32[]{:S(2)}, u32[]{:S(2)}) collective-permute-start(bf16[2,192,512]{2,1,0:T(8,128)(2,1)} %get-tuple-element.127), channel_id=1, source_target_pairs={{0,16},{16,0},{32,48},{48,32},{64,80},{80,64},{96,112},{112,96},{1... | collective-permute-start | bytes 1179656 | tf_op jit(solution)/shard_map/ppermute | solution.py:660
  95.8 16.5 %collective-permute-start.20 = (bf16[2,192,512]{2,1,0:T(8,128)(2,1)S(1)}, bf16[2,192,512]{2,1,0:T(8,128)(2,1)S(1)}, u32[]{:S(2)}, u32[]{:S(2)}) collective-permute-start(bf16[2,192,512]{2,1,0:T(8,128)(2,1)S(1)} %pad_maximum_fusion.4.refs_0_), channel_id=1, source_target_pairs={{0,96},{16,112},{32,0},{48,16},{64,32},{80,48},{96,64},{112,80},{1... | collective-permute-start | bytes 1179656 | tf_op jit(solution)/shard_map/ppermute | solution.py:660
  98.3 15.5 %collective-permute-start.21 = (bf16[2,192,512]{2,1,0:T(8,128)(2,1)S(1)}, bf16[2,192,512]{2,1,0:T(8,128)(2,1)S(1)}, u32[]{:S(2)}, u32[]{:S(2)}) collective-permute-start(bf16[2,192,512]{2,1,0:T(8,128)(2,1)S(1)} %pad_maximum_fusion.4.refs_0_), channel_id=1, source_target_pairs={{0,64},{16,80},{32,96},{48,112},{64,0},{80,16},{96,32},{112,48},{1... | collective-permute-start | bytes 1179656 | tf_op jit(solution)/shard_map/ppermute | solution.py:660
  115.9 33.5 %all-to-all-start = ((bf16[8,192,512]{2,1,0:T(8,128)(2,1)}), bf16[8,192,512]{2,1,0:T(8,128)(2,1)S(1)}, u32[]{:S(2)}, u32[]{:S(2)}) async-start(bf16[8,192,512]{2,1,0:T(8,128)(2,1)} %broadcast_in_dim.45), calls=%async_computation | async-start | bytes 3145728 | tf_op jit(solution)/shard_map/all_to_all | solution.py:646
  149.5 26.1 %all-to-all-start.1 = ((bf16[8,64,1536]{2,1,0:T(8,128)(2,1)}), bf16[8,64,1536]{2,1,0:T(8,128)(2,1)S(1)}, u32[]{:S(2)}, u32[]{:S(2)}) async-start(bf16[8,64,1536]{2,1,0:T(8,128)(2,1)} %get-tuple-element.146), calls=%async_computation.1 | async-start | bytes 3145728 | tf_op jit(solution)/shard_map/all_to_all | solution.py:650
  175.6 25.1 %all-to-all-start.2 = ((bf16[8,64,1536]{2,1,0:T(8,128)(2,1)}), bf16[8,64,1536]{2,1,0:T(8,128)(2,1)S(1)}, u32[]{:S(2)}, u32[]{:S(2)}) async-start(bf16[8,64,1536]{2,1,0:T(8,128)(2,1)} %get-tuple-element.161), calls=%async_computation.2 | async-start | bytes 3145728 | tf_op jit(solution)/shard_map/all_to_all | solution.py:650
  179.5 183.0 %reduce-scatter.2.cloned.1.call-start = ((), (), s32[]{:S(2)}) async-start(), calls=%async_computation.7 | async-start | bytes 5160960 | tf_op jit(solution)/shard_map/reduce_scatter | solution.py:880
  200.7 33.4 %collective-permute-start.24 = (bf16[8,96,2688]{2,1,0:T(8,128)(2,1)}, bf16[8,96,2688]{2,1,0:T(8,128)(2,1)}, u32[]{:S(2)}, u32[]{:S(2)}) collective-permute-start(bf16[8,96,2688]{2,1,0:T(8,128)(2,1)} %get-tuple-element.180), channel_id=1, source_target_pairs={{0,1},{1,0},{2,3},{3,2},{4,5},{5,4},{6,7},{7,6},{8,9},{9,8},{10,11... | collective-permute-start | bytes 12386312 | tf_op jit(solution)/shard_map/ppermute | solution.py:725
  205.2 19.4 %collective-permute-start.22 = (bf16[2,128,1536]{2,1,0:T(8,128)(2,1)S(1)}, bf16[2,128,1536]{2,1,0:T(8,128)(2,1)S(1)}, u32[]{:S(2)}, u32[]{:S(2)}) collective-permute-start(bf16[2,128,1536]{2,1,0:T(8,128)(2,1)S(1)} %get-tuple-element.226), channel_id=1, source_target_pairs={{0,96},{16,112},{32,0},{48,16},{64,32},{80,48},{96,64},{112,80},{1... | collective-permute-start | bytes 2359304 | tf_op jit(solution)/shard_map/ppermute | solution.py:660
  206.3 20.3 %collective-permute-start.23 = (bf16[2,128,1536]{2,1,0:T(8,128)(2,1)S(1)}, bf16[2,128,1536]{2,1,0:T(8,128)(2,1)S(1)}, u32[]{:S(2)}, u32[]{:S(2)}) collective-permute-start(bf16[2,128,1536]{2,1,0:T(8,128)(2,1)S(1)} %get-tuple-element.225), channel_id=1, source_target_pairs={{0,32},{16,48},{32,64},{48,80},{64,96},{80,112},{96,0},{112,16},{1... | collective-permute-start | bytes 2359304 | tf_op jit(solution)/shard_map/ppermute | solution.py:660
  240.2 14.4 %all-to-all-start.3 = ((bf16[8,192,128]{2,1,0:T(8,128)(2,1)}), bf16[8,192,128]{2,1,0:T(8,128)(2,1)}, u32[]{:S(2)}, u32[]{:S(2)}) async-start(bf16[8,192,128]{2,1,0:T(8,128)(2,1)} %bitcast.114), calls=%async_computation.3 | async-start | bytes 786432 | tf_op jit(solution)/shard_map/all_to_all | solution.py:650
  254.6 35.7 %collective-permute-start.26 = (bf16[2,128,1536]{2,1,0:T(8,128)(2,1)}, bf16[2,128,1536]{2,1,0:T(8,128)(2,1)}, u32[]{:S(2)}, u32[]{:S(2)}) collective-permute-start(bf16[2,128,1536]{2,1,0:T(8,128)(2,1)} %pad_maximum_fusion.3.refs_0_), channel_id=1, source_target_pairs={{0,32},{16,48},{32,64},{48,80},{64,96},{80,112},{96,0},{112,16},{1... | collective-permute-start | bytes 2359304 | tf_op jit(solution)/shard_map/ppermute | solution.py:660
  255.1 35.2 %collective-permute-start.27 = (bf16[2,128,1536]{2,1,0:T(8,128)(2,1)}, bf16[2,128,1536]{2,1,0:T(8,128)(2,1)}, u32[]{:S(2)}, u32[]{:S(2)}) collective-permute-start(bf16[2,128,1536]{2,1,0:T(8,128)(2,1)} %pad_maximum_fusion.3.refs_0_), channel_id=1, source_target_pairs={{0,96},{16,112},{32,0},{48,16},{64,32},{80,48},{96,64},{112,80},{1... | collective-permute-start | bytes 2359304 | tf_op jit(solution)/shard_map/ppermute | solution.py:660
  257.9 32.5 %collective-permute-start.28 = (bf16[2,128,1536]{2,1,0:T(8,128)(2,1)}, bf16[2,128,1536]{2,1,0:T(8,128)(2,1)}, u32[]{:S(2)}, u32[]{:S(2)}) collective-permute-start(bf16[2,128,1536]{2,1,0:T(8,128)(2,1)} %pad_maximum_fusion.3.refs_0_), channel_id=1, source_target_pairs={{0,64},{16,80},{32,96},{48,112},{64,0},{80,16},{96,32},{112,48},{1... | collective-permute-start | bytes 2359304 | tf_op jit(solution)/shard_map/ppermute | solution.py:660
  290.3 33.0 %collective-permute-start.29 = (bf16[2,128,1536]{2,1,0:T(8,128)(2,1)}, bf16[2,128,1536]{2,1,0:T(8,128)(2,1)}, u32[]{:S(2)}, u32[]{:S(2)}) collective-permute-start(bf16[2,128,1536]{2,1,0:T(8,128)(2,1)} %get-tuple-element.194), channel_id=1, source_target_pairs={{0,96},{16,112},{32,0},{48,16},{64,32},{80,48},{96,64},{112,80},{1... | collective-permute-start | bytes 2359304 | tf_op jit(solution)/shard_map/ppermute | solution.py:660
  293.7 32.4 %collective-permute-start.30 = (bf16[2,128,1536]{2,1,0:T(8,128)(2,1)}, bf16[2,128,1536]{2,1,0:T(8,128)(2,1)}, u32[]{:S(2)}, u32[]{:S(2)}) collective-permute-start(bf16[2,128,1536]{2,1,0:T(8,128)(2,1)} %get-tuple-element.195), channel_id=1, source_target_pairs={{0,32},{16,48},{32,64},{48,80},{64,96},{80,112},{96,0},{112,16},{1... | collective-permute-start | bytes 2359304 | tf_op jit(solution)/shard_map/ppermute | solution.py:660
  293.7 32.4 %collective-permute-start.31 = (bf16[2,128,1536]{2,1,0:T(8,128)(2,1)}, bf16[2,128,1536]{2,1,0:T(8,128)(2,1)}, u32[]{:S(2)}, u32[]{:S(2)}) collective-permute-start(bf16[2,128,1536]{2,1,0:T(8,128)(2,1)} %get-tuple-element.196), channel_id=1, source_target_pairs={{0,64},{16,80},{32,96},{48,112},{64,0},{80,16},{96,32},{112,48},{1... | collective-permute-start | bytes 2359304 | tf_op jit(solution)/shard_map/ppermute | solution.py:660
  303.2 25.2 %collective-permute-start.35 = (bf16[8,96,576]{2,1,0:T(8,128)(2,1)}, bf16[8,96,576]{2,1,0:T(8,128)(2,1)}, u32[]{:S(2)}, u32[]{:S(2)}) collective-permute-start(bf16[8,96,576]{2,1,0:T(8,128)(2,1)} %dynamic-slice_bitcast_fusion), channel_id=1, source_target_pairs={{0,1},{1,0},{2,3},{3,2},{4,5},{5,4},{6,7},{7,6},{8,9},{9,8},{10,11... | collective-permute-start | bytes 2654216 | tf_op jit(solution)/shard_map/ppermute | solution.py:725
  333.8 13.6 %collective-permute-start.32 = (bf16[2,128,1536]{2,1,0:T(8,128)(2,1)S(1)}, bf16[2,128,1536]{2,1,0:T(8,128)(2,1)S(1)}, u32[]{:S(2)}, u32[]{:S(2)}) collective-permute-start(bf16[2,128,1536]{2,1,0:T(8,128)(2,1)S(1)} %copy-done.28), channel_id=1, source_target_pairs={{0,64},{16,80},{32,96},{48,112},{64,0},{80,16},{96,32},{112,48},{1... | collective-permute-start | bytes 2359304 | tf_op jit(solution)/shard_map/ppermute | solution.py:660
  352.9 21.0 %all-to-all-start.4 = ((bf16[8,96,576]{2,1,0:T(8,128)(2,1)}), bf16[8,96,576]{2,1,0:T(8,128)(2,1)S(1)}, u32[]{:S(2)}, u32[]{:S(2)}) async-start(bf16[8,96,576]{2,1,0:T(8,128)(2,1)} %broadcast_in_dim.48), calls=%async_computation.4 | async-start | bytes 1966080 | tf_op jit(solution)/shard_map/all_to_all | solution.py:646
  364.4 16.2 %collective-permute-start.40 = (bf16[96,2688]{1,0:T(8,128)(2,1)}, bf16[96,2688]{1,0:T(8,128)(2,1)}, u32[]{:S(2)}, u32[]{:S(2)}) collective-permute-start(bf16[96,2688]{1,0:T(8,128)(2,1)} %dynamic-slice_bitcast_fusion.4), channel_id=1, source_target_pairs={{0,2},{1,3},{2,0},{3,1},{4,6},{5,7},{6,4},{7,5},{8,10},{9,11},{10,... | collective-permute-start | bytes 1548296 | tf_op jit(solution)/shard_map/ppermute | solution.py:725
  (59 other events, 556.9 us)
Sparse Core Ops, SparseCore 0:
  10.5 118.7 all-gather.1
  239.4 43.2 reduce-scatter.1

commit v3 on v2

--- a/solution.py
+++ b/solution.py
@@ -313,7 +313,7 @@
     att_refs, refs = refs[:pieces], refs[pieces:]
     x_ref, g_ref, gain_ref, w_ref = refs[:4]
     (
-        mid_ref, second_ref, hid_ref, gate_grad_ref, up_grad_ref, back_ref, out_ref,
+        mid_ref, second_ref, hid_ref, gate_grad_ref, up_grad_ref, back_ref, out_ref, own_ref,
         w_out, w_gate, w_up, w_down, sems, att_all,
     ) = refs[4:]
     places = (
@@ -350,6 +350,12 @@
                 at = pl.multiple_of(block_at(me_ref, dy, dx, n_seq) * part, part)
                 att_all[pl.ds(at, part), :] = ref[dx]
         att = att_all[...]
+    for i in range(n):
+
+        @pl.when(me_ref[0] == n * pl.program_id(0) + i)
+        def _(i=i):
+            own_ref[...] = att[:, i * rows : (i + 1) * rows]
+
     ready(0)
     middle = x + dot(att, w_out[...], 0, 1)
     mid_ref[...] = middle.reshape(n, rows, width)
@@ -406,6 +412,7 @@
             flat,
             stack,
             stack,
+            spec((width, rows), lambda i: (0, 0)),
         ],
         out_shape=(
             shape(n_seq, rows, width, dtype=F32),
@@ -415,6 +422,7 @@
             shape(count, pad),
             shape(n_seq, rows, width),
             shape(n_seq, rows, width),
+            shape(width, rows),
         ),
         scratch_shapes=[
             pltpu.VMEM((width, width), BF16),
@@ -475,6 +483,24 @@
         cost_estimate=cost(0.1),
         name="mlp_grads",
     )(core, *seconds, *([g_all] * HALVES), *gates, *ups, *hiddens)
+
+
+def core_sums_kernel(mine_ref, got_ref, out_ref):
+    out_ref[...] = (mine_ref[...].astype(F32) + got_ref[...].astype(F32)).astype(BF16)
+
+
+def core_sums(mine, got):
+    spec = pl.BlockSpec((2,) + mine.shape[1:], lambda i: (i, 0, 0))
+    return pl.pallas_call(
+        core_sums_kernel,
+        grid=(mine.shape[0] // 2,),
+        in_specs=[spec] * 2,
+        out_specs=spec,
+        out_shape=shape(*mine.shape),
+        compiler_params=pltpu.CompilerParams(vmem_limit_bytes=VMEM),
+        cost_estimate=cost(0.1),
+        name="core_sums",
+    )(mine, got)
 
 
 def middle_kernel(
@@ -536,48 +562,61 @@
     )(me, *backs, *mids, g_own, gain, weights)
 
 
-def qkv_grads_kernel(gt_ref, normed_ref, gains_ref, mlp_gain_ref, out_ref, *, per):
+def head_grads_kernel(
+    core_ref, gt_ref, normed_ref, gains_ref, mlp_gain_ref, branch_ref, *refs, per, shard,
+):
+    att_refs, (own_ref, other_ref) = refs[:-2], refs[-2:]
+    att = jnp.concatenate([ref[...] for ref in att_refs], axis=1)
+    out = dot(branch_ref[...], att, 0, 1).astype(BF16)
     qkv = dot(gt_ref[...], normed_ref[...], 1, 0)
     width = normed_ref.shape[1]
     gains = dot(gains_ref[:, :HEAD].astype(BF16), owners(width, per), 0, 0)
     row = lax.broadcasted_iota(jnp.int32, gains.shape, 0)
     gains = jnp.where(row == 2, mlp_gain_ref[...], gains)
-    out_ref[...] = jnp.concatenate([qkv, gains], axis=0).T.astype(BF16)
-
-
-def qkv_grads(gt, normed, gains, mlp_gain, per):
-    count, width = normed.shape
+    qkv = jnp.concatenate([qkv, gains], axis=0).T.astype(BF16)
+    core = core_ref[0]
+    cut = qkv.shape[1]
+    for i in range(width // shard):
+        rows = slice(i * shard, (i + 1) * shard)
+
+        def put(ref, rows=rows, i=i):
+            ref[i // 2, :, :cut] = qkv[rows]
+            ref[i // 2, :, cut:] = out[rows]
+
+        pl.when(core == i % 2)(functools.partial(put, own_ref))
+        pl.when(core != i % 2)(functools.partial(put, other_ref))
+
+
+def head_grads(core, gt, normed, gains, mlp_gain, branch, atts, per, shard):
+    width = normed.shape[1]
+    columns = gt.shape[0] + HEAD + atts[0].shape[0]
     return pl.pallas_call(
-        functools.partial(qkv_grads_kernel, per=per),
-        out_shape=shape(width, gt.shape[0] + HEAD),
+        functools.partial(head_grads_kernel, per=per, shard=shard),
+        in_specs=[smem()] + vmem(5 + len(atts)),
+        out_shape=(shape(width // shard // 2, shard, columns),) * 2,
         compiler_params=pltpu.CompilerParams(vmem_limit_bytes=VMEM),
         cost_estimate=cost(0.1),
-        name="qkv_grads",
-    )(gt, normed, gains, mlp_gain)
-
-
-def out_grads_kernel(me_ref, att_ref, *refs, n_seq):
-    branch_refs, out_ref, whole = refs[:-2], refs[-2], refs[-1]
-    local = branch_refs[0].shape[1]
-    for dy, ref in zip(STEPS, branch_refs):
-        for dx in range(2):
-            at = pl.multiple_of(block_at(me_ref, dy, dx, n_seq) * local, local)
-            whole[pl.ds(at, local), :] = ref[dx]
-    out_ref[...] = dot(att_ref[...], whole[...], 1, 0).T.astype(BF16)
-
-
-def out_grads(me, att, branch, n_seq):
-    q_own, length = att.shape
-    width = branch[0].shape[2]
+        name="head_grads",
+    )(core, gt, normed, gains, mlp_gain, branch, *atts)
+
+
+def out_blocks_kernel(sums_ref, got_ref, qkv_ref, out_ref):
+    total = sums_ref[...] + got_ref[...].astype(F32)
+    cut, part = qkv_ref.shape[1], out_ref.shape[2]
+    qkv_ref[...] = total[:, :cut].astype(BF16)
+    for j in range(out_ref.shape[0]):
+        out_ref[j] = total[:, cut + j * part : cut + (j + 1) * part].astype(BF16)
+
+
+def out_blocks(sums, got, n_seq, cut):
+    shard, columns = got.shape
     return pl.pallas_call(
-        functools.partial(out_grads_kernel, n_seq=n_seq),
-        in_specs=[smem()] + vmem(1 + len(branch)),
-        out_shape=shape(width, q_own),
-        scratch_shapes=[pltpu.VMEM((length, width), BF16)],
+        out_blocks_kernel,
+        out_shape=(shape(shard, cut), shape(n_seq, shard, (columns - cut) // n_seq)),
         compiler_params=pltpu.CompilerParams(vmem_limit_bytes=VMEM),
-        cost_estimate=cost(1),
-        name="out_grads",
-    )(me, att, *branch)
+        cost_estimate=cost(0.1),
+        name="out_blocks",
+    )(sums, got)
 
 
 def shards_kernel(
@@ -599,7 +638,7 @@
     ) / gain_ref[...].astype(F32)
     sums = jnp.sum(in_ref[:, :, 256:384].astype(F32), axis=0)
     lane = lax.broadcasted_iota(jnp.int32, sums.shape, 1)
-    gains_ref[...] = jnp.where(lane == 0, attn, sums)
+    gains_ref[...] = jnp.where(lane == 0, attn, sums).T
 
 
 def own_shards(parts, w_query, w_key, w_value, attn_gain, q_own, kv_own):
@@ -611,10 +650,10 @@
             shape(shard, w_key.shape[1], dtype=F32),
             shape(shard, w_value.shape[1], dtype=F32),
             shape(shard, q_all, dtype=F32),
-            shape(shard, 128, dtype=F32),
+            shape(128, shard, dtype=F32),
         ),
         compiler_params=pltpu.CompilerParams(vmem_limit_bytes=VMEM),
-        cost_estimate=cost(200),
+        cost_estimate=cost(1),
         name="own_shards",
     )(parts, w_query, w_key, w_value, attn_gain)
 
@@ -683,8 +722,8 @@
     return (pair,) + tuple(step_seq(pair, -dy) for dy in STEPS[1:])
 
 
-def send_along(parts):
-    return (parts[0],) + tuple(step_seq(part, dy) for dy, part in zip(STEPS[1:], parts[1:]))
+def near_of(parts, sign=1):
+    return tuple(step_seq(parts[i], sign * STEPS[i]) for i in (1, 2))
 
 
 def sum_pairs(pairs):
@@ -725,26 +764,20 @@
     return lax.ppermute(held, "fsdp", [(i, i ^ bit) for i in range(n)])
 
 
-def scatter_sum_fsdp(blocks):
+def along_z(grid):
     n = lax.axis_size("fsdp")
-    me = lax.axis_index("fsdp")
-    core, x_hi, z = me % 2, me // 2 % 2, me // 4
-    rest = blocks.shape[1:]
-    grid = blocks.reshape((n // 2, 2) + rest)
-    pick = lax.dynamic_index_in_dim
-    got = swap(pick(grid, 1 - core, 1, keepdims=False), 1)
-    held = (pick(grid, core, 1, keepdims=False).astype(F32) + got.astype(F32)).astype(blocks.dtype)
-    grid = held.reshape((n // 4, 2) + rest)
-    got = [
-        lax.ppermute(pick(grid, (z + by) % (n // 4), 0, keepdims=False), "fsdp", shift(n, 4 * by))
-        for by in range(1, n // 4)
-    ]
-    held = pick(grid, z, 0, keepdims=False).astype(F32)
-    for block in got:
-        held = held + block.astype(F32)
-    held = held.astype(blocks.dtype)
-    got = swap(pick(held, 1 - x_hi, 0, keepdims=False), 2)
-    return pick(held, x_hi, 0, keepdims=False).astype(F32) + got.astype(F32)
+    z = lax.axis_index("fsdp") // 4
+    grid = grid.reshape((n // 4, 2) + grid.shape[1:])
+    pick = functools.partial(lax.dynamic_index_in_dim, grid, axis=0, keepdims=False)
+    got = [lax.ppermute(pick((z + by) % (n // 4)), "fsdp", shift(n, 4 * by)) for by in range(1, 4)]
+    return [pick(z)] + got
+
+
+def sum_z(pairs):
+    x_hi = lax.axis_index("fsdp") // 2 % 2
+    pick = functools.partial(lax.dynamic_index_in_dim, axis=0, keepdims=False)
+    held = sum(pair.astype(F32) for pair in pairs)
+    return pick(held, x_hi), pick(held, 1 - x_hi).astype(pairs[0].dtype)
 
 
 def pair(mine, other, low):
@@ -862,41 +895,53 @@
     back_first = exchange(done[0][5])
     att_second, done[0] = after((att_second, done[0]))
     done.append(mlp(here, att_second, x_all, g_all, gain_rows, mlp_full, 1))
-    middle_parts, seconds, hiddens, gate_grads, up_grads, back_parts, out_parts = zip(*done)
+    middle_parts, seconds, hiddens, gate_grads, up_grads, back_parts, out_parts, att_own = zip(*done)
     back_sent, back_first = after((back_parts[1], back_first))
     backs = (back_first, exchange(back_sent))
     mine, other = mlp_grads(core, seconds, g_all, gate_grads, up_grads, hiddens, shard)
     mine, other, backs = after((mine, other, backs))
     got = swap(other, 1)
-    out_sent = pairs_for(jnp.concatenate(out_parts, axis=1))
-    out_near = [step_seq(pair, dy) for pair, dy in zip(out_sent[1:3], STEPS[1:3])]
-    backs, out_near = after((backs, out_near))
+
+    def sum_fsdp(core_sum):
+        parts = lax.psum_scatter(
+            core_sum.reshape(n_fsdp // 4, 2, shard, -1),
+            "fsdp",
+            scatter_dimension=0,
+            tiled=True,
+            axis_index_groups=[list(range(i, n_fsdp, 4)) for i in range(4)],
+        ).reshape(2, shard, -1)
+        far = lax.dynamic_index_in_dim(parts, 1 - x_hi[0], 0, keepdims=False)
+        return parts, far
 
     branch, grad_middle, grad_att, grad_mlp_g, middle = middle_back(
         here, backs, middle_parts, out_grad[0], gain_rows, mlp_full
     )
-    mine, got, branch = after((mine, got, branch))
-    chip_sums = (mine.astype(F32) + got.astype(F32)).astype(BF16)
-    mlp_sums = lax.psum_scatter(
-        chip_sums.reshape(n_fsdp // 4, 2, shard, -1),
-        "fsdp",
-        scatter_dimension=0,
-        tiled=True,
-        axis_index_groups=[list(range(i, n_fsdp, 4)) for i in range(4)],
-    ).reshape(2, shard, -1)
     grad_heads = exchange(grad_att.reshape(n_seq, q_own, local))
-    branch_pair = jnp.stack([branch, step_seq(branch, 0, 1)])
-    branch_pair, grad_heads, _ = after((branch_pair, grad_heads, chip_sums))
-    branch_pairs = along_y(branch_pair)
-
+    mine, got, out_parts, branch = after((mine, got, out_parts, branch))
+    chip_sums = core_sums(mine, got)
+    out = pairs_for(jnp.concatenate(out_parts, axis=1))
+    out, grad_heads, chip_sums = after((out, grad_heads, chip_sums))
+    mlp_sums, mlp_far = sum_fsdp(chip_sums)
+
+    out_pairs = (out[0], *near_of(out), step_seq(out[3], STEPS[3]))
     gt, *back, gain_grads = attend_backward(
         here, qt, kt, vt, raw, lse, pos, grad_heads, gains, freq, head_full
     )
-    back, branch_pairs = after((back, branch_pairs))
-    back_pairs = send_along(back)
+    head_mine, head_other = head_grads(
+        core, gt, normed, gain_grads, grad_mlp_g, branch, att_own, gain_own, shard
+    )
+    back, head_mine, head_other, out_pairs = after((back, head_mine, head_other, out_pairs))
+    back_pairs = (back[0], *near_of(back), step_seq(back[3], STEPS[3]))
+    z_pairs = along_z(core_sums(head_mine, swap(head_other, 1)))
+    mlp_got = swap(mlp_far, 2)
+    z_pairs, back_pairs, mlp_got = after((z_pairs, back_pairs, mlp_got))
+    head_own, head_far = sum_z(z_pairs)
+    qkv_owned, out_blocks_own = out_blocks(
+        head_own, swap(head_far, 2), n_seq, qkv_own + HEAD
+    )
+    out_owned = total_of(exchange(out_blocks_own)).astype(BF16)
+    att_owned = jnp.concatenate([qkv_owned, out_owned], axis=1)
     grad_normed = sum_pairs(back_pairs)
-    out_far, back_pairs = after((out_sent[3], back_pairs))
-    out_pairs = [out_sent[0], *out_near, step_seq(out_far, STEPS[3])]
     layer_out = (middle + sum_pairs(out_pairs)).astype(BF16)
     xf = x.astype(F32)
     inverse_x = lax.rsqrt(jnp.mean(xf * xf, axis=-1, keepdims=True) + EPS)
@@ -907,32 +952,23 @@
         - xf * inverse_x**3 * jnp.mean(ux * xf, axis=-1, keepdims=True)
     )
 
-    own_grads = jnp.concatenate(
-        [
-            qkv_grads(gt, normed, gain_grads, grad_mlp_g, gain_own),
-            out_grads(here, att, branch_pairs, n_seq),
-        ],
-        axis=1,
-    )
-    att_owned = scatter_sum_fsdp(own_grads.reshape(n_fsdp, shard, -1)).astype(BF16)
-    att_owned, grad_normed = after((att_owned, grad_normed))
+    mlp_owned = mlp_shards(x_hi, mlp_sums, mlp_got, hidden_own)
+    att_seq, (gw_gate, gw_up, gw_down) = after((to_all(att_owned), mlp_owned))
     gw_query, gw_key, gw_value, gw_out, gain_sums = own_shards(
-        to_all(att_owned), w_query, w_key, w_value, attn_gain[:, None], q_own, kv_own
-    )
-    far = lax.dynamic_index_in_dim(mlp_sums, 1 - x_hi[0], 0, keepdims=False)
-    gw_gate, gw_up, gw_down = mlp_shards(x_hi, mlp_sums, swap(far, 2), hidden_own)
+        att_seq, w_query, w_key, w_value, attn_gain[:, None], q_own, kv_own
+    )
     at = qkv_own - 256
     return (
         layer_out[None],
         grad_tokens[None],
-        gain_sums[:, 0],
+        gain_sums[0],
         gw_query,
         gw_key,
         gw_value,
-        gain_sums[:gain_own, at],
-        gain_sums[:gain_own, at + 1],
+        gain_sums[at, :gain_own],
+        gain_sums[at + 1, :gain_own],
         gw_out.T,
-        gain_sums[:, at + 2],
+        gain_sums[at + 2],
         gw_gate,
         gw_up,
         gw_down.T,

time: 397 us -> 382 us (0.962)
  waiting for transfers between devices: 143 us -> 121 us
  Pallas kernels: 106 us -> 119 us
  other arithmetic: 24.7 us -> 16.4 us
    ppermute x29 -> x25, waiting for transfers between devices: 110 us -> 71 us  [step_seq(): return lax.ppermute(block, 'seq', to)]
    pallas_call x2 -> x4, Pallas kernels: 8.48 us -> 21.7 us  [the longest x2 11 us: core_sums(): pl.pallas_call(core_sums_kernel, grid=(mine.shape[0] // 2,), in_specs=[sp...]
    ppermute x6, waiting for transfers between devices: 5.28 us -> 12.3 us  [swap(): return lax.ppermute(held, 'fsdp', [(i, i ^ bit) for i in range(n)])]
    convert_element_type x4 -> x0, other arithmetic: 6.8 us -> none  [the longest x1 5.17 us: on_device(): chip_sums = (mine.astype(F32) + got.astype(F32)).astype(BF16)]
    all_to_all x3 -> x4, waiting for transfers between devices: 6.41 us -> 13 us  [exchange(): return lax.all_to_all(blocks, 'seq', 0, 0, tiled=True)]
    ppermute x29 -> x25, starting transfers between devices: 41.9 us -> 36.9 us  [step_seq(): return lax.ppermute(block, 'seq', to)]
    squeeze x4 -> x5, local copies, waits for them, and re-layouts: 3.1 us -> 7.62 us  [the longest x1 3.18 us: along_z(): pick((z + by) % (n // 4))]
    all_to_all x3 -> x4, starting transfers between devices: 12.3 us -> 16.7 us  [exchange(): return lax.all_to_all(blocks, 'seq', 0, 0, tiled=True)]
  transfers between devices with their start and end apart: 48 -> 45, of which waited for: 25 -> 23; matrix products, arithmetic and copies ran while one was open for 8% -> 7% of each run, Pallas kernels for 27% -> 31%
where the time goes in v3:
time: 382 us; the launch traced here: 375 us
  waiting for transfers between devices  121 us (32%)
  Pallas kernels  119 us (31%)
  starting transfers between devices  78.6 us (21%)
  local copies, waits for them, and re-layouts  24.2 us (6%)
  other arithmetic  16.4 us (4%)
  between operations  15.3 us (4%)
    ppermute x25, waiting for transfers between devices, step_seq(): return lax.ppermute(block, 'seq', to)  71 us
    pallas_call x2, Pallas kernels, mlp(): pl.pallas_call(functools.partial(mlp_kernel, pieces=len(att), width=width...  40.3 us
    ppermute x25, starting transfers between devices, step_seq(): return lax.ppermute(block, 'seq', to)  36.9 us
    pallas_call x1, Pallas kernels, mlp_grads(): pl.pallas_call(functools.partial(mlp_grads_kernel, shard=shard), grid=(wi...  17.6 us
    all_to_all x4, starting transfers between devices, exchange(): return lax.all_to_all(blocks, 'seq', 0, 0, tiled=True)  16.7 us
    pallas_call x1, Pallas kernels, attend_backward(): pl.pallas_call(functools.partial(backward_kernel, heads=heads, block=bloc...  13.3 us
    all_to_all x4, waiting for transfers between devices, exchange(): return lax.all_to_all(blocks, 'seq', 0, 0, tiled=True)  13 us
    ppermute x6, waiting for transfers between devices, swap(): return lax.ppermute(held, 'fsdp', [(i, i ^ bit) for i in range(n)])  12.3 us
  transfers between devices with their start and end apart: 45, of which 23 were waited for; matrix products, arithmetic and copies ran while one was open for 7% of the time, Pallas kernels for 31%

profile of v3, /device:TPU:0, one launch (start us, length us, event | category | flops | bytes accessed | tf_op | source)
XLA Modules:
  0.0 374.6 jit_solution(3276963307062963668)
XLA Ops:
  19.9 5.3 %collective-permute-done.10 = bf16[1,96,384]{2,1,0:T(8,128)(2,1)S(1)} collective-permute-done((bf16[1,96,384]{2,1,0:T(8,128)(2,1)S(1)}, bf16[1,96,384]{2,1,0:T(8,128)(2,1)S(1)}, u32[]{:S(2)}, u32[]{:S(2)}) %collective-permute-start.10) | collective-permute-done | bytes 73760 | tf_op jit(solution)/shard_map/ppermute | solution.py:764
  35.7 3.8 %collective-permute-done.4.refs_4_ = bf16[128,1664]{1,0:T(8,128)(2,1)S(1)} collective-permute-done((bf16[128,1664]{1,0:T(8,128)(2,1)S(1)}, bf16[128,1664]{1,0:T(8,128)(2,1)S(1)}, u32[]{:S(2)}, u32[]{:S(2)}) %collective-permute-start.4) | collective-permute-done | bytes 426016 | tf_op jit(solution)/shard_map/ppermute | solution.py:699
  41.5 3.9 %collective-permute-start.13 = (bf16[1,4,96,384]{3,2,1,0:T(8,128)(2,1)S(1)}, bf16[1,4,96,384]{3,2,1,0:T(8,128)(2,1)S(1)}, u32[]{:S(2)}, u32[]{:S(2)}) collective-permute-start(bf16[1,4,96,384]{3,2,1,0:T(8,128)(2,1)S(1)} %bitcast.110), channel_id=1, source_target_pairs={{0,8},{1,9},{2,10},{3,11},{4,12},{5,13},{6,14},{7,15},{8,0},{9,1},... | collective-permute-start | bytes 884744 | tf_op jit(solution)/shard_map/ppermute | solution.py:802
  58.6 4.1 %collective-permute-done.13 = bf16[1,4,96,384]{3,2,1,0:T(8,128)(2,1)S(1)} collective-permute-done((bf16[1,4,96,384]{3,2,1,0:T(8,128)(2,1)S(1)}, bf16[1,4,96,384]{3,2,1,0:T(8,128)(2,1)S(1)}, u32[]{:S(2)}, u32[]{:S(2)}) %collective-permute-start.13) | collective-permute-done | bytes 294944 | tf_op jit(solution)/shard_map/ppermute | solution.py:802
  63.8 11.3 %attend_forward.1 = (bf16[1024,1536]{1,0:T(8,128)(2,1)}, bf16[1024,1536]{1,0:T(8,128)(2,1)}, f32[256,1024]{1,0:T(8,128)}, bf16[192,1024]{1,0:T(8,128)(2,1)}, bf1...) custom-call(s32[1]{0:T(128)} %bitcast.me_ref, ...), custom_call_target="tpu_custom_call" | custom-call | flops 115000000 | bytes 1024 | tf_op jit(solution)/shard_map/attend_forward/pallas_call | solution.py:177
  77.8 17.0 %collective-permute-done.15 = bf16[2,192,512]{2,1,0:T(8,128)(2,1)S(1)} collective-permute-done((bf16[2,192,512]{2,1,0:T(8,128)(2,1)}, bf16[2,192,512]{2,1,0:T(8,128)(2,1)S(1)}, u32[]{:S(2)}, u32[]{:S(2)}) %collective-permute-start.15) | collective-permute-done | bytes 393248 | tf_op jit(solution)/shard_map/ppermute | solution.py:699
  99.4 7.7 %collective-permute-done.19.refs_1_ = bf16[2,192,512]{2,1,0:T(8,128)(2,1)S(1)} collective-permute-done((bf16[2,192,512]{2,1,0:T(8,128)(2,1)S(1)}, bf16[2,192,512]{2,1,0:T(8,128)(2,1)S(1)}, u32[]{:S(2)}, u32[]{:S(2)}) %collective-permute-start.19) | collective-permute-done | bytes 393248 | tf_op jit(solution)/shard_map/ppermute | solution.py:699
  107.2 5.2 %collective-permute-done.20.refs_2_ = bf16[2,192,512]{2,1,0:T(8,128)(2,1)S(1)} collective-permute-done((bf16[2,192,512]{2,1,0:T(8,128)(2,1)S(1)}, bf16[2,192,512]{2,1,0:T(8,128)(2,1)S(1)}, u32[]{:S(2)}, u32[]{:S(2)}) %collective-permute-start.20) | collective-permute-done | bytes 393248 | tf_op jit(solution)/shard_map/ppermute | solution.py:699
  115.9 5.2 %all-to-all-start = ((bf16[8,192,512]{2,1,0:T(8,128)(2,1)}), bf16[8,192,512]{2,1,0:T(8,128)(2,1)S(1)}, u32[]{:S(2)}, u32[]{:S(2)}) async-start(bf16[8,192,512]{2,1,0:T(8,128)(2,1)} %broadcast_in_dim.45), calls=%async_computation | async-start | bytes 3145728 | tf_op jit(solution)/shard_map/all_to_all | solution.py:685
  121.1 4.0 %in_order.1.refs_5_.refs_2_.refs_3_ = bf16[8,128,1536]{2,1,0:T(8,128)(2,1)} custom-call(s32[1]{0:T(128)} %bitcast.me_ref, bf16[2,128,1536]{2,1,0:T(8,128)(2,1)} %copy-done.5, bf16[2,128,1536]{2,1,0:T(8,128)(2,1)} %copy-done.16, bf16[2,128,1536]{2,1,0:T(8,128)(2,1)} %copy-done.17, bf16[2,128,1536]{2,1,0:T(8,128)(2,1)} %copy-done.18), custom_call_target="tpu_custom_call" | custom-call | flops 115000000 | bytes 1024 | tf_op jit(solution)/shard_map/in_order/pallas_call | solution.py:752
  125.1 4.3 %all-gather.2.cloned.1.call-done.refs_7_.refs_4_.w_ref = bf16[1536,4224]{1,0:T(8,128)(2,1)} async-done(((bf16[96,4224]{1,0:T(8,128)(2,1)}), bf16[1536,4224]{1,0:T(8,128)(2,1)}) %all-gather.2.cloned.1.call-update) | async-done | bytes 12976144 | tf_op jit(solution)/shard_map/all_gather | solution.py:860
  129.3 20.3 %mlp_part.2 = (f32[8,64,1536]{2,1,0:T(8,128)}, bf16[512,1536]{1,0:T(8,128)(2,1)}, bf16[512,896]{1,0:T(8,128)(2,1)}, bf16[512,896]{1,0:T(8,128)(2,1)}, bf16[512,8...) custom-call(s32[1]{0:T(128)} %bitcast.me_ref, ...), custom_call_target="tpu_custom_call" | custom-call | flops 1150000000 | bytes 1024 | tf_op jit(solution)/shard_map/mlp_part/pallas_call | solution.py:393
  150.8 4.7 %all-to-all-start.1 = ((bf16[8,64,1536]{2,1,0:T(8,128)(2,1)}), bf16[8,64,1536]{2,1,0:T(8,128)(2,1)S(1)}, u32[]{:S(2)}, u32[]{:S(2)}) async-start(bf16[8,64,1536]{2,1,0:T(8,128)(2,1)} %get-tuple-element.167), calls=%async_computation.1 | async-start | bytes 3145728 | tf_op jit(solution)/shard_map/all_to_all | solution.py:689
  155.6 20.0 %mlp_part.3 = (f32[8,64,1536]{2,1,0:T(8,128)}, bf16[512,1536]{1,0:T(8,128)(2,1)}, bf16[512,896]{1,0:T(8,128)(2,1)}, bf16[512,896]{1,0:T(8,128)(2,1)}, bf16[512,8...) custom-call(s32[1]{0:T(128)} %bitcast.me_ref, ...), custom_call_target="tpu_custom_call" | custom-call | flops 1150000000 | bytes 1024 | tf_op jit(solution)/shard_map/mlp_part/pallas_call | solution.py:393
  178.5 4.2 %all-to-all-start.2 = ((bf16[8,64,1536]{2,1,0:T(8,128)(2,1)}), bf16[8,64,1536]{2,1,0:T(8,128)(2,1)S(1)}, u32[]{:S(2)}, u32[]{:S(2)}) async-start(bf16[8,64,1536]{2,1,0:T(8,128)(2,1)} %get-tuple-element.183), calls=%async_computation.2 | async-start | bytes 3145728 | tf_op jit(solution)/shard_map/all_to_all | solution.py:689
  182.8 17.6 %mlp_grads.1 = (bf16[8,96,2688]{2,1,0:T(8,128)(2,1)}, bf16[8,96,2688]{2,1,0:T(8,128)(2,1)}) custom-call(s32[1]{0:T(128)} %bitcast.1.core_ref, bf16[512,1536]{1,0:T(8,128)(2,1)} %get-tuple-element.170.refs_0_, bf16[512,1536]{1,0:T(8,128)(2,1)} %get-tuple-element.172.refs_1_, bf16[8,128,1536]{2,1,0:T(8,128)(2,1)} %in_order.1.refs_5_.refs_2_.refs_3_, ...), custom_call_target="tpu_custom_call" | custom-call | flops 115000000 | bytes 1024 | tf_op jit(solution)/shard_map/mlp_grads/pallas_call | solution.py:473
  200.3 3.7 all-to-all-done.2.back1_ref
  205.1 6.3 %middle_back.1 = (bf16[128,1536]{1,0:T(8,128)(2,1)}, f32[128,1536]{1,0:T(8,128)}, bf16[1536,128]{1,0:T(8,128)(2,1)}, f32[1,1536]{1,0:T(1,128)}, f32[128,1536]{1,0:T(8,128)}) custom-call(s32[1]{0:T(128)} %bitcast.me_ref, bf16[8,64,1536]{2,1,0:T(8,128)(2,1)} %copy-done.1, bf16[8,64,1536]{2,1,0:T(8,128)(2,1)} %copy-done.2, ...), custom_call_target="tpu_custom_call" | custom-call | flops 115000000 | bytes 1024 | tf_op jit(solution)/shard_map/middle_back/pallas_call | solution.py:544
  211.4 4.1 %all-to-all-start.3 = ((bf16[8,192,128]{2,1,0:T(8,128)(2,1)}), bf16[8,192,128]{2,1,0:T(8,128)(2,1)}, u32[]{:S(2)}, u32[]{:S(2)}) async-start(bf16[8,192,128]{2,1,0:T(8,128)(2,1)} %bitcast.113), calls=%async_computation.3 | async-start | bytes 786432 | tf_op jit(solution)/shard_map/all_to_all | solution.py:689
  218.0 6.0 %core_sums.2 = bf16[8,96,2688]{2,1,0:T(8,128)(2,1)} custom-call(bf16[8,96,2688]{2,1,0:T(8,128)(2,1)} %get-tuple-element.203.mine_ref, bf16[8,96,2688]{2,1,0:T(8,128)(2,1)} %collective-permute-done.22.got_ref), custom_call_target="tpu_custom_call" | custom-call | flops 115000000 | bytes 1024 | tf_op jit(solution)/shard_map/core_sums/pallas_call | solution.py:494
  231.2 13.3 %attend_backward.1 = (bf16[320,1024]{1,0:T(8,128)(2,1)}, bf16[2,128,1536]{2,1,0:T(8,128)(2,1)}, bf16[2,128,1536]{2,1,0:T(8,128)(2,1)}, bf16[2,128,1536]{2,1,0:T(...) custom-call(s32[1]{0:T(128)} %bitcast.me_ref, bf16[192,1024]{1,0:T(8,128)(2,1)} %get-tuple-element.189.qt_ref, ...), custom_call_target="tpu_custom_call" | custom-call | flops 115000000 | bytes 1024 | tf_op jit(solution)/shard_map/attend_backward/pallas_call | solution.py:289
  244.5 8.6 %head_grads.1 = (bf16[8,96,1920]{2,1,0:T(8,128)(2,1)}, bf16[8,96,1920]{2,1,0:T(8,128)(2,1)}) custom-call(s32[1]{0:T(128)} %bitcast.1.core_ref, bf16[320,1024]{1,0:T(8,128)(2,1)} %get-tuple-element.211.gt_ref, bf16[1024,1536]{1,0:T(8,128)(2,1)} %get-tuple-element.212.normed_ref, f32[64,128]{1,0:T(8,128)} %get-tuple-element.213.gains_ref, ...), custom_call_target="tpu_custom_call" | custom-call | flops 115000000 | bytes 1024 | tf_op jit(solution)/shard_map/head_grads/pallas_call | solution.py:593
  253.1 8.8 %collective-permute-done.23 = bf16[2,128,1536]{2,1,0:T(8,128)(2,1)S(1)} collective-permute-done((bf16[2,128,1536]{2,1,0:T(8,128)(2,1)}, bf16[2,128,1536]{2,1,0:T(8,128)(2,1)S(1)}, u32[]{:S(2)}, u32[]{:S(2)}) %collective-permute-start.23) | collective-permute-done | bytes 786464 | tf_op jit(solution)/shard_map/ppermute | solution.py:699
  271.0 5.0 %core_sums.3 = bf16[8,96,1920]{2,1,0:T(8,128)(2,1)} custom-call(bf16[8,96,1920]{2,1,0:T(8,128)(2,1)} %get-tuple-element.229.mine_ref, bf16[8,96,1920]{2,1,0:T(8,128)(2,1)} %collective-permute-done.27.got_ref), custom_call_target="tpu_custom_call" | custom-call | flops 115000000 | bytes 1024 | tf_op jit(solution)/shard_map/core_sums/pallas_call | solution.py:494
  282.4 3.5 collective-permute-done.31
  286.7 16.9 %collective-permute-done.32 = bf16[2,128,1536]{2,1,0:T(8,128)(2,1)} collective-permute-done((bf16[2,128,1536]{2,1,0:T(8,128)(2,1)}, bf16[2,128,1536]{2,1,0:T(8,128)(2,1)}, u32[]{:S(2)}, u32[]{:S(2)}) %collective-permute-start.32) | collective-permute-done | bytes 786464 | tf_op jit(solution)/shard_map/ppermute | solution.py:699
  308.2 6.8 %collective-permute-done.28 = bf16[2,96,1920]{2,1,0:T(8,128)(2,1)} collective-permute-done((bf16[2,96,1920]{2,1,0:T(8,128)(2,1)}, bf16[2,96,1920]{2,1,0:T(8,128)(2,1)}, u32[]{:S(2)}, u32[]{:S(2)}) %collective-permute-start.28) | collective-permute-done | bytes 737312 | tf_op jit(solution)/shard_map/ppermute | solution.py:772
  326.8 4.3 %collective-permute-done.36.got_ref = bf16[96,1920]{1,0:T(8,128)(2,1)S(1)} collective-permute-done((bf16[96,1920]{1,0:T(8,128)(2,1)S(1)}, bf16[96,1920]{1,0:T(8,128)(2,1)S(1)}, u32[]{:S(2)}, u32[]{:S(2)}) %collective-permute-start.36) | collective-permute-done | bytes 368672 | tf_op jit(solution)/shard_map/ppermute | solution.py:764
  334.0 3.6 all-to-all-start.4
  337.9 7.6 %all-to-all-done.4 = bf16[8,96,192]{2,1,0:T(8,128)(2,1)S(1)} async-done(((bf16[8,96,192]{2,1,0:T(8,128)(2,1)}), bf16[8,96,192]{2,1,0:T(8,128)(2,1)S(1)}, u32[]{:S(2)}, u32[]{:S(2)}) %all-to-all-start.4) | async-done | bytes 294944 | tf_op jit(solution)/shard_map/all_to_all | solution.py:689
  346.6 3.6 all-to-all-start.5
  352.5 8.8 %all-to-all-done.5.in_ref = bf16[8,96,576]{2,1,0:T(8,128)(2,1)S(1)} async-done(((bf16[8,96,576]{2,1,0:T(8,128)(2,1)}), bf16[8,96,576]{2,1,0:T(8,128)(2,1)S(1)}, u32[]{:S(2)}, u32[]{:S(2)}) %all-to-all-start.5) | async-done | bytes 884768 | tf_op jit(solution)/shard_map/all_to_all | solution.py:685
  (202 shorter events, 110.1 us)
Async XLA Ops:
  7.2 122.1 %all-gather.2.cloned.1.call-start = ((), (), s32[]{:S(2)}) async-start(), calls=%async_computation.7 | async-start | bytes 13787136 | tf_op jit(solution)/shard_map/all_gather | solution.py:860
  9.7 15.6 %collective-permute-start.1 = (bf16[128,1664]{1,0:T(8,128)(2,1)S(1)}, bf16[128,1664]{1,0:T(8,128)(2,1)S(1)}, u32[]{:S(2)}, u32[]{:S(2)}) collective-permute-start(bf16[128,1664]{1,0:T(8,128)(2,1)S(1)} %fusion.19.refs_0_), channel_id=1, source_target_pairs={{0,16},{16,0},{32,48},{48,32},{64,80},{80,64},{96,112},{112,96},{1... | collective-permute-start | bytes 1277960 | tf_op jit(solution)/shard_map/ppermute | solution.py:699
  25.3 20.0 %collective-permute-start = (bf16[128,1536]{1,0:T(8,128)(2,1)S(1)}, bf16[128,1536]{1,0:T(8,128)(2,1)}, u32[]{:S(2)}, u32[]{:S(2)}) collective-permute-start(bf16[128,1536]{1,0:T(8,128)(2,1)S(1)} %bitcast.108), channel_id=1, source_target_pairs={{0,16},{16,0},{32,48},{48,32},{64,80},{80,64},{96,112},{112,96},{1... | collective-permute-start | bytes 1179656 | tf_op jit(solution)/shard_map/ppermute | solution.py:699
  25.6 13.9 %collective-permute-start.4 = (bf16[128,1664]{1,0:T(8,128)(2,1)S(1)}, bf16[128,1664]{1,0:T(8,128)(2,1)S(1)}, u32[]{:S(2)}, u32[]{:S(2)}) collective-permute-start(bf16[128,1664]{1,0:T(8,128)(2,1)S(1)} %collective-permute-done.1.refs_1_), channel_id=1, source_target_pairs={{0,32},{16,48},{32,64},{48,80},{64,96},{80,112},{96,0},{112,16},{1... | collective-permute-start | bytes 1277960 | tf_op jit(solution)/shard_map/ppermute | solution.py:699
  31.3 14.6 %collective-permute-start.6 = (bf16[64,1664]{1,0:T(8,128)(2,1)S(1)}, bf16[64,1664]{1,0:T(8,128)(2,1)S(1)}, u32[]{:S(2)}, u32[]{:S(2)}) collective-permute-start(bf16[64,1664]{1,0:T(8,128)(2,1)S(1)} %slice.66), channel_id=1, source_target_pairs={{0,32},{16,48},{32,64},{48,80},{64,96},{80,112},{96,0},{112,16},{1... | collective-permute-start | bytes 638984 | tf_op jit(solution)/shard_map/ppermute | solution.py:699
  31.7 18.1 %collective-permute-start.7 = (bf16[64,1664]{1,0:T(8,128)(2,1)S(1)}, bf16[64,1664]{1,0:T(8,128)(2,1)S(1)}, u32[]{:S(2)}, u32[]{:S(2)}) collective-permute-start(bf16[64,1664]{1,0:T(8,128)(2,1)S(1)} %slice.67), channel_id=1, source_target_pairs={{0,96},{16,112},{32,0},{48,16},{64,32},{80,48},{96,64},{112,80},{1... | collective-permute-start | bytes 638984 | tf_op jit(solution)/shard_map/ppermute | solution.py:699
  39.5 17.0 %collective-permute-start.12 = (bf16[1,4,96,384]{3,2,1,0:T(8,128)(2,1)S(1)}, bf16[1,4,96,384]{3,2,1,0:T(8,128)(2,1)S(1)}, u32[]{:S(2)}, u32[]{:S(2)}) collective-permute-start(bf16[1,4,96,384]{3,2,1,0:T(8,128)(2,1)S(1)} %bitcast.109), channel_id=1, source_target_pairs={{0,4},{1,5},{2,6},{3,7},{4,8},{5,9},{6,10},{7,11},{8,12},{9,13},{1... | collective-permute-start | bytes 884744 | tf_op jit(solution)/shard_map/ppermute | solution.py:802
  41.5 21.2 %collective-permute-start.13 = (bf16[1,4,96,384]{3,2,1,0:T(8,128)(2,1)S(1)}, bf16[1,4,96,384]{3,2,1,0:T(8,128)(2,1)S(1)}, u32[]{:S(2)}, u32[]{:S(2)}) collective-permute-start(bf16[1,4,96,384]{3,2,1,0:T(8,128)(2,1)S(1)} %bitcast.110), channel_id=1, source_target_pairs={{0,8},{1,9},{2,10},{3,11},{4,12},{5,13},{6,14},{7,15},{8,0},{9,1},... | collective-permute-start | bytes 884744 | tf_op jit(solution)/shard_map/ppermute | solution.py:802
  53.2 41.7 %collective-permute-start.16 = (bf16[2,128,1536]{2,1,0:T(8,128)(2,1)S(1)}, bf16[2,128,1536]{2,1,0:T(8,128)(2,1)S(1)}, u32[]{:S(2)}, u32[]{:S(2)}) collective-permute-start(bf16[2,128,1536]{2,1,0:T(8,128)(2,1)S(1)} %pad_maximum_fusion.1.refs_0_), channel_id=1, source_target_pairs={{0,32},{16,48},{32,64},{48,80},{64,96},{80,112},{96,0},{112,16},{1... | collective-permute-start | bytes 2359304 | tf_op jit(solution)/shard_map/ppermute | solution.py:699
  54.2 40.7 %collective-permute-start.17 = (bf16[2,128,1536]{2,1,0:T(8,128)(2,1)S(1)}, bf16[2,128,1536]{2,1,0:T(8,128)(2,1)S(1)}, u32[]{:S(2)}, u32[]{:S(2)}) collective-permute-start(bf16[2,128,1536]{2,1,0:T(8,128)(2,1)S(1)} %pad_maximum_fusion.1.refs_0_), channel_id=1, source_target_pairs={{0,96},{16,112},{32,0},{48,16},{64,32},{80,48},{96,64},{112,80},{1... | collective-permute-start | bytes 2359304 | tf_op jit(solution)/shard_map/ppermute | solution.py:699
  56.5 38.5 %collective-permute-start.18 = (bf16[2,128,1536]{2,1,0:T(8,128)(2,1)S(1)}, bf16[2,128,1536]{2,1,0:T(8,128)(2,1)S(1)}, u32[]{:S(2)}, u32[]{:S(2)}) collective-permute-start(bf16[2,128,1536]{2,1,0:T(8,128)(2,1)S(1)} %pad_maximum_fusion.1.refs_0_), channel_id=1, source_target_pairs={{0,64},{16,80},{32,96},{48,112},{64,0},{80,16},{96,32},{112,48},{1... | collective-permute-start | bytes 2359304 | tf_op jit(solution)/shard_map/ppermute | solution.py:699
  75.2 19.7 %collective-permute-start.15 = (bf16[2,192,512]{2,1,0:T(8,128)(2,1)}, bf16[2,192,512]{2,1,0:T(8,128)(2,1)S(1)}, u32[]{:S(2)}, u32[]{:S(2)}) collective-permute-start(bf16[2,192,512]{2,1,0:T(8,128)(2,1)} %get-tuple-element.148), channel_id=1, source_target_pairs={{0,16},{16,0},{32,48},{48,32},{64,80},{80,64},{96,112},{112,96},{1... | collective-permute-start | bytes 1179656 | tf_op jit(solution)/shard_map/ppermute | solution.py:699
  95.8 16.5 %collective-permute-start.20 = (bf16[2,192,512]{2,1,0:T(8,128)(2,1)S(1)}, bf16[2,192,512]{2,1,0:T(8,128)(2,1)S(1)}, u32[]{:S(2)}, u32[]{:S(2)}) collective-permute-start(bf16[2,192,512]{2,1,0:T(8,128)(2,1)S(1)} %pad_maximum_fusion.2.refs_0_), channel_id=1, source_target_pairs={{0,96},{16,112},{32,0},{48,16},{64,32},{80,48},{96,64},{112,80},{1... | collective-permute-start | bytes 1179656 | tf_op jit(solution)/shard_map/ppermute | solution.py:699
  98.3 15.5 %collective-permute-start.21 = (bf16[2,192,512]{2,1,0:T(8,128)(2,1)S(1)}, bf16[2,192,512]{2,1,0:T(8,128)(2,1)S(1)}, u32[]{:S(2)}, u32[]{:S(2)}) collective-permute-start(bf16[2,192,512]{2,1,0:T(8,128)(2,1)S(1)} %pad_maximum_fusion.2.refs_0_), channel_id=1, source_target_pairs={{0,64},{16,80},{32,96},{48,112},{64,0},{80,16},{96,32},{112,48},{1... | collective-permute-start | bytes 1179656 | tf_op jit(solution)/shard_map/ppermute | solution.py:699
  115.9 33.7 %all-to-all-start = ((bf16[8,192,512]{2,1,0:T(8,128)(2,1)}), bf16[8,192,512]{2,1,0:T(8,128)(2,1)S(1)}, u32[]{:S(2)}, u32[]{:S(2)}) async-start(bf16[8,192,512]{2,1,0:T(8,128)(2,1)} %broadcast_in_dim.45), calls=%async_computation | async-start | bytes 3145728 | tf_op jit(solution)/shard_map/all_to_all | solution.py:685
  150.8 26.5 %all-to-all-start.1 = ((bf16[8,64,1536]{2,1,0:T(8,128)(2,1)}), bf16[8,64,1536]{2,1,0:T(8,128)(2,1)S(1)}, u32[]{:S(2)}, u32[]{:S(2)}) async-start(bf16[8,64,1536]{2,1,0:T(8,128)(2,1)} %get-tuple-element.167), calls=%async_computation.1 | async-start | bytes 3145728 | tf_op jit(solution)/shard_map/all_to_all | solution.py:689
  178.5 25.5 %all-to-all-start.2 = ((bf16[8,64,1536]{2,1,0:T(8,128)(2,1)}), bf16[8,64,1536]{2,1,0:T(8,128)(2,1)S(1)}, u32[]{:S(2)}, u32[]{:S(2)}) async-start(bf16[8,64,1536]{2,1,0:T(8,128)(2,1)} %get-tuple-element.183), calls=%async_computation.2 | async-start | bytes 3145728 | tf_op jit(solution)/shard_map/all_to_all | solution.py:689
  211.4 14.1 %all-to-all-start.3 = ((bf16[8,192,128]{2,1,0:T(8,128)(2,1)}), bf16[8,192,128]{2,1,0:T(8,128)(2,1)}, u32[]{:S(2)}, u32[]{:S(2)}) async-start(bf16[8,192,128]{2,1,0:T(8,128)(2,1)} %bitcast.113), calls=%async_computation.3 | async-start | bytes 786432 | tf_op jit(solution)/shard_map/all_to_all | solution.py:689
  215.5 65.8 %reduce-scatter.2.cloned.1.call-start = ((), (), s32[]{:S(2)}) async-start(), calls=%async_computation.8 | async-start | bytes 5160960 | tf_op jit(solution)/shard_map/reduce_scatter | solution.py:906
  225.6 36.4 %collective-permute-start.23 = (bf16[2,128,1536]{2,1,0:T(8,128)(2,1)}, bf16[2,128,1536]{2,1,0:T(8,128)(2,1)S(1)}, u32[]{:S(2)}, u32[]{:S(2)}) collective-permute-start(bf16[2,128,1536]{2,1,0:T(8,128)(2,1)} %get-tuple-element.221), channel_id=1, source_target_pairs={{0,96},{16,112},{32,0},{48,16},{64,32},{80,48},{96,64},{112,80},{1... | collective-permute-start | bytes 2359304 | tf_op jit(solution)/shard_map/ppermute | solution.py:699
  228.7 36.5 %collective-permute-start.24 = (bf16[2,128,1536]{2,1,0:T(8,128)(2,1)}, bf16[2,128,1536]{2,1,0:T(8,128)(2,1)S(1)}, u32[]{:S(2)}, u32[]{:S(2)}) collective-permute-start(bf16[2,128,1536]{2,1,0:T(8,128)(2,1)} %get-tuple-element.222), channel_id=1, source_target_pairs={{0,32},{16,48},{32,64},{48,80},{64,96},{80,112},{96,0},{112,16},{1... | collective-permute-start | bytes 2359304 | tf_op jit(solution)/shard_map/ppermute | solution.py:699
  228.7 36.5 %collective-permute-start.25 = (bf16[2,128,1536]{2,1,0:T(8,128)(2,1)}, bf16[2,128,1536]{2,1,0:T(8,128)(2,1)}, u32[]{:S(2)}, u32[]{:S(2)}) collective-permute-start(bf16[2,128,1536]{2,1,0:T(8,128)(2,1)} %get-tuple-element.223), channel_id=1, source_target_pairs={{0,64},{16,80},{32,96},{48,112},{64,0},{80,16},{96,32},{112,48},{1... | collective-permute-start | bytes 2359304 | tf_op jit(solution)/shard_map/ppermute | solution.py:699
  265.3 20.7 %collective-permute-start.31 = (bf16[2,128,1536]{2,1,0:T(8,128)(2,1)}, bf16[2,128,1536]{2,1,0:T(8,128)(2,1)}, u32[]{:S(2)}, u32[]{:S(2)}) collective-permute-start(bf16[2,128,1536]{2,1,0:T(8,128)(2,1)} %get-tuple-element.232), channel_id=1, source_target_pairs={{0,96},{16,112},{32,0},{48,16},{64,32},{80,48},{96,64},{112,80},{1... | collective-permute-start | bytes 2359304 | tf_op jit(solution)/shard_map/ppermute | solution.py:699
  265.6 38.0 %collective-permute-start.32 = (bf16[2,128,1536]{2,1,0:T(8,128)(2,1)}, bf16[2,128,1536]{2,1,0:T(8,128)(2,1)}, u32[]{:S(2)}, u32[]{:S(2)}) collective-permute-start(bf16[2,128,1536]{2,1,0:T(8,128)(2,1)} %get-tuple-element.233), channel_id=1, source_target_pairs={{0,32},{16,48},{32,64},{48,80},{64,96},{80,112},{96,0},{112,16},{1... | collective-permute-start | bytes 2359304 | tf_op jit(solution)/shard_map/ppermute | solution.py:699
  268.1 39.1 %collective-permute-start.33 = (bf16[2,128,1536]{2,1,0:T(8,128)(2,1)}, bf16[2,128,1536]{2,1,0:T(8,128)(2,1)}, u32[]{:S(2)}, u32[]{:S(2)}) collective-permute-start(bf16[2,128,1536]{2,1,0:T(8,128)(2,1)} %get-tuple-element.234), channel_id=1, source_target_pairs={{0,64},{16,80},{32,96},{48,112},{64,0},{80,16},{96,32},{112,48},{1... | collective-permute-start | bytes 2359304 | tf_op jit(solution)/shard_map/ppermute | solution.py:699
  279.1 35.9 %collective-permute-start.28 = (bf16[2,96,1920]{2,1,0:T(8,128)(2,1)}, bf16[2,96,1920]{2,1,0:T(8,128)(2,1)}, u32[]{:S(2)}, u32[]{:S(2)}) collective-permute-start(bf16[2,96,1920]{2,1,0:T(8,128)(2,1)} %get-tuple-element.267), channel_id=1, source_target_pairs={{0,4},{1,5},{2,6},{3,7},{4,8},{5,9},{6,10},{7,11},{8,12},{9,13},{1... | collective-permute-start | bytes 2211848 | tf_op jit(solution)/shard_map/ppermute | solution.py:772
  279.1 35.8 %collective-permute-start.29 = (bf16[2,96,1920]{2,1,0:T(8,128)(2,1)}, bf16[2,96,1920]{2,1,0:T(8,128)(2,1)}, u32[]{:S(2)}, u32[]{:S(2)}) collective-permute-start(bf16[2,96,1920]{2,1,0:T(8,128)(2,1)} %get-tuple-element.266), channel_id=1, source_target_pairs={{0,8},{1,9},{2,10},{3,11},{4,12},{5,13},{6,14},{7,15},{8,0},{9,1},... | collective-permute-start | bytes 2211848 | tf_op jit(solution)/shard_map/ppermute | solution.py:772
  285.9 29.6 %collective-permute-start.30 = (bf16[2,96,1920]{2,1,0:T(8,128)(2,1)}, bf16[2,96,1920]{2,1,0:T(8,128)(2,1)S(1)}, u32[]{:S(2)}, u32[]{:S(2)}) collective-permute-start(bf16[2,96,1920]{2,1,0:T(8,128)(2,1)} %get-tuple-element.265), channel_id=1, source_target_pairs={{0,12},{1,13},{2,14},{3,15},{4,0},{5,1},{6,2},{7,3},{8,4},{9,5},{1... | collective-permute-start | bytes 2211848 | tf_op jit(solution)/shard_map/ppermute | solution.py:772
  307.3 15.4 %collective-permute-start.26 = (bf16[128,1536]{1,0:T(8,128)(2,1)S(1)}, bf16[128,1536]{1,0:T(8,128)(2,1)S(1)}, u32[]{:S(2)}, u32[]{:S(2)}) collective-permute-start(bf16[128,1536]{1,0:T(8,128)(2,1)S(1)} %fusion.21), channel_id=1, source_target_pairs={{0,16},{16,0},{32,48},{48,32},{64,80},{80,64},{96,112},{112,96},{1... | collective-permute-start | bytes 1179656 | tf_op jit(solution)/shard_map/ppermute | solution.py:699
  318.1 13.1 %collective-permute-start.36 = (bf16[96,1920]{1,0:T(8,128)(2,1)S(1)}, bf16[96,1920]{1,0:T(8,128)(2,1)S(1)}, u32[]{:S(2)}, u32[]{:S(2)}) collective-permute-start(bf16[96,1920]{1,0:T(8,128)(2,1)S(1)} %fusion.23), channel_id=1, source_target_pairs={{0,2},{1,3},{2,0},{3,1},{4,6},{5,7},{6,4},{7,5},{8,10},{9,11},{10,... | collective-permute-start | bytes 1105928 | tf_op jit(solution)/shard_map/ppermute | solution.py:764
  321.7 15.9 %collective-permute-start.35 = (bf16[128,1536]{1,0:T(8,128)(2,1)S(1)}, bf16[128,1536]{1,0:T(8,128)(2,1)S(1)}, u32[]{:S(2)}, u32[]{:S(2)}) collective-permute-start(bf16[128,1536]{1,0:T(8,128)(2,1)S(1)} %fusion.22), channel_id=1, source_target_pairs={{0,16},{16,0},{32,48},{48,32},{64,80},{80,64},{96,112},{112,96},{1... | collective-permute-start | bytes 1179656 | tf_op jit(solution)/shard_map/ppermute | solution.py:699
  346.6 14.7 %all-to-all-start.5 = ((bf16[8,96,576]{2,1,0:T(8,128)(2,1)}), bf16[8,96,576]{2,1,0:T(8,128)(2,1)S(1)}, u32[]{:S(2)}, u32[]{:S(2)}) async-start(bf16[8,96,576]{2,1,0:T(8,128)(2,1)} %broadcast_in_dim.48), calls=%async_computation.6 | async-start | bytes 1966080 | tf_op jit(solution)/shard_map/all_to_all | solution.py:685
  (50 other events, 446.9 us)
Sparse Core Ops, SparseCore 0:
  10.5 118.7 all-gather.1
  225.7 45.4 reduce-scatter.1

commit v4 on v3

--- a/solution.py
+++ b/solution.py
@@ -358,7 +358,12 @@
 
     ready(0)
     middle = x + dot(att, w_out[...], 0, 1)
-    mid_ref[...] = middle.reshape(n, rows, width)
+    for i in range(n):
+
+        @pl.when(me_ref[0] == n * pl.program_id(0) + i)
+        def _(i=i):
+            mid_ref[...] = middle[i * rows : (i + 1) * rows]
+
     inverse = lax.rsqrt(jnp.mean(middle * middle, axis=1, keepdims=True) + EPS)
     second = (middle * inverse * gain_ref[1:2, :]).astype(BF16)
     second_ref[...] = second
@@ -405,7 +410,7 @@
             spec(memory_space=pl.ANY),
         ],
         out_specs=[
-            stack,
+            spec((rows, width), lambda i: (0, 0)),
             spec((step, width), lambda i: (i, 0)),
             flat,
             flat,
@@ -415,7 +420,7 @@
             spec((width, rows), lambda i: (0, 0)),
         ],
         out_shape=(
-            shape(n_seq, rows, width, dtype=F32),
+            shape(rows, width, dtype=F32),
             shape(count, width),
             shape(count, pad),
             shape(count, pad),
@@ -504,25 +509,16 @@
 
 
 def middle_kernel(
-    me_ref, back0_ref, back1_ref, mid0_ref, mid1_ref, g_ref, gain_ref, w_ref,
+    back0_ref, back1_ref, mid0_ref, mid1_ref, g_ref, gain_ref, w_ref,
     branch_ref, grad_ref, att_ref, gain_grad_ref, mid_out_ref,
-    mid, w, sems, *, width,
+    w, sem, *, width,
 ):
-    half = back0_ref.shape[1]
-    me = me_ref[0]
-    copies = [
-        pltpu.make_async_copy(mid0_ref.at[me], mid.at[pl.ds(0, half)], sems.at[0]),
-        pltpu.make_async_copy(mid1_ref.at[me], mid.at[pl.ds(half, half)], sems.at[1]),
-        pltpu.make_async_copy(w_ref.at[:, :width], w, sems.at[2]),
-    ]
-    for copy in copies:
-        copy.start()
+    copy = pltpu.make_async_copy(w_ref.at[:, :width], w, sem)
+    copy.start()
     grad = jnp.concatenate(
         [jnp.sum(ref[...].astype(F32), axis=0) for ref in (back0_ref, back1_ref)], axis=0
     )
-    copies[0].wait()
-    copies[1].wait()
-    middle = mid[...]
+    middle = jnp.concatenate([mid0_ref[...], mid1_ref[...]], axis=0)
     mid_out_ref[...] = middle
     inverse = lax.rsqrt(jnp.mean(middle * middle, axis=1, keepdims=True) + EPS)
     u = grad * gain_ref[1:2, :]
@@ -534,16 +530,15 @@
     grad_ref[...] = grad_middle
     branch = grad_middle.astype(BF16)
     branch_ref[...] = branch
-    copies[2].wait()
+    copy.wait()
     att_ref[...] = dot(branch, w[...], 1, 0).T.astype(BF16)
 
 
-def middle_back(me, backs, mids, g_own, gain, weights):
+def middle_back(backs, mids, g_own, gain, weights):
     local, width = g_own.shape
-    anywhere = pl.BlockSpec(memory_space=pl.ANY)
     return pl.pallas_call(
         functools.partial(middle_kernel, width=width),
-        in_specs=[smem()] + vmem(2) + [anywhere] * 2 + vmem(2) + [anywhere],
+        in_specs=vmem(6) + [pl.BlockSpec(memory_space=pl.ANY)],
         out_shape=(
             shape(local, width),
             shape(local, width, dtype=F32),
@@ -552,76 +547,92 @@
             shape(local, width, dtype=F32),
         ),
         scratch_shapes=[
-            pltpu.VMEM((local, width), F32),
             pltpu.VMEM((width, width), BF16),
-            pltpu.SemaphoreType.DMA((3,)),
+            pltpu.SemaphoreType.DMA(()),
         ],
         compiler_params=pltpu.CompilerParams(vmem_limit_bytes=VMEM),
         cost_estimate=cost(0.1),
         name="middle_back",
-    )(me, *backs, *mids, g_own, gain, weights)
-
-
-def head_grads_kernel(
-    core_ref, gt_ref, normed_ref, gains_ref, mlp_gain_ref, branch_ref, *refs, per, shard,
+    )(*backs, *mids, g_own, gain, weights)
+
+
+def split_rows(core_ref, rows, shard, own_ref, other_ref):
+    core = core_ref[0]
+    for i in range(rows.shape[0] // shard):
+
+        def put(ref, i=i):
+            ref[i // 2] = rows[i * shard : (i + 1) * shard]
+
+        pl.when(core == i % 2)(functools.partial(put, own_ref))
+        pl.when(core != i % 2)(functools.partial(put, other_ref))
+
+
+def qkv_grads_kernel(
+    core_ref, gt_ref, normed_ref, gains_ref, mlp_gain_ref, own_ref, other_ref, *, per, shard,
 ):
-    att_refs, (own_ref, other_ref) = refs[:-2], refs[-2:]
-    att = jnp.concatenate([ref[...] for ref in att_refs], axis=1)
-    out = dot(branch_ref[...], att, 0, 1).astype(BF16)
     qkv = dot(gt_ref[...], normed_ref[...], 1, 0)
     width = normed_ref.shape[1]
     gains = dot(gains_ref[:, :HEAD].astype(BF16), owners(width, per), 0, 0)
     row = lax.broadcasted_iota(jnp.int32, gains.shape, 0)
     gains = jnp.where(row == 2, mlp_gain_ref[...], gains)
-    qkv = jnp.concatenate([qkv, gains], axis=0).T.astype(BF16)
-    core = core_ref[0]
-    cut = qkv.shape[1]
-    for i in range(width // shard):
-        rows = slice(i * shard, (i + 1) * shard)
-
-        def put(ref, rows=rows, i=i):
-            ref[i // 2, :, :cut] = qkv[rows]
-            ref[i // 2, :, cut:] = out[rows]
-
-        pl.when(core == i % 2)(functools.partial(put, own_ref))
-        pl.when(core != i % 2)(functools.partial(put, other_ref))
-
-
-def head_grads(core, gt, normed, gains, mlp_gain, branch, atts, per, shard):
-    width = normed.shape[1]
-    columns = gt.shape[0] + HEAD + atts[0].shape[0]
-    return pl.pallas_call(
-        functools.partial(head_grads_kernel, per=per, shard=shard),
-        in_specs=[smem()] + vmem(5 + len(atts)),
-        out_shape=(shape(width // shard // 2, shard, columns),) * 2,
+    rows = jnp.concatenate([qkv, gains], axis=0).T.astype(BF16)
+    split_rows(core_ref, rows, shard, own_ref, other_ref)
+
+
+def qkv_grads(core, gt, normed, gains, mlp_gain, per, shard):
+    count, width = normed.shape
+    return pl.pallas_call(
+        functools.partial(qkv_grads_kernel, per=per, shard=shard),
+        in_specs=[smem()] + vmem(4),
+        out_shape=(shape(width // shard // 2, shard, gt.shape[0] + HEAD),) * 2,
         compiler_params=pltpu.CompilerParams(vmem_limit_bytes=VMEM),
         cost_estimate=cost(0.1),
-        name="head_grads",
-    )(core, gt, normed, gains, mlp_gain, branch, *atts)
-
-
-def out_blocks_kernel(sums_ref, got_ref, qkv_ref, out_ref):
-    total = sums_ref[...] + got_ref[...].astype(F32)
-    cut, part = qkv_ref.shape[1], out_ref.shape[2]
-    qkv_ref[...] = total[:, :cut].astype(BF16)
+        name="qkv_grads",
+    )(core, gt, normed, gains, mlp_gain)
+
+
+def out_grads_kernel(core_ref, branch_ref, *refs, shard):
+    att_refs, (own_ref, other_ref) = refs[:-2], refs[-2:]
+    att = jnp.concatenate([ref[...] for ref in att_refs], axis=1)
+    rows = dot(branch_ref[...], att, 0, 1).astype(BF16)
+    split_rows(core_ref, rows, shard, own_ref, other_ref)
+
+
+def out_grads(core, branch, atts, shard):
+    width = branch.shape[1]
+    heads = atts[0].shape[0]
+    return pl.pallas_call(
+        functools.partial(out_grads_kernel, shard=shard),
+        in_specs=[smem()] + vmem(1 + len(atts)),
+        out_shape=(shape(width // shard // 2, shard, heads),) * 2,
+        compiler_params=pltpu.CompilerParams(vmem_limit_bytes=VMEM),
+        cost_estimate=cost(0.1),
+        name="out_grads",
+    )(core, branch, *atts)
+
+
+def out_blocks_kernel(x_ref, sums_ref, got_ref, out_ref):
+    total = (sums_ref[x_ref[0]].astype(F32) + got_ref[...].astype(F32)).astype(BF16)
+    part = out_ref.shape[2]
     for j in range(out_ref.shape[0]):
-        out_ref[j] = total[:, cut + j * part : cut + (j + 1) * part].astype(BF16)
-
-
-def out_blocks(sums, got, n_seq, cut):
-    shard, columns = got.shape
+        out_ref[j] = total[:, j * part : (j + 1) * part]
+
+
+def out_blocks(x_hi, sums, got, n_seq):
+    shard, heads = got.shape
     return pl.pallas_call(
         out_blocks_kernel,
-        out_shape=(shape(shard, cut), shape(n_seq, shard, (columns - cut) // n_seq)),
+        in_specs=[smem()] + vmem(2),
+        out_shape=shape(n_seq, shard, heads // n_seq),
         compiler_params=pltpu.CompilerParams(vmem_limit_bytes=VMEM),
         cost_estimate=cost(0.1),
         name="out_blocks",
-    )(sums, got)
+    )(x_hi, sums, got)
 
 
 def shards_kernel(
     in_ref, wq_ref, wk_ref, wv_ref, gain_ref,
-    gq_ref, gk_ref, gv_ref, go_ref, gains_ref, *, q_own, kv_own,
+    gq_ref, gk_ref, gv_ref, go_ref, *gain_refs, q_own, kv_own,
 ):
     n = in_ref.shape[0]
 
@@ -638,10 +649,13 @@
     ) / gain_ref[...].astype(F32)
     sums = jnp.sum(in_ref[:, :, 256:384].astype(F32), axis=0)
     lane = lax.broadcasted_iota(jnp.int32, sums.shape, 1)
-    gains_ref[...] = jnp.where(lane == 0, attn, sums).T
-
-
-def own_shards(parts, w_query, w_key, w_value, attn_gain, q_own, kv_own):
+    gains = jnp.where(lane == 0, attn, sums).T
+    at = v_at + kv_own - 256
+    for row, ref in zip((0, at, at + 1, at + 2), gain_refs):
+        ref[...] = gains[row : row + 1, : ref.shape[1]]
+
+
+def own_shards(parts, w_query, w_key, w_value, attn_gain, q_own, kv_own, gain_own):
     shard, q_all = w_query.shape
     return pl.pallas_call(
         functools.partial(shards_kernel, q_own=q_own, kv_own=kv_own),
@@ -650,7 +664,10 @@
             shape(shard, w_key.shape[1], dtype=F32),
             shape(shard, w_value.shape[1], dtype=F32),
             shape(shard, q_all, dtype=F32),
-            shape(128, shard, dtype=F32),
+            shape(1, shard, dtype=F32),
+            shape(1, gain_own, dtype=F32),
+            shape(1, gain_own, dtype=F32),
+            shape(1, shard, dtype=F32),
         ),
         compiler_params=pltpu.CompilerParams(vmem_limit_bytes=VMEM),
         cost_estimate=cost(1),
@@ -777,7 +794,8 @@
     x_hi = lax.axis_index("fsdp") // 2 % 2
     pick = functools.partial(lax.dynamic_index_in_dim, axis=0, keepdims=False)
     held = sum(pair.astype(F32) for pair in pairs)
-    return pick(held, x_hi), pick(held, 1 - x_hi).astype(pairs[0].dtype)
+    got = swap(pick(held, 1 - x_hi).astype(pairs[0].dtype), 2)
+    return pick(held, x_hi) + got.astype(F32)
 
 
 def pair(mine, other, low):
@@ -914,33 +932,33 @@
         return parts, far
 
     branch, grad_middle, grad_att, grad_mlp_g, middle = middle_back(
-        here, backs, middle_parts, out_grad[0], gain_rows, mlp_full
+        backs, middle_parts, out_grad[0], gain_rows, mlp_full
     )
     grad_heads = exchange(grad_att.reshape(n_seq, q_own, local))
-    mine, got, out_parts, branch = after((mine, got, out_parts, branch))
-    chip_sums = core_sums(mine, got)
+    out_mine, out_other = out_grads(core, branch, att_own, shard)
+    out_core = core_sums(out_mine, swap(out_other, 1))
+    out_parts, branch = after((out_parts, branch))
     out = pairs_for(jnp.concatenate(out_parts, axis=1))
-    out, grad_heads, chip_sums = after((out, grad_heads, chip_sums))
-    mlp_sums, mlp_far = sum_fsdp(chip_sums)
+    out, grad_heads, out_core = after((out, grad_heads, out_core))
+    out_sums, out_far = sum_fsdp(out_core)
 
     out_pairs = (out[0], *near_of(out), step_seq(out[3], STEPS[3]))
     gt, *back, gain_grads = attend_backward(
         here, qt, kt, vt, raw, lse, pos, grad_heads, gains, freq, head_full
     )
-    head_mine, head_other = head_grads(
-        core, gt, normed, gain_grads, grad_mlp_g, branch, att_own, gain_own, shard
-    )
-    back, head_mine, head_other, out_pairs = after((back, head_mine, head_other, out_pairs))
+    qkv_mine, qkv_other = qkv_grads(core, gt, normed, gain_grads, grad_mlp_g, gain_own, shard)
+    mine, got, qkv_mine = after((mine, got, qkv_mine))
+    chip_sums = core_sums(mine, got)
+    back, qkv_other, chip_sums, out_pairs = after((back, qkv_other, chip_sums, out_pairs))
+    mlp_sums, mlp_far = sum_fsdp(chip_sums)
     back_pairs = (back[0], *near_of(back), step_seq(back[3], STEPS[3]))
-    z_pairs = along_z(core_sums(head_mine, swap(head_other, 1)))
+    z_pairs = along_z(core_sums(qkv_mine, swap(qkv_other, 1)))
+    out_owned = exchange(out_blocks(x_hi, out_sums, swap(out_far, 2), n_seq))
+    z_pairs, out_owned = after((z_pairs, out_owned))
+    att_owned = jnp.concatenate([sum_z(z_pairs), total_of(out_owned)], axis=1).astype(BF16)
+    att_owned, back_pairs, mlp_far = after((att_owned, back_pairs, mlp_far))
     mlp_got = swap(mlp_far, 2)
-    z_pairs, back_pairs, mlp_got = after((z_pairs, back_pairs, mlp_got))
-    head_own, head_far = sum_z(z_pairs)
-    qkv_owned, out_blocks_own = out_blocks(
-        head_own, swap(head_far, 2), n_seq, qkv_own + HEAD
-    )
-    out_owned = total_of(exchange(out_blocks_own)).astype(BF16)
-    att_owned = jnp.concatenate([qkv_owned, out_owned], axis=1)
+    att_seq = to_all(att_owned)
     grad_normed = sum_pairs(back_pairs)
     layer_out = (middle + sum_pairs(out_pairs)).astype(BF16)
     xf = x.astype(F32)
@@ -953,22 +971,21 @@
     )
 
     mlp_owned = mlp_shards(x_hi, mlp_sums, mlp_got, hidden_own)
-    att_seq, (gw_gate, gw_up, gw_down) = after((to_all(att_owned), mlp_owned))
-    gw_query, gw_key, gw_value, gw_out, gain_sums = own_shards(
-        att_seq, w_query, w_key, w_value, attn_gain[:, None], q_own, kv_own
-    )
-    at = qkv_own - 256
+    att_seq, (gw_gate, gw_up, gw_down) = after((att_seq, mlp_owned))
+    gw_query, gw_key, gw_value, gw_out, g_attn, g_query, g_key, g_mlp = own_shards(
+        att_seq, w_query, w_key, w_value, attn_gain[:, None], q_own, kv_own, gain_own
+    )
     return (
         layer_out[None],
         grad_tokens[None],
-        gain_sums[0],
+        g_attn[0],
         gw_query,
         gw_key,
         gw_value,
-        gain_sums[at, :gain_own],
-        gain_sums[at + 1, :gain_own],
+        g_query[0],
+        g_key[0],
         gw_out.T,
-        gain_sums[at + 2],
+        g_mlp[0],
         gw_gate,
         gw_up,
         gw_down.T,

time: 382 us -> 379 us (level)
  waiting for transfers between devices: 121 us -> 104 us
  starting transfers between devices: 78.6 us -> 85.1 us
  Pallas kernels: 119 us -> 123 us
    ppermute x25, waiting for transfers between devices: 71 us -> 50.6 us  [step_seq(): return lax.ppermute(block, 'seq', to)]
    all_to_all x4, waiting for transfers between devices: 13 us -> 22.5 us  [exchange(): return lax.all_to_all(blocks, 'seq', 0, 0, tiled=True)]
    all_to_all x2, waiting for transfers between devices: 8.81 us -> 0.41 us  [to_all(): lax.all_to_all(jnp.broadcast_to(block[None], (n,) + block.shape), 'seq',...]
    ppermute x6 -> x8, waiting for transfers between devices: 12.3 us -> 16.3 us  [swap(): return lax.ppermute(held, 'fsdp', [(i, i ^ bit) for i in range(n)])]
    unnamed x74 -> x80, local copies, waits for them, and re-layouts: 7.85 us -> 10.8 us
    pallas_call x2 -> x3, Pallas kernels: 11 us -> 13.9 us  [core_sums(): pl.pallas_call(core_sums_kernel, grid=(mine.shape[0] // 2,), in_specs=[sp...]
    ppermute x6 -> x8, starting transfers between devices: 6.58 us -> 8.39 us  [swap(): return lax.ppermute(held, 'fsdp', [(i, i ^ bit) for i in range(n)])]
    pallas_call x3 -> x4, Pallas kernels: 17 us -> 18.1 us  [the longest x1 6.13 us: middle_back(): pl.pallas_call(functools.partial(middle_kernel, width=width), in_specs=vm...]
  transfers between devices with their start and end apart: 45 -> 48, of which waited for: 23 -> 23; matrix products, arithmetic and copies ran while one was open for 7% -> 8% of each run, Pallas kernels for 31% -> 29%
where the time goes in v4:
time: 379 us; the launch traced here: 371 us
  Pallas kernels  123 us (32%)
  waiting for transfers between devices  104 us (27%)
  starting transfers between devices  85.1 us (22%)
  local copies, waits for them, and re-layouts  25.7 us (7%)
  other arithmetic  18.5 us (5%)
  between operations  14.7 us (4%)
    ppermute x25, waiting for transfers between devices, step_seq(): return lax.ppermute(block, 'seq', to)  50.6 us
    ppermute x25, starting transfers between devices, step_seq(): return lax.ppermute(block, 'seq', to)  40.6 us
    pallas_call x2, Pallas kernels, mlp(): pl.pallas_call(functools.partial(mlp_kernel, pieces=len(att), width=width...  39.9 us
    all_to_all x4, waiting for transfers between devices, exchange(): return lax.all_to_all(blocks, 'seq', 0, 0, tiled=True)  22.5 us
    pallas_call x1, Pallas kernels, mlp_grads(): pl.pallas_call(functools.partial(mlp_grads_kernel, shard=shard), grid=(wi...  17.6 us
    all_to_all x4, starting transfers between devices, exchange(): return lax.all_to_all(blocks, 'seq', 0, 0, tiled=True)  16.7 us
    ppermute x8, waiting for transfers between devices, swap(): return lax.ppermute(held, 'fsdp', [(i, i ^ bit) for i in range(n)])  16.3 us
    pallas_call x3, Pallas kernels, core_sums(): pl.pallas_call(core_sums_kernel, grid=(mine.shape[0] // 2,), in_specs=[sp...  13.9 us
  transfers between devices with their start and end apart: 48, of which 23 were waited for; matrix products, arithmetic and copies ran while one was open for 8% of the time, Pallas kernels for 29%

profile of v4, /device:TPU:0, one launch (start us, length us, event | category | flops | bytes accessed | tf_op | source)
XLA Modules:
  0.0 371.4 jit_solution(15052667533542569009)
XLA Ops:
  19.9 5.3 %collective-permute-done.10 = bf16[1,96,384]{2,1,0:T(8,128)(2,1)S(1)} collective-permute-done((bf16[1,96,384]{2,1,0:T(8,128)(2,1)S(1)}, bf16[1,96,384]{2,1,0:T(8,128)(2,1)S(1)}, u32[]{:S(2)}, u32[]{:S(2)}) %collective-permute-start.10) | collective-permute-done | bytes 73760 | tf_op jit(solution)/shard_map/ppermute | solution.py:781
  31.7 3.0 collective-permute-start.7
  34.8 4.9 %collective-permute-done.4.refs_4_ = bf16[128,1664]{1,0:T(8,128)(2,1)S(1)} collective-permute-done((bf16[128,1664]{1,0:T(8,128)(2,1)}, bf16[128,1664]{1,0:T(8,128)(2,1)S(1)}, u32[]{:S(2)}, u32[]{:S(2)}) %collective-permute-start.4) | collective-permute-done | bytes 426016 | tf_op jit(solution)/shard_map/ppermute | solution.py:716
  41.7 3.9 %collective-permute-start.13 = (bf16[1,4,96,384]{3,2,1,0:T(8,128)(2,1)S(1)}, bf16[1,4,96,384]{3,2,1,0:T(8,128)(2,1)S(1)}, u32[]{:S(2)}, u32[]{:S(2)}) collective-permute-start(bf16[1,4,96,384]{3,2,1,0:T(8,128)(2,1)S(1)} %bitcast.114), channel_id=1, source_target_pairs={{0,8},{1,9},{2,10},{3,11},{4,12},{5,13},{6,14},{7,15},{8,0},{9,1},... | collective-permute-start | bytes 884744 | tf_op jit(solution)/shard_map/ppermute | solution.py:820
  58.4 4.3 %collective-permute-done.13 = bf16[1,4,96,384]{3,2,1,0:T(8,128)(2,1)S(1)} collective-permute-done((bf16[1,4,96,384]{3,2,1,0:T(8,128)(2,1)S(1)}, bf16[1,4,96,384]{3,2,1,0:T(8,128)(2,1)S(1)}, u32[]{:S(2)}, u32[]{:S(2)}) %collective-permute-start.13) | collective-permute-done | bytes 294944 | tf_op jit(solution)/shard_map/ppermute | solution.py:820
  63.9 11.3 %attend_forward.1 = (bf16[1024,1536]{1,0:T(8,128)(2,1)}, bf16[1024,1536]{1,0:T(8,128)(2,1)}, f32[256,1024]{1,0:T(8,128)}, bf16[192,1024]{1,0:T(8,128)(2,1)}, bf1...) custom-call(s32[1]{0:T(128)} %bitcast.1.me_ref, ...), custom_call_target="tpu_custom_call" | custom-call | flops 115000000 | bytes 1024 | tf_op jit(solution)/shard_map/attend_forward/pallas_call | solution.py:177
  78.0 17.0 %collective-permute-done.15 = bf16[2,192,512]{2,1,0:T(8,128)(2,1)S(1)} collective-permute-done((bf16[2,192,512]{2,1,0:T(8,128)(2,1)}, bf16[2,192,512]{2,1,0:T(8,128)(2,1)S(1)}, u32[]{:S(2)}, u32[]{:S(2)}) %collective-permute-start.15) | collective-permute-done | bytes 393248 | tf_op jit(solution)/shard_map/ppermute | solution.py:716
  99.6 7.9 %collective-permute-done.19.refs_1_ = bf16[2,192,512]{2,1,0:T(8,128)(2,1)S(1)} collective-permute-done((bf16[2,192,512]{2,1,0:T(8,128)(2,1)S(1)}, bf16[2,192,512]{2,1,0:T(8,128)(2,1)S(1)}, u32[]{:S(2)}, u32[]{:S(2)}) %collective-permute-start.19) | collective-permute-done | bytes 393248 | tf_op jit(solution)/shard_map/ppermute | solution.py:716
  107.5 5.1 %collective-permute-done.20.refs_2_ = bf16[2,192,512]{2,1,0:T(8,128)(2,1)S(1)} collective-permute-done((bf16[2,192,512]{2,1,0:T(8,128)(2,1)S(1)}, bf16[2,192,512]{2,1,0:T(8,128)(2,1)S(1)}, u32[]{:S(2)}, u32[]{:S(2)}) %collective-permute-start.20) | collective-permute-done | bytes 393248 | tf_op jit(solution)/shard_map/ppermute | solution.py:716
  115.4 5.1 %all-to-all-start = ((bf16[8,192,512]{2,1,0:T(8,128)(2,1)}), bf16[8,192,512]{2,1,0:T(8,128)(2,1)S(1)}, u32[]{:S(2)}, u32[]{:S(2)}) async-start(bf16[8,192,512]{2,1,0:T(8,128)(2,1)} %broadcast_in_dim.45), calls=%async_computation | async-start | bytes 3145728 | tf_op jit(solution)/shard_map/all_to_all | solution.py:702
  120.4 3.7 in_order.1.refs_5_.refs_2_.refs_3_
  124.1 5.4 %all-gather.2.cloned.1.call-done.refs_7_.refs_4_.w_ref = bf16[1536,4224]{1,0:T(8,128)(2,1)} async-done(((bf16[96,4224]{1,0:T(8,128)(2,1)}), bf16[1536,4224]{1,0:T(8,128)(2,1)}) %all-gather.2.cloned.1.call-update) | async-done | bytes 12976144 | tf_op jit(solution)/shard_map/all_gather | solution.py:878
  129.5 20.1 %mlp_part.2 = (f32[64,1536]{1,0:T(8,128)}, bf16[512,1536]{1,0:T(8,128)(2,1)}, bf16[512,896]{1,0:T(8,128)(2,1)}, bf16[512,896]{1,0:T(8,128)(2,1)}, bf16[512,896]{...) custom-call(s32[1]{0:T(128)} %bitcast.1.me_ref, ...), custom_call_target="tpu_custom_call" | custom-call | flops 1150000000 | bytes 1024 | tf_op jit(solution)/shard_map/mlp_part/pallas_call | solution.py:398
  150.8 4.8 %all-to-all-start.1 = ((bf16[8,64,1536]{2,1,0:T(8,128)(2,1)}), bf16[8,64,1536]{2,1,0:T(8,128)(2,1)S(1)}, u32[]{:S(2)}, u32[]{:S(2)}) async-start(bf16[8,64,1536]{2,1,0:T(8,128)(2,1)} %get-tuple-element.172), calls=%async_computation.1 | async-start | bytes 3145728 | tf_op jit(solution)/shard_map/all_to_all | solution.py:706
  155.6 19.9 %mlp_part.3 = (f32[64,1536]{1,0:T(8,128)}, bf16[512,1536]{1,0:T(8,128)(2,1)}, bf16[512,896]{1,0:T(8,128)(2,1)}, bf16[512,896]{1,0:T(8,128)(2,1)}, bf16[512,896]{...) custom-call(s32[1]{0:T(128)} %bitcast.1.me_ref, ...), custom_call_target="tpu_custom_call" | custom-call | flops 1150000000 | bytes 1024 | tf_op jit(solution)/shard_map/mlp_part/pallas_call | solution.py:398
  178.5 4.4 %all-to-all-start.2 = ((bf16[8,64,1536]{2,1,0:T(8,128)(2,1)}), bf16[8,64,1536]{2,1,0:T(8,128)(2,1)S(1)}, u32[]{:S(2)}, u32[]{:S(2)}) async-start(bf16[8,64,1536]{2,1,0:T(8,128)(2,1)} %get-tuple-element.188), calls=%async_computation.2 | async-start | bytes 3145728 | tf_op jit(solution)/shard_map/all_to_all | solution.py:706
  182.9 17.6 %mlp_grads.1 = (bf16[8,96,2688]{2,1,0:T(8,128)(2,1)}, bf16[8,96,2688]{2,1,0:T(8,128)(2,1)}) custom-call(s32[1]{0:T(128)} %bitcast.core_ref, bf16[512,1536]{1,0:T(8,128)(2,1)} %get-tuple-element.175.refs_0_, bf16[512,1536]{1,0:T(8,128)(2,1)} %get-tuple-element.177.refs_1_, bf16[8,128,1536]{2,1,0:T(8,128)(2,1)} %in_order.1.refs_5_.refs_2_.refs_3_, ...), custom_call_target="tpu_custom_call" | custom-call | flops 115000000 | bytes 1024 | tf_op jit(solution)/shard_map/mlp_grads/pallas_call | solution.py:478
  200.5 3.6 all-to-all-done.2.back1_ref
  205.2 6.1 %middle_back.1 = (bf16[128,1536]{1,0:T(8,128)(2,1)}, f32[128,1536]{1,0:T(8,128)}, bf16[1536,128]{1,0:T(8,128)(2,1)}, f32[1,1536]{1,0:T(1,128)}, f32[128,1536]{1,0:T(8,128)}) custom-call(bf16[8,64,1536]{2,1,0:T(8,128)(2,1)} %copy-done.1, bf16[8,64,1536]{2,1,0:T(8,128)(2,1)} %copy-done.3, f32[64,1536]{1,0:T(8,128)} %get-tuple-element.191.mid0_ref, ...), custom_call_target="tpu_custom_call" | custom-call | flops 115000000 | bytes 1024 | tf_op jit(solution)/shard_map/middle_back/pallas_call | solution.py:539
  211.3 5.3 %out_grads.1 = (bf16[8,96,1536]{2,1,0:T(8,128)(2,1)}, bf16[8,96,1536]{2,1,0:T(8,128)(2,1)}) custom-call(s32[1]{0:T(128)} %bitcast.core_ref, bf16[128,1536]{1,0:T(8,128)(2,1)} %get-tuple-element.202.branch_ref, bf16[1536,64]{1,0:T(8,128)(2,1)} %get-tuple-element.206.refs_0_, bf16[1536,64]{1,0:T(8,128)(2,1)} %get-tuple-element.207.refs_1_), custom_call_target="tpu_custom_call" | custom-call | flops 115000000 | bytes 1024 | tf_op jit(solution)/shard_map/out_grads/pallas_call | solution.py:604
  216.7 4.1 %all-to-all-start.3 = ((bf16[8,192,128]{2,1,0:T(8,128)(2,1)}), bf16[8,192,128]{2,1,0:T(8,128)(2,1)}, u32[]{:S(2)}, u32[]{:S(2)}) async-start(bf16[8,192,128]{2,1,0:T(8,128)(2,1)} %bitcast.117), calls=%async_computation.3 | async-start | bytes 786432 | tf_op jit(solution)/shard_map/all_to_all | solution.py:706
  226.4 4.5 %core_sums.3 = bf16[8,96,1536]{2,1,0:T(8,128)(2,1)} custom-call(bf16[8,96,1536]{2,1,0:T(8,128)(2,1)} %get-tuple-element.208.mine_ref, bf16[8,96,1536]{2,1,0:T(8,128)(2,1)} %copy-done.7), custom_call_target="tpu_custom_call" | custom-call | flops 115000000 | bytes 1024 | tf_op jit(solution)/shard_map/core_sums/pallas_call | solution.py:499
  237.1 13.6 %attend_backward.1 = (bf16[320,1024]{1,0:T(8,128)(2,1)}, bf16[2,128,1536]{2,1,0:T(8,128)(2,1)}, bf16[2,128,1536]{2,1,0:T(8,128)(2,1)}, bf16[2,128,1536]{2,1,0:T(...) custom-call(s32[1]{0:T(128)} %bitcast.1.me_ref, bf16[192,1024]{1,0:T(8,128)(2,1)} %get-tuple-element.194.qt_ref, ...), custom_call_target="tpu_custom_call" | custom-call | flops 115000000 | bytes 1024 | tf_op jit(solution)/shard_map/attend_backward/pallas_call | solution.py:289
  250.7 4.6 %qkv_grads.1 = (bf16[8,96,384]{2,1,0:T(8,128)(2,1)}, bf16[8,96,384]{2,1,0:T(8,128)(2,1)}) custom-call(s32[1]{0:T(128)} %bitcast.core_ref, bf16[320,1024]{1,0:T(8,128)(2,1)} %get-tuple-element.216.gt_ref, bf16[1024,1536]{1,0:T(8,128)(2,1)} %get-tuple-element.217.normed_ref, f32[64,128]{1,0:T(8,128)} %get-tuple-element.218.gains_ref, ...), custom_call_target="tpu_custom_call" | custom-call | flops 115000000 | bytes 1024 | tf_op jit(solution)/shard_map/qkv_grads/pallas_call | solution.py:584
  257.4 6.0 %core_sums.4 = bf16[8,96,2688]{2,1,0:T(8,128)(2,1)} custom-call(bf16[8,96,2688]{2,1,0:T(8,128)(2,1)} %get-tuple-element.224.mine_ref, bf16[8,96,2688]{2,1,0:T(8,128)(2,1)} %copy-done.4), custom_call_target="tpu_custom_call" | custom-call | flops 115000000 | bytes 1024 | tf_op jit(solution)/shard_map/core_sums/pallas_call | solution.py:499
  263.4 5.4 %collective-permute-done.24 = bf16[2,128,1536]{2,1,0:T(8,128)(2,1)S(1)} collective-permute-done((bf16[2,128,1536]{2,1,0:T(8,128)(2,1)}, bf16[2,128,1536]{2,1,0:T(8,128)(2,1)S(1)}, u32[]{:S(2)}, u32[]{:S(2)}) %collective-permute-start.24) | collective-permute-done | bytes 786464 | tf_op jit(solution)/shard_map/ppermute | solution.py:716
  268.8 3.3 collective-permute-done.25
  279.5 3.4 core_sums.5
  290.8 3.5 all-to-all-start.4
  302.8 17.1 %all-to-all-done.4 = bf16[8,96,192]{2,1,0:T(8,128)(2,1)S(1)} async-done(((bf16[8,96,192]{2,1,0:T(8,128)(2,1)}), bf16[8,96,192]{2,1,0:T(8,128)(2,1)S(1)}, u32[]{:S(2)}, u32[]{:S(2)}) %all-to-all-start.4) | async-done | bytes 294944 | tf_op jit(solution)/shard_map/all_to_all | solution.py:706
  339.2 3.6 all-to-all-start.5
  348.6 9.0 %collective-permute-done.38.got_ref = bf16[96,2688]{1,0:T(8,128)(2,1)S(1)} collective-permute-done((bf16[96,2688]{1,0:T(8,128)(2,1)}, bf16[96,2688]{1,0:T(8,128)(2,1)S(1)}, u32[]{:S(2)}, u32[]{:S(2)}) %collective-permute-start.38) | collective-permute-done | bytes 516128 | tf_op jit(solution)/shard_map/ppermute | solution.py:781
  (216 shorter events, 120.2 us)
Async XLA Ops:
  7.2 122.3 %all-gather.2.cloned.1.call-start = ((), (), s32[]{:S(2)}) async-start(), calls=%async_computation.8 | async-start | bytes 13787136 | tf_op jit(solution)/shard_map/all_gather | solution.py:878
  9.7 15.6 %collective-permute-start.1 = (bf16[128,1664]{1,0:T(8,128)(2,1)S(1)}, bf16[128,1664]{1,0:T(8,128)(2,1)}, u32[]{:S(2)}, u32[]{:S(2)}) collective-permute-start(bf16[128,1664]{1,0:T(8,128)(2,1)S(1)} %fusion.19.refs_0_), channel_id=1, source_target_pairs={{0,16},{16,0},{32,48},{48,32},{64,80},{80,64},{96,112},{112,96},{1... | collective-permute-start | bytes 1277960 | tf_op jit(solution)/shard_map/ppermute | solution.py:716
  25.4 20.2 %collective-permute-start = (bf16[128,1536]{1,0:T(8,128)(2,1)S(1)}, bf16[128,1536]{1,0:T(8,128)(2,1)}, u32[]{:S(2)}, u32[]{:S(2)}) collective-permute-start(bf16[128,1536]{1,0:T(8,128)(2,1)S(1)} %bitcast.111), channel_id=1, source_target_pairs={{0,16},{16,0},{32,48},{48,32},{64,80},{80,64},{96,112},{112,96},{1... | collective-permute-start | bytes 1179656 | tf_op jit(solution)/shard_map/ppermute | solution.py:716
  25.7 14.1 %collective-permute-start.4 = (bf16[128,1664]{1,0:T(8,128)(2,1)}, bf16[128,1664]{1,0:T(8,128)(2,1)S(1)}, u32[]{:S(2)}, u32[]{:S(2)}) collective-permute-start(bf16[128,1664]{1,0:T(8,128)(2,1)} %collective-permute-done.1.refs_1_), channel_id=1, source_target_pairs={{0,32},{16,48},{32,64},{48,80},{64,96},{80,112},{96,0},{112,16},{1... | collective-permute-start | bytes 1277960 | tf_op jit(solution)/shard_map/ppermute | solution.py:716
  31.3 14.9 %collective-permute-start.6 = (bf16[64,1664]{1,0:T(8,128)(2,1)S(1)}, bf16[64,1664]{1,0:T(8,128)(2,1)S(1)}, u32[]{:S(2)}, u32[]{:S(2)}) collective-permute-start(bf16[64,1664]{1,0:T(8,128)(2,1)S(1)} %slice.50), channel_id=1, source_target_pairs={{0,32},{16,48},{32,64},{48,80},{64,96},{80,112},{96,0},{112,16},{1... | collective-permute-start | bytes 638984 | tf_op jit(solution)/shard_map/ppermute | solution.py:716
  31.7 18.3 %collective-permute-start.7 = (bf16[64,1664]{1,0:T(8,128)(2,1)S(1)}, bf16[64,1664]{1,0:T(8,128)(2,1)S(1)}, u32[]{:S(2)}, u32[]{:S(2)}) collective-permute-start(bf16[64,1664]{1,0:T(8,128)(2,1)S(1)} %slice.51), channel_id=1, source_target_pairs={{0,96},{16,112},{32,0},{48,16},{64,32},{80,48},{96,64},{112,80},{1... | collective-permute-start | bytes 638984 | tf_op jit(solution)/shard_map/ppermute | solution.py:716
  39.7 17.2 %collective-permute-start.12 = (bf16[1,4,96,384]{3,2,1,0:T(8,128)(2,1)S(1)}, bf16[1,4,96,384]{3,2,1,0:T(8,128)(2,1)S(1)}, u32[]{:S(2)}, u32[]{:S(2)}) collective-permute-start(bf16[1,4,96,384]{3,2,1,0:T(8,128)(2,1)S(1)} %bitcast.113), channel_id=1, source_target_pairs={{0,4},{1,5},{2,6},{3,7},{4,8},{5,9},{6,10},{7,11},{8,12},{9,13},{1... | collective-permute-start | bytes 884744 | tf_op jit(solution)/shard_map/ppermute | solution.py:820
  41.7 21.0 %collective-permute-start.13 = (bf16[1,4,96,384]{3,2,1,0:T(8,128)(2,1)S(1)}, bf16[1,4,96,384]{3,2,1,0:T(8,128)(2,1)S(1)}, u32[]{:S(2)}, u32[]{:S(2)}) collective-permute-start(bf16[1,4,96,384]{3,2,1,0:T(8,128)(2,1)S(1)} %bitcast.114), channel_id=1, source_target_pairs={{0,8},{1,9},{2,10},{3,11},{4,12},{5,13},{6,14},{7,15},{8,0},{9,1},... | collective-permute-start | bytes 884744 | tf_op jit(solution)/shard_map/ppermute | solution.py:820
  52.7 42.3 %collective-permute-start.16 = (bf16[2,128,1536]{2,1,0:T(8,128)(2,1)S(1)}, bf16[2,128,1536]{2,1,0:T(8,128)(2,1)S(1)}, u32[]{:S(2)}, u32[]{:S(2)}) collective-permute-start(bf16[2,128,1536]{2,1,0:T(8,128)(2,1)S(1)} %pad_maximum_fusion.1.refs_0_), channel_id=1, source_target_pairs={{0,32},{16,48},{32,64},{48,80},{64,96},{80,112},{96,0},{112,16},{1... | collective-permute-start | bytes 2359304 | tf_op jit(solution)/shard_map/ppermute | solution.py:716
  53.8 41.3 %collective-permute-start.17 = (bf16[2,128,1536]{2,1,0:T(8,128)(2,1)S(1)}, bf16[2,128,1536]{2,1,0:T(8,128)(2,1)S(1)}, u32[]{:S(2)}, u32[]{:S(2)}) collective-permute-start(bf16[2,128,1536]{2,1,0:T(8,128)(2,1)S(1)} %pad_maximum_fusion.1.refs_0_), channel_id=1, source_target_pairs={{0,96},{16,112},{32,0},{48,16},{64,32},{80,48},{96,64},{112,80},{1... | collective-permute-start | bytes 2359304 | tf_op jit(solution)/shard_map/ppermute | solution.py:716
  57.0 38.1 %collective-permute-start.18 = (bf16[2,128,1536]{2,1,0:T(8,128)(2,1)S(1)}, bf16[2,128,1536]{2,1,0:T(8,128)(2,1)S(1)}, u32[]{:S(2)}, u32[]{:S(2)}) collective-permute-start(bf16[2,128,1536]{2,1,0:T(8,128)(2,1)S(1)} %pad_maximum_fusion.1.refs_0_), channel_id=1, source_target_pairs={{0,64},{16,80},{32,96},{48,112},{64,0},{80,16},{96,32},{112,48},{1... | collective-permute-start | bytes 2359304 | tf_op jit(solution)/shard_map/ppermute | solution.py:716
  75.2 19.8 %collective-permute-start.15 = (bf16[2,192,512]{2,1,0:T(8,128)(2,1)}, bf16[2,192,512]{2,1,0:T(8,128)(2,1)S(1)}, u32[]{:S(2)}, u32[]{:S(2)}) collective-permute-start(bf16[2,192,512]{2,1,0:T(8,128)(2,1)} %get-tuple-element.153), channel_id=1, source_target_pairs={{0,16},{16,0},{32,48},{48,32},{64,80},{80,64},{96,112},{112,96},{1... | collective-permute-start | bytes 1179656 | tf_op jit(solution)/shard_map/ppermute | solution.py:716
  96.1 16.6 %collective-permute-start.20 = (bf16[2,192,512]{2,1,0:T(8,128)(2,1)S(1)}, bf16[2,192,512]{2,1,0:T(8,128)(2,1)S(1)}, u32[]{:S(2)}, u32[]{:S(2)}) collective-permute-start(bf16[2,192,512]{2,1,0:T(8,128)(2,1)S(1)} %pad_maximum_fusion.2.refs_0_), channel_id=1, source_target_pairs={{0,96},{16,112},{32,0},{48,16},{64,32},{80,48},{96,64},{112,80},{1... | collective-permute-start | bytes 1179656 | tf_op jit(solution)/shard_map/ppermute | solution.py:716
  98.4 15.6 %collective-permute-start.21 = (bf16[2,192,512]{2,1,0:T(8,128)(2,1)S(1)}, bf16[2,192,512]{2,1,0:T(8,128)(2,1)S(1)}, u32[]{:S(2)}, u32[]{:S(2)}) collective-permute-start(bf16[2,192,512]{2,1,0:T(8,128)(2,1)S(1)} %pad_maximum_fusion.2.refs_0_), channel_id=1, source_target_pairs={{0,64},{16,80},{32,96},{48,112},{64,0},{80,16},{96,32},{112,48},{1... | collective-permute-start | bytes 1179656 | tf_op jit(solution)/shard_map/ppermute | solution.py:716
  115.4 34.2 %all-to-all-start = ((bf16[8,192,512]{2,1,0:T(8,128)(2,1)}), bf16[8,192,512]{2,1,0:T(8,128)(2,1)S(1)}, u32[]{:S(2)}, u32[]{:S(2)}) async-start(bf16[8,192,512]{2,1,0:T(8,128)(2,1)} %broadcast_in_dim.45), calls=%async_computation | async-start | bytes 3145728 | tf_op jit(solution)/shard_map/all_to_all | solution.py:702
  150.8 26.6 %all-to-all-start.1 = ((bf16[8,64,1536]{2,1,0:T(8,128)(2,1)}), bf16[8,64,1536]{2,1,0:T(8,128)(2,1)S(1)}, u32[]{:S(2)}, u32[]{:S(2)}) async-start(bf16[8,64,1536]{2,1,0:T(8,128)(2,1)} %get-tuple-element.172), calls=%async_computation.1 | async-start | bytes 3145728 | tf_op jit(solution)/shard_map/all_to_all | solution.py:706
  178.5 25.6 %all-to-all-start.2 = ((bf16[8,64,1536]{2,1,0:T(8,128)(2,1)}), bf16[8,64,1536]{2,1,0:T(8,128)(2,1)S(1)}, u32[]{:S(2)}, u32[]{:S(2)}) async-start(bf16[8,64,1536]{2,1,0:T(8,128)(2,1)} %get-tuple-element.188), calls=%async_computation.2 | async-start | bytes 3145728 | tf_op jit(solution)/shard_map/all_to_all | solution.py:706
  216.7 14.2 %all-to-all-start.3 = ((bf16[8,192,128]{2,1,0:T(8,128)(2,1)}), bf16[8,192,128]{2,1,0:T(8,128)(2,1)}, u32[]{:S(2)}, u32[]{:S(2)}) async-start(bf16[8,192,128]{2,1,0:T(8,128)(2,1)} %bitcast.117), calls=%async_computation.3 | async-start | bytes 786432 | tf_op jit(solution)/shard_map/all_to_all | solution.py:706
  220.8 52.5 %reduce-scatter.3.cloned.1.call-start = ((), (), s32[]{:S(2)}) async-start(), calls=%async_computation.9 | async-start | bytes 2949120 | tf_op jit(solution)/shard_map/reduce_scatter | solution.py:924
  230.9 96.8 %reduce-scatter.5.cloned.1.call-start = ((), (), s32[]{:S(2)}) async-start(), calls=%async_computation.10 | async-start | bytes 5160960 | tf_op jit(solution)/shard_map/reduce_scatter | solution.py:924
  231.0 24.4 %collective-permute-start.23 = (bf16[8,96,2688]{2,1,0:T(8,128)(2,1)}, bf16[8,96,2688]{2,1,0:T(8,128)(2,1)S(1)}, u32[]{:S(2)}, u32[]{:S(2)}) collective-permute-start(bf16[8,96,2688]{2,1,0:T(8,128)(2,1)} %get-tuple-element.222), channel_id=1, source_target_pairs={{0,1},{1,0},{2,3},{3,2},{4,5},{5,4},{6,7},{7,6},{8,9},{9,8},{10,11... | collective-permute-start | bytes 12386312 | tf_op jit(solution)/shard_map/ppermute | solution.py:781
  231.6 37.2 %collective-permute-start.24 = (bf16[2,128,1536]{2,1,0:T(8,128)(2,1)}, bf16[2,128,1536]{2,1,0:T(8,128)(2,1)S(1)}, u32[]{:S(2)}, u32[]{:S(2)}) collective-permute-start(bf16[2,128,1536]{2,1,0:T(8,128)(2,1)} %get-tuple-element.227), channel_id=1, source_target_pairs={{0,96},{16,112},{32,0},{48,16},{64,32},{80,48},{96,64},{112,80},{1... | collective-permute-start | bytes 2359304 | tf_op jit(solution)/shard_map/ppermute | solution.py:716
  234.4 37.7 %collective-permute-start.25 = (bf16[2,128,1536]{2,1,0:T(8,128)(2,1)}, bf16[2,128,1536]{2,1,0:T(8,128)(2,1)S(1)}, u32[]{:S(2)}, u32[]{:S(2)}) collective-permute-start(bf16[2,128,1536]{2,1,0:T(8,128)(2,1)} %get-tuple-element.228), channel_id=1, source_target_pairs={{0,32},{16,48},{32,64},{48,80},{64,96},{80,112},{96,0},{112,16},{1... | collective-permute-start | bytes 2359304 | tf_op jit(solution)/shard_map/ppermute | solution.py:716
  234.4 37.7 %collective-permute-start.26 = (bf16[2,128,1536]{2,1,0:T(8,128)(2,1)}, bf16[2,128,1536]{2,1,0:T(8,128)(2,1)S(1)}, u32[]{:S(2)}, u32[]{:S(2)}) collective-permute-start(bf16[2,128,1536]{2,1,0:T(8,128)(2,1)} %get-tuple-element.229), channel_id=1, source_target_pairs={{0,64},{16,80},{32,96},{48,112},{64,0},{80,16},{96,32},{112,48},{1... | collective-permute-start | bytes 2359304 | tf_op jit(solution)/shard_map/ppermute | solution.py:716
  277.2 52.4 %collective-permute-start.34 = (bf16[2,128,1536]{2,1,0:T(8,128)(2,1)}, bf16[2,128,1536]{2,1,0:T(8,128)(2,1)}, u32[]{:S(2)}, u32[]{:S(2)}) collective-permute-start(bf16[2,128,1536]{2,1,0:T(8,128)(2,1)} %get-tuple-element.244), channel_id=1, source_target_pairs={{0,96},{16,112},{32,0},{48,16},{64,32},{80,48},{96,64},{112,80},{1... | collective-permute-start | bytes 2359304 | tf_op jit(solution)/shard_map/ppermute | solution.py:716
  278.0 51.6 %collective-permute-start.35 = (bf16[2,128,1536]{2,1,0:T(8,128)(2,1)}, bf16[2,128,1536]{2,1,0:T(8,128)(2,1)}, u32[]{:S(2)}, u32[]{:S(2)}) collective-permute-start(bf16[2,128,1536]{2,1,0:T(8,128)(2,1)} %get-tuple-element.245), channel_id=1, source_target_pairs={{0,32},{16,48},{32,64},{48,80},{64,96},{80,112},{96,0},{112,16},{1... | collective-permute-start | bytes 2359304 | tf_op jit(solution)/shard_map/ppermute | solution.py:716
  284.8 16.3 %collective-permute-start.30 = (bf16[2,96,384]{2,1,0:T(8,128)(2,1)}, bf16[2,96,384]{2,1,0:T(8,128)(2,1)}, u32[]{:S(2)}, u32[]{:S(2)}) collective-permute-start(bf16[2,96,384]{2,1,0:T(8,128)(2,1)} %get-tuple-element.276), channel_id=1, source_target_pairs={{0,8},{1,9},{2,10},{3,11},{4,12},{5,13},{6,14},{7,15},{8,0},{9,1},... | collective-permute-start | bytes 442376 | tf_op jit(solution)/shard_map/ppermute | solution.py:789
  287.1 15.7 %collective-permute-start.31 = (bf16[2,96,384]{2,1,0:T(8,128)(2,1)S(1)}, bf16[2,96,384]{2,1,0:T(8,128)(2,1)}, u32[]{:S(2)}, u32[]{:S(2)}) collective-permute-start(bf16[2,96,384]{2,1,0:T(8,128)(2,1)S(1)} %get-tuple-element.275), channel_id=1, source_target_pairs={{0,12},{1,13},{2,14},{3,15},{4,0},{5,1},{6,2},{7,3},{8,4},{9,5},{1... | collective-permute-start | bytes 442376 | tf_op jit(solution)/shard_map/ppermute | solution.py:789
  290.8 29.1 %all-to-all-start.4 = ((bf16[8,96,192]{2,1,0:T(8,128)(2,1)}), bf16[8,96,192]{2,1,0:T(8,128)(2,1)S(1)}, u32[]{:S(2)}, u32[]{:S(2)}) async-start(bf16[8,96,192]{2,1,0:T(8,128)(2,1)} %out_blocks.1), calls=%async_computation.5 | async-start | bytes 786432 | tf_op jit(solution)/shard_map/all_to_all | solution.py:706
  297.0 32.6 %collective-permute-start.36 = (bf16[2,128,1536]{2,1,0:T(8,128)(2,1)}, bf16[2,128,1536]{2,1,0:T(8,128)(2,1)}, u32[]{:S(2)}, u32[]{:S(2)}) collective-permute-start(bf16[2,128,1536]{2,1,0:T(8,128)(2,1)} %get-tuple-element.246), channel_id=1, source_target_pairs={{0,64},{16,80},{32,96},{48,112},{64,0},{80,16},{96,32},{112,48},{1... | collective-permute-start | bytes 2359304 | tf_op jit(solution)/shard_map/ppermute | solution.py:716
  335.5 22.1 %collective-permute-start.38 = (bf16[96,2688]{1,0:T(8,128)(2,1)}, bf16[96,2688]{1,0:T(8,128)(2,1)S(1)}, u32[]{:S(2)}, u32[]{:S(2)}) collective-permute-start(bf16[96,2688]{1,0:T(8,128)(2,1)} %dynamic-slice_bitcast_fusion.4), channel_id=1, source_target_pairs={{0,2},{1,3},{2,0},{3,1},{4,6},{5,7},{6,4},{7,5},{8,10},{9,11},{10,... | collective-permute-start | bytes 1548296 | tf_op jit(solution)/shard_map/ppermute | solution.py:781
  339.2 21.9 %all-to-all-start.5 = ((bf16[8,96,576]{2,1,0:T(8,128)(2,1)}), bf16[8,96,576]{2,1,0:T(8,128)(2,1)S(1)}, u32[]{:S(2)}, u32[]{:S(2)}) async-start(bf16[8,96,576]{2,1,0:T(8,128)(2,1)} %broadcast_in_dim.48), calls=%async_computation.7 | async-start | bytes 1966080 | tf_op jit(solution)/shard_map/all_to_all | solution.py:702
  (56 other events, 463.6 us)
Sparse Core Ops, SparseCore 0:
  10.5 118.9 all-gather.1
  231.0 30.8 reduce-scatter.2
  272.2 48.8 reduce-scatter.4

commit v5 on v4

--- a/solution.py
+++ b/solution.py
@@ -508,6 +508,35 @@
     )(mine, got)
 
 
+def core_halves_kernel(mine_ref, low_ref, high_ref, out_ref, *, steps):
+    def add(got_ref):
+        out_ref[...] = (mine_ref[...].astype(F32) + got_ref[...].astype(F32)).astype(BF16)
+
+    low = pl.program_id(0) < steps
+    pl.when(low)(functools.partial(add, low_ref))
+    pl.when(jnp.logical_not(low))(functools.partial(add, high_ref))
+
+
+def core_halves(mine, low, high):
+    steps = low.shape[0] // 2
+    block = (2,) + mine.shape[1:]
+    spec = pl.BlockSpec(block, lambda i: (i, 0, 0))
+    return pl.pallas_call(
+        functools.partial(core_halves_kernel, steps=steps),
+        grid=(2 * steps,),
+        in_specs=[
+            spec,
+            pl.BlockSpec(block, lambda i: (jnp.minimum(i, steps - 1), 0, 0)),
+            pl.BlockSpec(block, lambda i: (jnp.maximum(i - steps, 0), 0, 0)),
+        ],
+        out_specs=spec,
+        out_shape=shape(*mine.shape),
+        compiler_params=pltpu.CompilerParams(vmem_limit_bytes=VMEM),
+        cost_estimate=cost(0.1),
+        name="core_halves",
+    )(mine, low, high)
+
+
 def middle_kernel(
     back0_ref, back1_ref, mid0_ref, mid1_ref, g_ref, gain_ref, w_ref,
     branch_ref, grad_ref, att_ref, gain_grad_ref, mid_out_ref,
@@ -592,10 +621,12 @@
 
 
 def out_grads_kernel(core_ref, branch_ref, *refs, shard):
-    att_refs, (own_ref, other_ref) = refs[:-2], refs[-2:]
+    att_refs, (own_ref, low_ref, high_ref) = refs[:-3], refs[-3:]
     att = jnp.concatenate([ref[...] for ref in att_refs], axis=1)
     rows = dot(branch_ref[...], att, 0, 1).astype(BF16)
-    split_rows(core_ref, rows, shard, own_ref, other_ref)
+    half = low_ref.shape[0]
+    split_rows(core_ref, rows[: 2 * half * shard], shard, own_ref.at[:half], low_ref)
+    split_rows(core_ref, rows[2 * half * shard :], shard, own_ref.at[half:], high_ref)
 
 
 def out_grads(core, branch, atts, shard):
@@ -604,7 +635,11 @@
     return pl.pallas_call(
         functools.partial(out_grads_kernel, shard=shard),
         in_specs=[smem()] + vmem(1 + len(atts)),
-        out_shape=(shape(width // shard // 2, shard, heads),) * 2,
+        out_shape=(
+            shape(width // shard // 2, shard, heads),
+            shape(width // shard // 4, shard, heads),
+            shape(width // shard // 4, shard, heads),
+        ),
         compiler_params=pltpu.CompilerParams(vmem_limit_bytes=VMEM),
         cost_estimate=cost(0.1),
         name="out_grads",
@@ -935,8 +970,8 @@
         backs, middle_parts, out_grad[0], gain_rows, mlp_full
     )
     grad_heads = exchange(grad_att.reshape(n_seq, q_own, local))
-    out_mine, out_other = out_grads(core, branch, att_own, shard)
-    out_core = core_sums(out_mine, swap(out_other, 1))
+    out_mine, out_low, out_high = out_grads(core, branch, att_own, shard)
+    out_core = core_halves(out_mine, swap(out_low, 1), swap(out_high, 1))
     out_parts, branch = after((out_parts, branch))
     out = pairs_for(jnp.concatenate(out_parts, axis=1))
     out, grad_heads, out_core = after((out, grad_heads, out_core))

time: 379 us -> 378 us (level)
    pallas_call x0 -> x1, Pallas kernels: none -> 4.59 us  [core_halves(): pl.pallas_call(functools.partial(core_halves_kernel, steps=steps), grid=(...]
    pallas_call x3 -> x2, Pallas kernels: 13.9 us -> 9.53 us  [core_sums(): pl.pallas_call(core_sums_kernel, grid=(mine.shape[0] // 2,), in_specs=[sp...]
    unnamed x80 -> x82, local copies, waits for them, and re-layouts: 10.8 us -> 10.2 us
    ppermute x8 -> x9, starting transfers between devices: 8.39 us -> 8.4 us  [swap(): return lax.ppermute(held, 'fsdp', [(i, i ^ bit) for i in range(n)])]
    ppermute x8 -> x9, waiting for transfers between devices: 16.3 us -> 16.3 us  [swap(): return lax.ppermute(held, 'fsdp', [(i, i ^ bit) for i in range(n)])]
  transfers between devices with their start and end apart: 48 -> 49, of which waited for: 23 -> 23; matrix products, arithmetic and copies ran while one was open for 8% -> 8% of each run, Pallas kernels for 29% -> 29%
where the time goes in v5:
time: 378 us; the launch traced here: 371 us
  Pallas kernels  123 us (33%)
  waiting for transfers between devices  105 us (28%)
  starting transfers between devices  84.3 us (22%)
  local copies, waits for them, and re-layouts  25 us (7%)
  other arithmetic  18 us (5%)
  between operations  15 us (4%)
    ppermute x25, waiting for transfers between devices, step_seq(): return lax.ppermute(block, 'seq', to)  51.2 us
    ppermute x25, starting transfers between devices, step_seq(): return lax.ppermute(block, 'seq', to)  40.5 us
    pallas_call x2, Pallas kernels, mlp(): pl.pallas_call(functools.partial(mlp_kernel, pieces=len(att), width=width...  39.9 us
    all_to_all x4, waiting for transfers between devices, exchange(): return lax.all_to_all(blocks, 'seq', 0, 0, tiled=True)  22.5 us
    pallas_call x1, Pallas kernels, mlp_grads(): pl.pallas_call(functools.partial(mlp_grads_kernel, shard=shard), grid=(wi...  17.5 us
    ppermute x9, waiting for transfers between devices, swap(): return lax.ppermute(held, 'fsdp', [(i, i ^ bit) for i in range(n)])  16.3 us
    all_to_all x4, starting transfers between devices, exchange(): return lax.all_to_all(blocks, 'seq', 0, 0, tiled=True)  15.7 us
    pallas_call x1, Pallas kernels, attend_backward(): pl.pallas_call(functools.partial(backward_kernel, heads=heads, block=bloc...  13.3 us
  transfers between devices with their start and end apart: 49, of which 23 were waited for; matrix products, arithmetic and copies ran while one was open for 8% of the time, Pallas kernels for 29%

profile of v5, /device:TPU:0, one launch (start us, length us, event | category | flops | bytes accessed | tf_op | source)
XLA Modules:
  0.0 370.8 jit_solution(8859584024608005279)
XLA Ops:
  19.9 5.3 %collective-permute-done.10 = bf16[1,96,384]{2,1,0:T(8,128)(2,1)S(1)} collective-permute-done((bf16[1,96,384]{2,1,0:T(8,128)(2,1)S(1)}, bf16[1,96,384]{2,1,0:T(8,128)(2,1)S(1)}, u32[]{:S(2)}, u32[]{:S(2)}) %collective-permute-start.10) | collective-permute-done | bytes 73760 | tf_op jit(solution)/shard_map/ppermute | solution.py:816
  34.8 4.9 %collective-permute-done.4.refs_4_ = bf16[128,1664]{1,0:T(8,128)(2,1)S(1)} collective-permute-done((bf16[128,1664]{1,0:T(8,128)(2,1)}, bf16[128,1664]{1,0:T(8,128)(2,1)S(1)}, u32[]{:S(2)}, u32[]{:S(2)}) %collective-permute-start.4) | collective-permute-done | bytes 426016 | tf_op jit(solution)/shard_map/ppermute | solution.py:751
  41.7 3.9 %collective-permute-start.13 = (bf16[1,4,96,384]{3,2,1,0:T(8,128)(2,1)S(1)}, bf16[1,4,96,384]{3,2,1,0:T(8,128)(2,1)S(1)}, u32[]{:S(2)}, u32[]{:S(2)}) collective-permute-start(bf16[1,4,96,384]{3,2,1,0:T(8,128)(2,1)S(1)} %bitcast.114), channel_id=1, source_target_pairs={{0,8},{1,9},{2,10},{3,11},{4,12},{5,13},{6,14},{7,15},{8,0},{9,1},... | collective-permute-start | bytes 884744 | tf_op jit(solution)/shard_map/ppermute | solution.py:855
  58.1 4.6 %collective-permute-done.13 = bf16[1,4,96,384]{3,2,1,0:T(8,128)(2,1)S(1)} collective-permute-done((bf16[1,4,96,384]{3,2,1,0:T(8,128)(2,1)S(1)}, bf16[1,4,96,384]{3,2,1,0:T(8,128)(2,1)S(1)}, u32[]{:S(2)}, u32[]{:S(2)}) %collective-permute-start.13) | collective-permute-done | bytes 294944 | tf_op jit(solution)/shard_map/ppermute | solution.py:855
  63.9 11.3 %attend_forward.1 = (bf16[1024,1536]{1,0:T(8,128)(2,1)}, bf16[1024,1536]{1,0:T(8,128)(2,1)}, f32[256,1024]{1,0:T(8,128)}, bf16[192,1024]{1,0:T(8,128)(2,1)}, bf1...) custom-call(s32[1]{0:T(128)} %bitcast.1.me_ref, ...), custom_call_target="tpu_custom_call" | custom-call | flops 115000000 | bytes 1024 | tf_op jit(solution)/shard_map/attend_forward/pallas_call | solution.py:177
  78.0 17.0 %collective-permute-done.15 = bf16[2,192,512]{2,1,0:T(8,128)(2,1)S(1)} collective-permute-done((bf16[2,192,512]{2,1,0:T(8,128)(2,1)}, bf16[2,192,512]{2,1,0:T(8,128)(2,1)S(1)}, u32[]{:S(2)}, u32[]{:S(2)}) %collective-permute-start.15) | collective-permute-done | bytes 393248 | tf_op jit(solution)/shard_map/ppermute | solution.py:751
  99.6 7.9 %collective-permute-done.19.refs_1_ = bf16[2,192,512]{2,1,0:T(8,128)(2,1)S(1)} collective-permute-done((bf16[2,192,512]{2,1,0:T(8,128)(2,1)S(1)}, bf16[2,192,512]{2,1,0:T(8,128)(2,1)S(1)}, u32[]{:S(2)}, u32[]{:S(2)}) %collective-permute-start.19) | collective-permute-done | bytes 393248 | tf_op jit(solution)/shard_map/ppermute | solution.py:751
  107.6 5.1 %collective-permute-done.20.refs_2_ = bf16[2,192,512]{2,1,0:T(8,128)(2,1)S(1)} collective-permute-done((bf16[2,192,512]{2,1,0:T(8,128)(2,1)S(1)}, bf16[2,192,512]{2,1,0:T(8,128)(2,1)S(1)}, u32[]{:S(2)}, u32[]{:S(2)}) %collective-permute-start.20) | collective-permute-done | bytes 393248 | tf_op jit(solution)/shard_map/ppermute | solution.py:751
  115.3 5.3 %all-to-all-start = ((bf16[8,192,512]{2,1,0:T(8,128)(2,1)}), bf16[8,192,512]{2,1,0:T(8,128)(2,1)S(1)}, u32[]{:S(2)}, u32[]{:S(2)}) async-start(bf16[8,192,512]{2,1,0:T(8,128)(2,1)} %broadcast_in_dim.45), calls=%async_computation | async-start | bytes 3145728 | tf_op jit(solution)/shard_map/all_to_all | solution.py:737
  120.6 3.7 in_order.1.refs_5_.refs_2_.refs_3_
  124.3 5.2 %all-gather.2.cloned.1.call-done.refs_7_.refs_4_.w_ref = bf16[1536,4224]{1,0:T(8,128)(2,1)} async-done(((bf16[96,4224]{1,0:T(8,128)(2,1)}), bf16[1536,4224]{1,0:T(8,128)(2,1)}) %all-gather.2.cloned.1.call-update) | async-done | bytes 12976144 | tf_op jit(solution)/shard_map/all_gather | solution.py:913
  129.6 20.1 %mlp_part.2 = (f32[64,1536]{1,0:T(8,128)}, bf16[512,1536]{1,0:T(8,128)(2,1)}, bf16[512,896]{1,0:T(8,128)(2,1)}, bf16[512,896]{1,0:T(8,128)(2,1)}, bf16[512,896]{...) custom-call(s32[1]{0:T(128)} %bitcast.1.me_ref, ...), custom_call_target="tpu_custom_call" | custom-call | flops 1150000000 | bytes 1024 | tf_op jit(solution)/shard_map/mlp_part/pallas_call | solution.py:398
  150.8 4.6 %all-to-all-start.1 = ((bf16[8,64,1536]{2,1,0:T(8,128)(2,1)}), bf16[8,64,1536]{2,1,0:T(8,128)(2,1)S(1)}, u32[]{:S(2)}, u32[]{:S(2)}) async-start(bf16[8,64,1536]{2,1,0:T(8,128)(2,1)} %get-tuple-element.173), calls=%async_computation.1 | async-start | bytes 3145728 | tf_op jit(solution)/shard_map/all_to_all | solution.py:741
  155.3 19.9 %mlp_part.3 = (f32[64,1536]{1,0:T(8,128)}, bf16[512,1536]{1,0:T(8,128)(2,1)}, bf16[512,896]{1,0:T(8,128)(2,1)}, bf16[512,896]{1,0:T(8,128)(2,1)}, bf16[512,896]{...) custom-call(s32[1]{0:T(128)} %bitcast.1.me_ref, ...), custom_call_target="tpu_custom_call" | custom-call | flops 1150000000 | bytes 1024 | tf_op jit(solution)/shard_map/mlp_part/pallas_call | solution.py:398
  178.2 4.3 %all-to-all-start.2 = ((bf16[8,64,1536]{2,1,0:T(8,128)(2,1)}), bf16[8,64,1536]{2,1,0:T(8,128)(2,1)S(1)}, u32[]{:S(2)}, u32[]{:S(2)}) async-start(bf16[8,64,1536]{2,1,0:T(8,128)(2,1)} %get-tuple-element.189), calls=%async_computation.2 | async-start | bytes 3145728 | tf_op jit(solution)/shard_map/all_to_all | solution.py:741
  182.6 17.5 %mlp_grads.1 = (bf16[8,96,2688]{2,1,0:T(8,128)(2,1)}, bf16[8,96,2688]{2,1,0:T(8,128)(2,1)}) custom-call(s32[1]{0:T(128)} %bitcast.core_ref, bf16[512,1536]{1,0:T(8,128)(2,1)} %get-tuple-element.176.refs_0_, bf16[512,1536]{1,0:T(8,128)(2,1)} %get-tuple-element.178.refs_1_, bf16[8,128,1536]{2,1,0:T(8,128)(2,1)} %in_order.1.refs_5_.refs_2_.refs_3_, ...), custom_call_target="tpu_custom_call" | custom-call | flops 115000000 | bytes 1024 | tf_op jit(solution)/shard_map/mlp_grads/pallas_call | solution.py:478
  200.2 3.5 all-to-all-done.2.back1_ref
  204.8 6.1 %middle_back.1 = (bf16[128,1536]{1,0:T(8,128)(2,1)}, f32[128,1536]{1,0:T(8,128)}, bf16[1536,128]{1,0:T(8,128)(2,1)}, f32[1,1536]{1,0:T(1,128)}, f32[128,1536]{1,0:T(8,128)}) custom-call(bf16[8,64,1536]{2,1,0:T(8,128)(2,1)} %copy-done.1, bf16[8,64,1536]{2,1,0:T(8,128)(2,1)} %copy-done.2, f32[64,1536]{1,0:T(8,128)} %get-tuple-element.192.mid0_ref, ...), custom_call_target="tpu_custom_call" | custom-call | flops 115000000 | bytes 1024 | tf_op jit(solution)/shard_map/middle_back/pallas_call | solution.py:568
  211.0 5.5 %out_grads.1 = (bf16[8,96,1536]{2,1,0:T(8,128)(2,1)}, bf16[4,96,1536]{2,1,0:T(8,128)(2,1)}, bf16[4,96,1536]{2,1,0:T(8,128)(2,1)}) custom-call(s32[1]{0:T(128)} %bitcast.core_ref, bf16[128,1536]{1,0:T(8,128)(2,1)} %get-tuple-element.203.branch_ref, bf16[1536,64]{1,0:T(8,128)(2,1)} %get-tuple-element.207.refs_0_, bf16[1536,64]{1,0:T(8,128)(2,1)} %get-tuple-element.208.refs_1_), custom_call_target="tpu_custom_call" | custom-call | flops 115000000 | bytes 1024 | tf_op jit(solution)/shard_map/out_grads/pallas_call | solution.py:635
  217.0 3.5 all-to-all-start.3
  225.3 4.6 %core_halves.1 = bf16[8,96,1536]{2,1,0:T(8,128)(2,1)} custom-call(bf16[8,96,1536]{2,1,0:T(8,128)(2,1)} %get-tuple-element.209.mine_ref, bf16[4,96,1536]{2,1,0:T(8,128)(2,1)} %copy-done.12, bf16[4,96,1536]{2,1,0:T(8,128)(2,1)} %collective-permute-done.23.high_ref), custom_call_target="tpu_custom_call" | custom-call | flops 115000000 | bytes 1024 | tf_op jit(solution)/shard_map/core_halves/pallas_call | solution.py:524
  230.0 3.2 collective-permute-start.25
  235.7 13.3 %attend_backward.1 = (bf16[320,1024]{1,0:T(8,128)(2,1)}, bf16[2,128,1536]{2,1,0:T(8,128)(2,1)}, bf16[2,128,1536]{2,1,0:T(8,128)(2,1)}, bf16[2,128,1536]{2,1,0:T(...) custom-call(s32[1]{0:T(128)} %bitcast.1.me_ref, bf16[192,1024]{1,0:T(8,128)(2,1)} %get-tuple-element.195.qt_ref, ...), custom_call_target="tpu_custom_call" | custom-call | flops 115000000 | bytes 1024 | tf_op jit(solution)/shard_map/attend_backward/pallas_call | solution.py:289
  249.0 4.7 %qkv_grads.1 = (bf16[8,96,384]{2,1,0:T(8,128)(2,1)}, bf16[8,96,384]{2,1,0:T(8,128)(2,1)}) custom-call(s32[1]{0:T(128)} %bitcast.core_ref, bf16[320,1024]{1,0:T(8,128)(2,1)} %get-tuple-element.218.gt_ref, bf16[1024,1536]{1,0:T(8,128)(2,1)} %get-tuple-element.219.normed_ref, f32[64,128]{1,0:T(8,128)} %get-tuple-element.220.gains_ref, ...), custom_call_target="tpu_custom_call" | custom-call | flops 115000000 | bytes 1024 | tf_op jit(solution)/shard_map/qkv_grads/pallas_call | solution.py:613
  255.7 6.1 %core_sums.2 = bf16[8,96,2688]{2,1,0:T(8,128)(2,1)} custom-call(bf16[8,96,2688]{2,1,0:T(8,128)(2,1)} %get-tuple-element.226.mine_ref, bf16[8,96,2688]{2,1,0:T(8,128)(2,1)} %copy-done.4), custom_call_target="tpu_custom_call" | custom-call | flops 115000000 | bytes 1024 | tf_op jit(solution)/shard_map/core_sums/pallas_call | solution.py:499
  261.8 6.0 %collective-permute-done.25 = bf16[2,128,1536]{2,1,0:T(8,128)(2,1)S(1)} collective-permute-done((bf16[2,128,1536]{2,1,0:T(8,128)(2,1)}, bf16[2,128,1536]{2,1,0:T(8,128)(2,1)S(1)}, u32[]{:S(2)}, u32[]{:S(2)}) %collective-permute-start.25) | collective-permute-done | bytes 786464 | tf_op jit(solution)/shard_map/ppermute | solution.py:751
  267.8 3.3 collective-permute-done.26
  278.4 3.4 core_sums.3
  289.7 3.5 all-to-all-start.4
  301.7 17.1 %all-to-all-done.4 = bf16[8,96,192]{2,1,0:T(8,128)(2,1)S(1)} async-done(((bf16[8,96,192]{2,1,0:T(8,128)(2,1)}), bf16[8,96,192]{2,1,0:T(8,128)(2,1)S(1)}, u32[]{:S(2)}, u32[]{:S(2)}) %all-to-all-start.4) | async-done | bytes 294944 | tf_op jit(solution)/shard_map/all_to_all | solution.py:741
  338.1 3.6 all-to-all-start.5
  347.5 9.0 %collective-permute-done.39.got_ref = bf16[96,2688]{1,0:T(8,128)(2,1)S(1)} collective-permute-done((bf16[96,2688]{1,0:T(8,128)(2,1)}, bf16[96,2688]{1,0:T(8,128)(2,1)S(1)}, u32[]{:S(2)}, u32[]{:S(2)}) %collective-permute-start.39) | collective-permute-done | bytes 516128 | tf_op jit(solution)/shard_map/ppermute | solution.py:816
  (220 shorter events, 119.1 us)
Async XLA Ops:
  7.2 122.3 %all-gather.2.cloned.1.call-start = ((), (), s32[]{:S(2)}) async-start(), calls=%async_computation.8 | async-start | bytes 13787136 | tf_op jit(solution)/shard_map/all_gather | solution.py:913
  9.7 15.6 %collective-permute-start.1 = (bf16[128,1664]{1,0:T(8,128)(2,1)S(1)}, bf16[128,1664]{1,0:T(8,128)(2,1)}, u32[]{:S(2)}, u32[]{:S(2)}) collective-permute-start(bf16[128,1664]{1,0:T(8,128)(2,1)S(1)} %fusion.19.refs_0_), channel_id=1, source_target_pairs={{0,16},{16,0},{32,48},{48,32},{64,80},{80,64},{96,112},{112,96},{1... | collective-permute-start | bytes 1277960 | tf_op jit(solution)/shard_map/ppermute | solution.py:751
  18.3 13.1 %collective-permute-start.3 = (bf16[128,1664]{1,0:T(8,128)(2,1)S(1)}, bf16[128,1664]{1,0:T(8,128)(2,1)S(1)}, u32[]{:S(2)}, u32[]{:S(2)}) collective-permute-start(bf16[128,1664]{1,0:T(8,128)(2,1)S(1)} %fusion.19.refs_0_), channel_id=1, source_target_pairs={{0,96},{16,112},{32,0},{48,16},{64,32},{80,48},{96,64},{112,80},{1... | collective-permute-start | bytes 1277960 | tf_op jit(solution)/shard_map/ppermute | solution.py:751
  25.4 20.2 %collective-permute-start = (bf16[128,1536]{1,0:T(8,128)(2,1)S(1)}, bf16[128,1536]{1,0:T(8,128)(2,1)}, u32[]{:S(2)}, u32[]{:S(2)}) collective-permute-start(bf16[128,1536]{1,0:T(8,128)(2,1)S(1)} %bitcast.111), channel_id=1, source_target_pairs={{0,16},{16,0},{32,48},{48,32},{64,80},{80,64},{96,112},{112,96},{1... | collective-permute-start | bytes 1179656 | tf_op jit(solution)/shard_map/ppermute | solution.py:751
  25.7 14.1 %collective-permute-start.4 = (bf16[128,1664]{1,0:T(8,128)(2,1)}, bf16[128,1664]{1,0:T(8,128)(2,1)S(1)}, u32[]{:S(2)}, u32[]{:S(2)}) collective-permute-start(bf16[128,1664]{1,0:T(8,128)(2,1)} %collective-permute-done.1.refs_1_), channel_id=1, source_target_pairs={{0,32},{16,48},{32,64},{48,80},{64,96},{80,112},{96,0},{112,16},{1... | collective-permute-start | bytes 1277960 | tf_op jit(solution)/shard_map/ppermute | solution.py:751
  31.3 14.9 %collective-permute-start.6 = (bf16[64,1664]{1,0:T(8,128)(2,1)S(1)}, bf16[64,1664]{1,0:T(8,128)(2,1)S(1)}, u32[]{:S(2)}, u32[]{:S(2)}) collective-permute-start(bf16[64,1664]{1,0:T(8,128)(2,1)S(1)} %slice.50), channel_id=1, source_target_pairs={{0,32},{16,48},{32,64},{48,80},{64,96},{80,112},{96,0},{112,16},{1... | collective-permute-start | bytes 638984 | tf_op jit(solution)/shard_map/ppermute | solution.py:751
  31.7 18.3 %collective-permute-start.7 = (bf16[64,1664]{1,0:T(8,128)(2,1)S(1)}, bf16[64,1664]{1,0:T(8,128)(2,1)S(1)}, u32[]{:S(2)}, u32[]{:S(2)}) collective-permute-start(bf16[64,1664]{1,0:T(8,128)(2,1)S(1)} %slice.51), channel_id=1, source_target_pairs={{0,96},{16,112},{32,0},{48,16},{64,32},{80,48},{96,64},{112,80},{1... | collective-permute-start | bytes 638984 | tf_op jit(solution)/shard_map/ppermute | solution.py:751
  39.7 17.2 %collective-permute-start.12 = (bf16[1,4,96,384]{3,2,1,0:T(8,128)(2,1)S(1)}, bf16[1,4,96,384]{3,2,1,0:T(8,128)(2,1)S(1)}, u32[]{:S(2)}, u32[]{:S(2)}) collective-permute-start(bf16[1,4,96,384]{3,2,1,0:T(8,128)(2,1)S(1)} %bitcast.113), channel_id=1, source_target_pairs={{0,4},{1,5},{2,6},{3,7},{4,8},{5,9},{6,10},{7,11},{8,12},{9,13},{1... | collective-permute-start | bytes 884744 | tf_op jit(solution)/shard_map/ppermute | solution.py:855
  41.7 21.0 %collective-permute-start.13 = (bf16[1,4,96,384]{3,2,1,0:T(8,128)(2,1)S(1)}, bf16[1,4,96,384]{3,2,1,0:T(8,128)(2,1)S(1)}, u32[]{:S(2)}, u32[]{:S(2)}) collective-permute-start(bf16[1,4,96,384]{3,2,1,0:T(8,128)(2,1)S(1)} %bitcast.114), channel_id=1, source_target_pairs={{0,8},{1,9},{2,10},{3,11},{4,12},{5,13},{6,14},{7,15},{8,0},{9,1},... | collective-permute-start | bytes 884744 | tf_op jit(solution)/shard_map/ppermute | solution.py:855
  52.7 42.3 %collective-permute-start.16 = (bf16[2,128,1536]{2,1,0:T(8,128)(2,1)S(1)}, bf16[2,128,1536]{2,1,0:T(8,128)(2,1)S(1)}, u32[]{:S(2)}, u32[]{:S(2)}) collective-permute-start(bf16[2,128,1536]{2,1,0:T(8,128)(2,1)S(1)} %pad_maximum_fusion.1.refs_0_), channel_id=1, source_target_pairs={{0,32},{16,48},{32,64},{48,80},{64,96},{80,112},{96,0},{112,16},{1... | collective-permute-start | bytes 2359304 | tf_op jit(solution)/shard_map/ppermute | solution.py:751
  53.8 41.3 %collective-permute-start.17 = (bf16[2,128,1536]{2,1,0:T(8,128)(2,1)S(1)}, bf16[2,128,1536]{2,1,0:T(8,128)(2,1)S(1)}, u32[]{:S(2)}, u32[]{:S(2)}) collective-permute-start(bf16[2,128,1536]{2,1,0:T(8,128)(2,1)S(1)} %pad_maximum_fusion.1.refs_0_), channel_id=1, source_target_pairs={{0,96},{16,112},{32,0},{48,16},{64,32},{80,48},{96,64},{112,80},{1... | collective-permute-start | bytes 2359304 | tf_op jit(solution)/shard_map/ppermute | solution.py:751
  57.0 38.1 %collective-permute-start.18 = (bf16[2,128,1536]{2,1,0:T(8,128)(2,1)S(1)}, bf16[2,128,1536]{2,1,0:T(8,128)(2,1)S(1)}, u32[]{:S(2)}, u32[]{:S(2)}) collective-permute-start(bf16[2,128,1536]{2,1,0:T(8,128)(2,1)S(1)} %pad_maximum_fusion.1.refs_0_), channel_id=1, source_target_pairs={{0,64},{16,80},{32,96},{48,112},{64,0},{80,16},{96,32},{112,48},{1... | collective-permute-start | bytes 2359304 | tf_op jit(solution)/shard_map/ppermute | solution.py:751
  75.2 19.8 %collective-permute-start.15 = (bf16[2,192,512]{2,1,0:T(8,128)(2,1)}, bf16[2,192,512]{2,1,0:T(8,128)(2,1)S(1)}, u32[]{:S(2)}, u32[]{:S(2)}) collective-permute-start(bf16[2,192,512]{2,1,0:T(8,128)(2,1)} %get-tuple-element.154), channel_id=1, source_target_pairs={{0,16},{16,0},{32,48},{48,32},{64,80},{80,64},{96,112},{112,96},{1... | collective-permute-start | bytes 1179656 | tf_op jit(solution)/shard_map/ppermute | solution.py:751
  96.1 16.6 %collective-permute-start.20 = (bf16[2,192,512]{2,1,0:T(8,128)(2,1)S(1)}, bf16[2,192,512]{2,1,0:T(8,128)(2,1)S(1)}, u32[]{:S(2)}, u32[]{:S(2)}) collective-permute-start(bf16[2,192,512]{2,1,0:T(8,128)(2,1)S(1)} %pad_maximum_fusion.2.refs_0_), channel_id=1, source_target_pairs={{0,96},{16,112},{32,0},{48,16},{64,32},{80,48},{96,64},{112,80},{1... | collective-permute-start | bytes 1179656 | tf_op jit(solution)/shard_map/ppermute | solution.py:751
  98.4 15.6 %collective-permute-start.21 = (bf16[2,192,512]{2,1,0:T(8,128)(2,1)S(1)}, bf16[2,192,512]{2,1,0:T(8,128)(2,1)S(1)}, u32[]{:S(2)}, u32[]{:S(2)}) collective-permute-start(bf16[2,192,512]{2,1,0:T(8,128)(2,1)S(1)} %pad_maximum_fusion.2.refs_0_), channel_id=1, source_target_pairs={{0,64},{16,80},{32,96},{48,112},{64,0},{80,16},{96,32},{112,48},{1... | collective-permute-start | bytes 1179656 | tf_op jit(solution)/shard_map/ppermute | solution.py:751
  115.3 34.3 %all-to-all-start = ((bf16[8,192,512]{2,1,0:T(8,128)(2,1)}), bf16[8,192,512]{2,1,0:T(8,128)(2,1)S(1)}, u32[]{:S(2)}, u32[]{:S(2)}) async-start(bf16[8,192,512]{2,1,0:T(8,128)(2,1)} %broadcast_in_dim.45), calls=%async_computation | async-start | bytes 3145728 | tf_op jit(solution)/shard_map/all_to_all | solution.py:737
  150.8 26.3 %all-to-all-start.1 = ((bf16[8,64,1536]{2,1,0:T(8,128)(2,1)}), bf16[8,64,1536]{2,1,0:T(8,128)(2,1)S(1)}, u32[]{:S(2)}, u32[]{:S(2)}) async-start(bf16[8,64,1536]{2,1,0:T(8,128)(2,1)} %get-tuple-element.173), calls=%async_computation.1 | async-start | bytes 3145728 | tf_op jit(solution)/shard_map/all_to_all | solution.py:741
  178.2 25.4 %all-to-all-start.2 = ((bf16[8,64,1536]{2,1,0:T(8,128)(2,1)}), bf16[8,64,1536]{2,1,0:T(8,128)(2,1)S(1)}, u32[]{:S(2)}, u32[]{:S(2)}) async-start(bf16[8,64,1536]{2,1,0:T(8,128)(2,1)} %get-tuple-element.189), calls=%async_computation.2 | async-start | bytes 3145728 | tf_op jit(solution)/shard_map/all_to_all | solution.py:741
  220.4 51.6 %reduce-scatter.3.cloned.1.call-start = ((), (), s32[]{:S(2)}) async-start(), calls=%async_computation.9 | async-start | bytes 2949120 | tf_op jit(solution)/shard_map/reduce_scatter | solution.py:959
  229.9 96.7 %reduce-scatter.5.cloned.1.call-start = ((), (), s32[]{:S(2)}) async-start(), calls=%async_computation.10 | async-start | bytes 5160960 | tf_op jit(solution)/shard_map/reduce_scatter | solution.py:959
  229.9 23.7 %collective-permute-start.24 = (bf16[8,96,2688]{2,1,0:T(8,128)(2,1)}, bf16[8,96,2688]{2,1,0:T(8,128)(2,1)S(1)}, u32[]{:S(2)}, u32[]{:S(2)}) collective-permute-start(bf16[8,96,2688]{2,1,0:T(8,128)(2,1)} %get-tuple-element.224), channel_id=1, source_target_pairs={{0,1},{1,0},{2,3},{3,2},{4,5},{5,4},{6,7},{7,6},{8,9},{9,8},{10,11... | collective-permute-start | bytes 12386312 | tf_op jit(solution)/shard_map/ppermute | solution.py:816
  230.0 37.8 %collective-permute-start.25 = (bf16[2,128,1536]{2,1,0:T(8,128)(2,1)}, bf16[2,128,1536]{2,1,0:T(8,128)(2,1)S(1)}, u32[]{:S(2)}, u32[]{:S(2)}) collective-permute-start(bf16[2,128,1536]{2,1,0:T(8,128)(2,1)} %get-tuple-element.229), channel_id=1, source_target_pairs={{0,96},{16,112},{32,0},{48,16},{64,32},{80,48},{96,64},{112,80},{1... | collective-permute-start | bytes 2359304 | tf_op jit(solution)/shard_map/ppermute | solution.py:751
  233.2 37.9 %collective-permute-start.26 = (bf16[2,128,1536]{2,1,0:T(8,128)(2,1)}, bf16[2,128,1536]{2,1,0:T(8,128)(2,1)S(1)}, u32[]{:S(2)}, u32[]{:S(2)}) collective-permute-start(bf16[2,128,1536]{2,1,0:T(8,128)(2,1)} %get-tuple-element.230), channel_id=1, source_target_pairs={{0,32},{16,48},{32,64},{48,80},{64,96},{80,112},{96,0},{112,16},{1... | collective-permute-start | bytes 2359304 | tf_op jit(solution)/shard_map/ppermute | solution.py:751
  233.2 37.9 %collective-permute-start.27 = (bf16[2,128,1536]{2,1,0:T(8,128)(2,1)}, bf16[2,128,1536]{2,1,0:T(8,128)(2,1)}, u32[]{:S(2)}, u32[]{:S(2)}) collective-permute-start(bf16[2,128,1536]{2,1,0:T(8,128)(2,1)} %get-tuple-element.231), channel_id=1, source_target_pairs={{0,64},{16,80},{32,96},{48,112},{64,0},{80,16},{96,32},{112,48},{1... | collective-permute-start | bytes 2359304 | tf_op jit(solution)/shard_map/ppermute | solution.py:751
  276.0 52.5 %collective-permute-start.35 = (bf16[2,128,1536]{2,1,0:T(8,128)(2,1)}, bf16[2,128,1536]{2,1,0:T(8,128)(2,1)}, u32[]{:S(2)}, u32[]{:S(2)}) collective-permute-start(bf16[2,128,1536]{2,1,0:T(8,128)(2,1)} %get-tuple-element.246), channel_id=1, source_target_pairs={{0,96},{16,112},{32,0},{48,16},{64,32},{80,48},{96,64},{112,80},{1... | collective-permute-start | bytes 2359304 | tf_op jit(solution)/shard_map/ppermute | solution.py:751
  276.9 51.6 %collective-permute-start.36 = (bf16[2,128,1536]{2,1,0:T(8,128)(2,1)}, bf16[2,128,1536]{2,1,0:T(8,128)(2,1)}, u32[]{:S(2)}, u32[]{:S(2)}) collective-permute-start(bf16[2,128,1536]{2,1,0:T(8,128)(2,1)} %get-tuple-element.247), channel_id=1, source_target_pairs={{0,32},{16,48},{32,64},{48,80},{64,96},{80,112},{96,0},{112,16},{1... | collective-permute-start | bytes 2359304 | tf_op jit(solution)/shard_map/ppermute | solution.py:751
  283.7 16.3 %collective-permute-start.31 = (bf16[2,96,384]{2,1,0:T(8,128)(2,1)}, bf16[2,96,384]{2,1,0:T(8,128)(2,1)}, u32[]{:S(2)}, u32[]{:S(2)}) collective-permute-start(bf16[2,96,384]{2,1,0:T(8,128)(2,1)} %get-tuple-element.278), channel_id=1, source_target_pairs={{0,8},{1,9},{2,10},{3,11},{4,12},{5,13},{6,14},{7,15},{8,0},{9,1},... | collective-permute-start | bytes 442376 | tf_op jit(solution)/shard_map/ppermute | solution.py:824
  286.0 15.7 %collective-permute-start.32 = (bf16[2,96,384]{2,1,0:T(8,128)(2,1)S(1)}, bf16[2,96,384]{2,1,0:T(8,128)(2,1)}, u32[]{:S(2)}, u32[]{:S(2)}) collective-permute-start(bf16[2,96,384]{2,1,0:T(8,128)(2,1)S(1)} %get-tuple-element.277), channel_id=1, source_target_pairs={{0,12},{1,13},{2,14},{3,15},{4,0},{5,1},{6,2},{7,3},{8,4},{9,5},{1... | collective-permute-start | bytes 442376 | tf_op jit(solution)/shard_map/ppermute | solution.py:824
  289.7 29.0 %all-to-all-start.4 = ((bf16[8,96,192]{2,1,0:T(8,128)(2,1)}), bf16[8,96,192]{2,1,0:T(8,128)(2,1)S(1)}, u32[]{:S(2)}, u32[]{:S(2)}) async-start(bf16[8,96,192]{2,1,0:T(8,128)(2,1)} %out_blocks.1), calls=%async_computation.5 | async-start | bytes 786432 | tf_op jit(solution)/shard_map/all_to_all | solution.py:741
  295.9 32.6 %collective-permute-start.37 = (bf16[2,128,1536]{2,1,0:T(8,128)(2,1)}, bf16[2,128,1536]{2,1,0:T(8,128)(2,1)}, u32[]{:S(2)}, u32[]{:S(2)}) collective-permute-start(bf16[2,128,1536]{2,1,0:T(8,128)(2,1)} %get-tuple-element.248), channel_id=1, source_target_pairs={{0,64},{16,80},{32,96},{48,112},{64,0},{80,16},{96,32},{112,48},{1... | collective-permute-start | bytes 2359304 | tf_op jit(solution)/shard_map/ppermute | solution.py:751
  334.4 22.1 %collective-permute-start.39 = (bf16[96,2688]{1,0:T(8,128)(2,1)}, bf16[96,2688]{1,0:T(8,128)(2,1)S(1)}, u32[]{:S(2)}, u32[]{:S(2)}) collective-permute-start(bf16[96,2688]{1,0:T(8,128)(2,1)} %dynamic-slice_bitcast_fusion.4), channel_id=1, source_target_pairs={{0,2},{1,3},{2,0},{3,1},{4,6},{5,7},{6,4},{7,5},{8,10},{9,11},{10,... | collective-permute-start | bytes 1548296 | tf_op jit(solution)/shard_map/ppermute | solution.py:816
  338.1 22.2 %all-to-all-start.5 = ((bf16[8,96,576]{2,1,0:T(8,128)(2,1)}), bf16[8,96,576]{2,1,0:T(8,128)(2,1)S(1)}, u32[]{:S(2)}, u32[]{:S(2)}) async-start(bf16[8,96,576]{2,1,0:T(8,128)(2,1)} %broadcast_in_dim.48), calls=%async_computation.7 | async-start | bytes 1966080 | tf_op jit(solution)/shard_map/all_to_all | solution.py:737
  (58 other events, 484.6 us)
Sparse Core Ops, SparseCore 0:
  10.5 119.0 all-gather.1
  230.0 30.9 reduce-scatter.2
  271.2 49.0 reduce-scatter.4
